TPU v7x, 256 devices: a whole 4x4x8 slice. The times are simulated.
256 devices in a mesh: chan: 32 (over z, x), arow: 4 (over y), acol: 2 (over core).
Axes of the slice: x: 4, y: 4, z: 8, core: 2. Of those that a mesh axis runs over, the one named last changes fastest.
Arguments:
- voltages: bfloat16 [32, 8, 512, 2048], P(None, ('arow', 'acol'), 'chan'), may hold values from -1.078125 to 1.078125
Outputs:
- band: float32 [32, 2, 8, 4, 512, 512], P('chan', None, ('arow', 'acol'))
- far: float32 [32, 2, 8, 256, 512], P('chan', None, ('arow', 'acol'))
All inputs are finite; a program needn't handle non-finite values.
Results may differ from a plain program's by a relative error of at most 0.0003.
Values may be sent and summed in bfloat16 or wider, within the bound.
No kernel may reach another device: no remote copies, remote signals or barrier semaphores. Data moves between devices by JAX's collectives and lax.ppermute only.
A program may use at most 128 MiB of HBM per device.

v0:
```python
import jax
import jax.numpy as jnp
from jax import lax
from jax.sharding import PartitionSpec as P


def from_behind(block, axis, distance):
    devices = range(lax.axis_size(axis))
    route = [((i - distance) % len(devices), i) for i in devices]
    return lax.ppermute(block, axis, route)


def cross_tile(left, right):
    product = jnp.einsum("crk,cjk->crj", left, right, preferred_element_type=jnp.float32)
    return product.reshape(product.shape[0], 2, product.shape[1] // 2, product.shape[2])


def stacked(block):
    width = block.shape[-1] // 2
    swapped = jnp.concatenate([block[..., width:], -block[..., :width]], -1)
    return jnp.concatenate([block, swapped], 1)


def shards(voltages):
    turned = lax.all_to_all(voltages, "chan", split_axis=0, concat_axis=2, tiled=True)
    own = turned[:, 0]
    groups = lax.axis_size(("arow", "acol"))
    offsets = groups // 2
    member = lax.axis_index(("arow", "acol"))
    group_rows = own.shape[1]
    left = stacked(own)
    tiles = [cross_tile(left, own)]
    current = own
    for offset in range(1, offsets + 1):
        current = from_behind(current, ("arow", "acol"), -1)
        if offset < offsets:
            tiles.append(cross_tile(left, current))
    band = jnp.stack(tiles, 2)[:, :, None]
    upper = member // offsets
    first = upper == 0
    row_source = jnp.where(first, own, current)
    col_source = jnp.where(first, current, own)
    half_rows = group_rows // 2
    rows_part = lax.dynamic_slice_in_dim(row_source, upper * half_rows, half_rows, 1)
    far = cross_tile(stacked(rows_part), col_source)[:, :, None]
    return (band, far)


def solution(mesh):
    return jax.shard_map(
        shards,
        mesh=mesh,
        in_specs=(P(None, ("arow", "acol"), "chan", None),),
        out_specs=(
            P("chan", None, ("arow", "acol"), None, None, None),
            P("chan", None, ("arow", "acol"), None, None),
        ),
        check_vma=False,
    )
```

profile of v0, /device:TPU:1, one launch (start us, length us, event | category | flops | bytes accessed | tf_op | source)
XLA Modules:
  0.0 170.3 jit_solution(9275658793356682169)
XLA Ops:
  0.6 60.6 %all_to_all.4 = bf16[32,1,16,2048]{3,2,1,0:T(8,128)(2,1)S(1)} all-to-all(bf16[32,1,16,2048]{3,2,1,0:T(8,128)(2,1)} %param.1), channel_id=1, replica_groups=mesh['chan'=32,'arow'=4,'acol'=2] {'chan'}, dimensions={0} | all-to-all | bytes 4194304 | tf_op jit(solution)/shard_map/all_to_all | solution.py:25
  61.2 2.8 %collective-permute-start = (bf16[1,512,2048]{2,1,0:T(8,128)(2,1)S(1)}, bf16[1,512,2048]{2,1,0:T(8,128)(2,1)S(1)}, u32[]{:S(2)}, u32[]{:S(2)}) collective-permute-start(bf16[1,512,2048]{2,1,0:T(8,128)(2,1)S(1)} %bitcast.50), channel_id=1, source_target_pairs={{1,0},{2,1},{3,2},{4,3},{5,4},{6,5},{7,6},{0,7},{9,8},{10,9},{11,1... | collective-permute-start | bytes 6291464 | tf_op jit(solution)/shard_map/ppermute | solution.py:10
  64.0 24.9 %collective-permute-done = bf16[1,512,2048]{2,1,0:T(8,128)(2,1)S(1)} collective-permute-done((bf16[1,512,2048]{2,1,0:T(8,128)(2,1)S(1)}, bf16[1,512,2048]{2,1,0:T(8,128)(2,1)S(1)}, u32[]{:S(2)}, u32[]{:S(2)}) %collective-permute-start) | collective-permute-done | bytes 2097184 | tf_op jit(solution)/shard_map/ppermute | solution.py:10
  88.9 0.0 copy-start
  88.9 1.3 copy-done
  90.2 0.0 collective-permute-start.1
  90.2 25.6 %collective-permute-done.1 = bf16[1,512,2048]{2,1,0:T(8,128)(2,1)} collective-permute-done((bf16[1,512,2048]{2,1,0:T(8,128)(2,1)S(1)}, bf16[1,512,2048]{2,1,0:T(8,128)(2,1)}, u32[]{:S(2)}, u32[]{:S(2)}) %collective-permute-start.1) | collective-permute-done | bytes 2097184 | tf_op jit(solution)/shard_map/ppermute | solution.py:10
  115.8 0.1 collective-permute-start.2
  115.9 0.1 fusion.22
  116.0 10.6 %maximum_maximum_fusion = bf16[1,1024,2048]{2,1,0:T(8,128)(2,1)S(1)} fusion(bf16[1,512,1024]{2,1,0:T(8,128)(2,1)S(1)} %get-tuple-element.5, bf16[1,512,1024]{2,1,0:T(8,128)(2,1)S(1)} %get-tuple-element.4, bf16[1,512,2048]{2,1,0:T(8,128)(2,1)S(1)} %bitcast.52), kind=kLoop, calls=%fused_computation.1 | loop fusion | flops 12582912 | bytes 8388608 | tf_op jit(solution)/shard_map/concatenate | solution.py:21
  126.6 0.0 copy-start.1
  126.6 2.4 %convolution_bitcast_fusion = f32[1,2,1,512,512]{4,3,1,2,0:T(8,128)S(1)} fusion(bf16[2,512,2048]{2,1,0:T(8,128)(2,1)S(1)} %bitcast.56, bf16[512,2048,1]{1,0,2:T(8,128)(2,1)S(1)} %bitcast.53), kind=kOutput, calls=%fused_computation.16 | convolution fusion | flops 2147483648 | bytes 8388608 | tf_op jit(solution)/shard_map/crk,cjk->crj/dot_general | solution.py:14
  129.0 12.6 %collective-permute-done.2 = bf16[1,512,2048]{2,1,0:T(8,128)(2,1)} collective-permute-done((bf16[1,512,2048]{2,1,0:T(8,128)(2,1)}, bf16[1,512,2048]{2,1,0:T(8,128)(2,1)}, u32[]{:S(2)}, u32[]{:S(2)}) %collective-permute-start.2) | collective-permute-done | bytes 2097184 | tf_op jit(solution)/shard_map/ppermute | solution.py:10
  141.6 1.4 collective-permute-start.3
  142.9 0.0 copy-done.1
  143.0 2.4 %fusion.10 = f32[1,2,1,512,512]{4,3,1,2,0:T(8,128)S(1)} fusion(bf16[2,512,2048]{2,1,0:T(8,128)(2,1)S(1)} %bitcast.57, bf16[1,512,2048]{2,1,0:T(8,128)(2,1)S(1)} %copy-done.1), kind=kOutput, calls=%fused_computation.13 | convolution fusion | flops 2147483648 | bytes 8388608 | tf_op jit(solution)/shard_map/crk,cjk->crj/dot_general | solution.py:14
  145.3 4.0 %fusion.13 = f32[1,2,1,512,512]{4,3,1,2,0:T(8,128)S(1)} fusion(bf16[2,512,2048]{2,1,0:T(8,128)(2,1)S(1)} %bitcast.58, bf16[1,512,2048]{2,1,0:T(8,128)(2,1)} %collective-permute-done.1), kind=kOutput, calls=%fused_computation.14 | convolution fusion | flops 2147483648 | bytes 8388608 | tf_op jit(solution)/shard_map/crk,cjk->crj/dot_general | solution.py:14
  149.3 4.0 %fusion.16 = f32[1,2,1,512,512]{4,3,1,2,0:T(8,128)S(1)} fusion(bf16[2,512,2048]{2,1,0:T(8,128)(2,1)S(1)} %bitcast.59, bf16[1,512,2048]{2,1,0:T(8,128)(2,1)} %collective-permute-done.2), kind=kOutput, calls=%fused_computation.15 | convolution fusion | flops 2147483648 | bytes 8388608 | tf_op jit(solution)/shard_map/crk,cjk->crj/dot_general | solution.py:14
  153.2 0.9 maximum_bitcast_fusion
  154.2 4.5 %copy.3 = f32[1,2,1,4,512,512]{5,4,3,2,1,0:T(8,128)} copy(f32[1,2,1,4,512,512]{5,4,1,3,2,0:T(8,128)S(1)} %maximum_bitcast_fusion) | data formatting | bytes 16777216
  158.6 8.6 %collective-permute-done.3 = bf16[1,512,2048]{2,1,0:T(8,128)(2,1)S(1)} collective-permute-done((bf16[1,512,2048]{2,1,0:T(8,128)(2,1)}, bf16[1,512,2048]{2,1,0:T(8,128)(2,1)S(1)}, u32[]{:S(2)}, u32[]{:S(2)}) %collective-permute-start.3) | collective-permute-done | bytes 2097184 | tf_op jit(solution)/shard_map/ppermute | solution.py:10
  167.2 0.4 dynamic-slice_select_fusion
  167.6 0.1 fusion.23
  167.7 0.2 maximum_maximum_fusion.1
  167.9 2.4 %fusion.19 = f32[1,2,1,256,512]{4,3,2,1,0:T(8,128)} fusion(bf16[2,256,2048]{2,1,0:T(8,128)(2,1)S(1)} %bitcast.60, bf16[1,512,2048]{2,1,0:T(8,128)(2,1)S(1)} %collective-permute-done.3, bf16[1,512,2048]{2,1,0:T(8,128)(2,1)S(1)} %bitcast.55, pred[]{:T(512)S(6)} %eq.3), kind=kOutput, calls=%fused_computation.17 | convolution fusion | flops 1074790400 | bytes 7340033 | tf_op jit(solution)/shard_map/crk,cjk->crj/dot_general | solution.py:14
Async XLA Ops:
  61.2 27.7 %collective-permute-start = (bf16[1,512,2048]{2,1,0:T(8,128)(2,1)S(1)}, bf16[1,512,2048]{2,1,0:T(8,128)(2,1)S(1)}, u32[]{:S(2)}, u32[]{:S(2)}) collective-permute-start(bf16[1,512,2048]{2,1,0:T(8,128)(2,1)S(1)} %bitcast.50), channel_id=1, source_target_pairs={{1,0},{2,1},{3,2},{4,3},{5,4},{6,5},{7,6},{0,7},{9,8},{10,9},{11,1... | collective-permute-start | bytes 6291464 | tf_op jit(solution)/shard_map/ppermute | solution.py:10
  88.9 1.3 copy-start
  90.2 25.6 %collective-permute-start.1 = (bf16[1,512,2048]{2,1,0:T(8,128)(2,1)S(1)}, bf16[1,512,2048]{2,1,0:T(8,128)(2,1)}, u32[]{:S(2)}, u32[]{:S(2)}) collective-permute-start(bf16[1,512,2048]{2,1,0:T(8,128)(2,1)S(1)} %collective-permute-done), channel_id=1, source_target_pairs={{1,0},{2,1},{3,2},{4,3},{5,4},{6,5},{7,6},{0,7},{9,8},{10,9},{11,1... | collective-permute-start | bytes 6291464 | tf_op jit(solution)/shard_map/ppermute | solution.py:10
  115.8 25.8 %collective-permute-start.2 = (bf16[1,512,2048]{2,1,0:T(8,128)(2,1)}, bf16[1,512,2048]{2,1,0:T(8,128)(2,1)}, u32[]{:S(2)}, u32[]{:S(2)}) collective-permute-start(bf16[1,512,2048]{2,1,0:T(8,128)(2,1)} %collective-permute-done.1), channel_id=1, source_target_pairs={{1,0},{2,1},{3,2},{4,3},{5,4},{6,5},{7,6},{0,7},{9,8},{10,9},{11,1... | collective-permute-start | bytes 6291464 | tf_op jit(solution)/shard_map/ppermute | solution.py:10
  126.6 16.3 %copy-start.1 = (bf16[1,512,2048]{2,1,0:T(8,128)(2,1)S(1)}, bf16[1,512,2048]{2,1,0:T(8,128)(2,1)}, u32[]{:S(2)}) copy-start(bf16[1,512,2048]{2,1,0:T(8,128)(2,1)} %copy-done) | copy-start | bytes 6291460
  141.6 25.7 %collective-permute-start.3 = (bf16[1,512,2048]{2,1,0:T(8,128)(2,1)}, bf16[1,512,2048]{2,1,0:T(8,128)(2,1)S(1)}, u32[]{:S(2)}, u32[]{:S(2)}) collective-permute-start(bf16[1,512,2048]{2,1,0:T(8,128)(2,1)} %collective-permute-done.2), channel_id=1, source_target_pairs={{1,0},{2,1},{3,2},{4,3},{5,4},{6,5},{7,6},{0,7},{9,8},{10,9},{11,1... | collective-permute-start | bytes 6291464 | tf_op jit(solution)/shard_map/ppermute | solution.py:10
where the time goes:
time: 173 us; the launch traced here: 170 us
  waiting for transfers between devices  71.7 us (41%)
  blocking collectives  60.6 us (35%)
  matrix products  15 us (9%)
  other arithmetic  12.4 us (7%)
  local copies, waits for them, and re-layouts  5.78 us (3%)
  starting transfers between devices  4.27 us (2%)
    ppermute x4, waiting for transfers between devices, from_behind(): return lax.ppermute(block, axis, route)  71.7 us
    all_to_all x1, blocking collectives, shards(): lax.all_to_all(voltages, 'chan', split_axis=0, concat_axis=2, tiled=True)  60.6 us
    dot_general x5, matrix products, cross_tile(): jnp.einsum('crk,cjk->crj', left, right, preferred_element_type=jnp.float32)  15 us
    concatenate x2, other arithmetic, stacked(): return jnp.concatenate([block, swapped], 1)  10.8 us
    unnamed x5, local copies, waits for them, and re-layouts  5.78 us
    ppermute x4, starting transfers between devices, from_behind(): return lax.ppermute(block, axis, route)  4.27 us
  transfers between devices with their start and end apart: 4, of which 4 were waited for; matrix products, arithmetic and copies ran while one was open for 17% of the time, Pallas kernels for 0%

commit v1 on v0

v1 whole, which is shorter than its diff:
```python
import jax
import jax.numpy as jnp
from jax import lax
from jax.experimental import pallas as pl
from jax.experimental.pallas import tpu as pltpu
from jax.sharding import PartitionSpec as P

DOWN_ROWS = 304
VMEM_BYTES = 28 * 1024 * 1024


def from_ahead(block, distance):
    size = lax.axis_size("arow")
    return lax.ppermute(block, "arow", [((i + distance) % size, i) for i in range(size)])


def from_sibling(block, cores=(0, 1)):
    return lax.ppermute(block, "acol", [(1 - core, core) for core in cores])


def turn(block):
    turned = lax.all_to_all(block, "chan", split_axis=0, concat_axis=0, tiled=True)
    return turned.reshape(-1, block.shape[-1])


def cut_kernel(voltages, early, late):
    width = voltages.shape[-1] // 2
    cut = width // 2
    for part in range(2):
        to = pl.ds(part * cut, cut)
        early[:, :, to] = voltages[:, 0, :, pl.ds(part * width, cut)]
        late[:, :, to] = voltages[:, 0, :, pl.ds(part * width + cut, cut)]


def halves(voltages):
    channels, _, rows, span = voltages.shape
    step = channels // 4
    half = jax.ShapeDtypeStruct((channels, rows, span // 2), voltages.dtype)
    return pl.pallas_call(
        cut_kernel,
        out_shape=(half, half),
        grid=(channels // step,),
        in_specs=[pl.BlockSpec((step, 1, rows, span), lambda i: (i, 0, 0, 0))],
        out_specs=[pl.BlockSpec((step, rows, span // 2), lambda i: (i, 0, 0))] * 2,
    )(voltages)


def quadrature(rows):
    width = rows.shape[-1] // 2
    return jnp.concatenate([rows[:, width:], -rows[:, :width]], -1)


def times(left, right):
    return lax.dot_general(
        left, right, (((1,), (1,)), ((), ())), preferred_element_type=jnp.float32
    )


def far_tile(upper, own, swapped, beyond, put):
    rows = own.shape[0] // 2

    @pl.when(upper == 0)
    def _():
        for part, left in enumerate((own, swapped)):
            put(part, times(left[:rows, :], beyond[...]))

    @pl.when(upper != 0)
    def _():
        lower = beyond[rows:, :]
        put(0, times(lower, own[...]))
        put(1, times(quadrature(lower), own[...]))


def early_kernel(
    place, own_at, down_1, up_3, down_2, up_2, sib_own, sib_down_1, sib_up_3, sib_down_2, sib_up_2,
    band, far, swapped, own, ahead, beyond, sib_ahead, other, sems,
):
    core, upper = place[0], place[1]
    first, second = pl.ds(0, down_1.shape[0]), pl.ds(down_1.shape[0], up_3.shape[0])

    def load(number, source, target):
        return pltpu.make_async_copy(source, target, sems.at[number])

    own_load = load(0, own_at, own)
    ahead_loads = [load(1, down_1, ahead.at[first]), load(2, up_3, ahead.at[second])]
    beyond_loads = [load(3, down_2, beyond.at[first]), load(4, up_2, beyond.at[second])]
    sib_loads = [load(5, sib_down_1, sib_ahead.at[first]), load(6, sib_up_3, sib_ahead.at[second])]
    near_load = load(7, sib_own, other)
    far_loads = [load(7, sib_down_2, other.at[first]), load(8, sib_up_2, other.at[second])]

    for copy in (own_load, *ahead_loads, *beyond_loads, *sib_loads):
        copy.start()

    @pl.when(core == 0)
    def _():
        near_load.start()

    @pl.when(core != 0)
    def _():
        for copy in far_loads:
            copy.start()

    def tile(slot, columns):
        for part, left in enumerate((own, swapped)):
            band[0, part, 0, slot] = times(left[...], columns[...])

    def put(part, product):
        far[0, part, 0] = product

    own_load.wait()
    swapped[...] = quadrature(own[...])
    tile(0, own)
    for copy in ahead_loads:
        copy.wait()
    tile(2, ahead)
    for copy in beyond_loads:
        copy.wait()
    far_tile(upper, own, swapped, beyond, put)
    for copy in sib_loads:
        copy.wait()
    tile(3 - 2 * core, sib_ahead)

    @pl.when(core == 0)
    def _():
        near_load.wait()

    @pl.when(core != 0)
    def _():
        for copy in far_loads:
            copy.wait()

    tile(1 + 2 * core, other)


def late_kernel(
    place, own_at, ahead_at, beyond_at, sib_ahead_at, band_in, far_in, band, far_at,
    swapped, own, ahead, beyond, sib_ahead, far, sems,
):
    core, upper = place[0], place[1]
    step = pl.program_id(0)
    last = pl.num_programs(0) - 1
    pairs = ((own_at, own), (beyond_at, beyond), (ahead_at, ahead), (sib_ahead_at, sib_ahead))
    loads = [pltpu.make_async_copy(*pair, sems.at[i]) for i, pair in enumerate(pairs)]
    store = pltpu.make_async_copy(far, far_at.at[0, :, 0], sems.at[4])

    def tile(slot, columns):
        for part, left in enumerate((own, swapped)):
            band[0, part, 0, 0] = times(left[...], columns[...]) + band_in[0, part, 0, slot]

    @pl.when(step == 0)
    def _():
        for load in loads:
            load.start()
        loads[0].wait()
        swapped[...] = quadrature(own[...])
        tile(0, own)
        loads[1].wait()

        def put(part, product):
            far[part] = product + far_in[0, part, 0]

        far_tile(upper, own, swapped, beyond, put)
        store.start()

    @pl.when(step == 1)
    def _():
        loads[2].wait()
        tile(2, ahead)

    @pl.when(step == last)
    def _():
        loads[3].wait()
        tile(3 - 2 * core, sib_ahead)
        store.wait()


def last_kernel(
    place, own_at, sib_own_at, sib_beyond_at, band_in, band_part, band, swapped, own, columns, sems
):
    core, half = place[0], pl.program_id(0)
    slot = 1 + 2 * core
    rows = band.shape[4]
    here = pl.ds(pl.multiple_of(half * rows, rows), rows)

    @pl.when(half == 0)
    def _():
        load = pltpu.make_async_copy(own_at, own, sems.at[0])
        load.start()
        for chosen, source in ((core == 0, sib_own_at), (core != 0, sib_beyond_at)):

            @pl.when(chosen)
            def _(source=source):
                other = pltpu.make_async_copy(source, columns, sems.at[1])
                other.start()
                other.wait()

        load.wait()
        swapped[...] = quadrature(own[...])

    for part, left in enumerate((own, swapped)):
        band[0, part, 0, 0] = (
            times(left[here, :], columns[...]) + band_in[0, part, 0, slot, here, :]
        )


IN_VMEM = pl.BlockSpec(memory_space=pltpu.VMEM)


def call(kernel, grid, place, blocks, sums, outs, specs, alias, tiles, scratch):
    rows, span = blocks[0].shape
    sums = [pltpu.with_memory_space_constraint(total, pltpu.VMEM) for total in sums]
    ins = [pl.BlockSpec(memory_space=pl.ANY)] * len(blocks) + [IN_VMEM] * len(sums)
    operands = [*blocks, *sums]
    aliases = {}
    if alias is not None:
        aliases = {1 + len(operands): 0}
        operands.append(alias)
        ins.append(pl.BlockSpec(memory_space=pl.ANY))
    return pl.pallas_call(
        kernel,
        out_shape=outs,
        grid_spec=pltpu.PrefetchScalarGridSpec(
            num_scalar_prefetch=1,
            grid=grid,
            in_specs=ins,
            out_specs=specs,
            scratch_shapes=[pltpu.VMEM((rows, span), jnp.bfloat16), *scratch],
        ),
        input_output_aliases=aliases,
        cost_estimate=pl.CostEstimate(
            flops=tiles * 4 * rows * rows * span,
            bytes_accessed=tiles * 8 * rows * rows,
            transcendentals=0,
        ),
        compiler_params=pltpu.CompilerParams(vmem_limit_bytes=VMEM_BYTES),
    )(place, *operands)


def shards(voltages):
    core = lax.axis_index("acol")
    upper = lax.axis_index("arow") // (lax.axis_size("arow") // 2)
    place = jnp.stack([core, upper]).astype(jnp.int32)

    early, late = halves(voltages)
    late_hub = from_ahead(late, 1)
    own = turn(early)
    late_ahead = turn(late_hub)

    down, up = own[:DOWN_ROWS], own[DOWN_ROWS:]
    down_1 = from_ahead(down, 1)
    up_1 = from_ahead(up, -1)
    up_2 = from_ahead(up_1, -1)
    down_2 = from_ahead(down_1, 1)
    up_3 = from_ahead(up_2, -1)
    sib_own = from_sibling(own, (0,))
    sib_down_1 = from_sibling(down_1)
    sib_up_2 = from_sibling(up_2, (1,))
    late_ahead, down_1, down_2, up_2, up_3, sib_own, sib_down_1, sib_up_2 = lax.optimization_barrier(
        (late_ahead, down_1, down_2, up_2, up_3, sib_own, sib_down_1, sib_up_2)
    )
    late_own = from_ahead(late_ahead, -1)
    late_beyond = from_ahead(late_ahead, 1)
    late_sib_ahead = from_sibling(late_ahead)

    sib_up_3 = from_sibling(up_3)
    sib_down_2 = from_sibling(down_2, (1,))

    rows = own.shape[0]
    block = pltpu.VMEM(own.shape, own.dtype)
    band_shape, far_shape = (1, 2, 1, 4, rows, rows), (1, 2, 1, rows // 2, rows)
    band_sum, far_sum = call(
        early_kernel, (1,), place,
        (own, down_1, up_3, down_2, up_2, sib_own, sib_down_1, sib_up_3, sib_down_2, sib_up_2), (),
        [pltpu.VMEM(band_shape, jnp.float32), pltpu.VMEM(far_shape, jnp.float32)],
        [IN_VMEM, IN_VMEM], None, 0,
        (block, block, block, block, block, pltpu.SemaphoreType.DMA((9,))),
    )
    late_own, late_beyond, late_sib_ahead, band_sum, far_sum = lax.optimization_barrier(
        (late_own, late_beyond, late_sib_ahead, band_sum, far_sum)
    )
    late_sib_own = from_sibling(late_own, (0,))
    late_sib_beyond = from_sibling(late_beyond, (1,))
    band_out = jax.ShapeDtypeStruct(band_shape, jnp.float32)
    far_out = jax.ShapeDtypeStruct(far_shape, jnp.float32)
    band, far = call(
        late_kernel, (3,), place, (late_own, late_ahead, late_beyond, late_sib_ahead),
        (band_sum, far_sum), [band_out, far_out],
        [
            pl.BlockSpec(
                (1, 2, 1, 1, rows, rows),
                lambda step, place: (
                    0, 0, 0,
                    jnp.where(step == 0, 0, jnp.where(step == 1, 2, 3 - 2 * place[0])),
                    0, 0,
                ),
            ),
            pl.BlockSpec(memory_space=pl.ANY),
        ],
        None, 4,
        (
            block, block, block, block,
            pltpu.VMEM((2, rows // 2, rows), jnp.float32), pltpu.SemaphoreType.DMA((5,)),
        ),
    )
    (band,) = call(
        last_kernel, (2,), place, (late_own, late_sib_own, late_sib_beyond), (band_sum,), [band_out],
        [
            pl.BlockSpec(
                (1, 2, 1, 1, rows // 2, rows),
                lambda half, place: (0, 0, 0, 1 + 2 * place[0], half, 0),
            )
        ],
        band, 1, (block, block, pltpu.SemaphoreType.DMA((2,))),
    )
    return band, far


def solution(mesh):
    return jax.shard_map(
        shards,
        mesh=mesh,
        in_specs=(P(None, ("arow", "acol"), "chan", None),),
        out_specs=(
            P("chan", None, ("arow", "acol"), None, None, None),
            P("chan", None, ("arow", "acol"), None, None),
        ),
        check_vma=False,
    )
```

time: 173 us -> 133 us (0.77); the launches traced: 170 us -> 132 us
  blocking collectives: 60.6 us -> 0 us
  starting transfers between devices: 4.27 us -> 50.5 us
  Pallas kernels: 0 us -> 23.1 us
  matrix products: 15 us -> 0 us
  waiting for transfers between devices: 71.7 us -> 57.5 us
  other arithmetic: 12.4 us -> 0.07 us
  local copies, waits for them, and re-layouts: 5.78 us -> 0.08 us
    all_to_all x1 -> x0, blocking collectives: 60.6 us -> none  [shards(): lax.all_to_all(voltages, 'chan', split_axis=0, concat_axis=2, tiled=True)]
    ppermute x4 -> x16, starting transfers between devices: 4.27 us -> 31.3 us  [the longest x8 18.4 us: from_sibling(): return lax.ppermute(block, 'acol', [(1 - core, core) for core in cores])]
    pallas_call x0 -> x4, Pallas kernels: none -> 23.1 us  [the longest x3 19.3 us: call(): pl.pallas_call(kernel, out_shape=outs, grid_spec=pltpu.PrefetchScalarGrid...]
    all_to_all x0 -> x2, starting transfers between devices: none -> 19.2 us  [turn(): lax.all_to_all(block, 'chan', split_axis=0, concat_axis=0, tiled=True)]
    ppermute x4 -> x16, waiting for transfers between devices: 71.7 us -> 54.4 us  [the longest x8 52.7 us: from_ahead(): lax.ppermute(block, 'arow', [((i + distance) % size, i) for i in range(si...]
    dot_general x5 -> x0, matrix products: 15 us -> none  [cross_tile(): jnp.einsum('crk,cjk->crj', left, right, preferred_element_type=jnp.float32)]
    concatenate x2 -> x0, other arithmetic: 10.8 us -> none  [stacked(): return jnp.concatenate([block, swapped], 1)]
    unnamed x5 -> x0, local copies, waits for them, and re-layouts: 5.78 us -> none
  transfers between devices with their start and end apart: 4 -> 18, of which waited for: 4 -> 9; matrix products, arithmetic and copies ran while one was open for 17% -> 0% of each run, Pallas kernels for 0% -> 11%
where the time goes in v1:
time: 133 us; the launch traced here: 132 us
  waiting for transfers between devices  57.5 us (43%)
  starting transfers between devices  50.5 us (38%)
  Pallas kernels  23.1 us (17%)
    ppermute x8, waiting for transfers between devices, from_ahead(): lax.ppermute(block, 'arow', [((i + distance) % size, i) for i in range(si...  52.7 us
    pallas_call x3, Pallas kernels, call(): pl.pallas_call(kernel, out_shape=outs, grid_spec=pltpu.PrefetchScalarGrid...  19.3 us
    all_to_all x2, starting transfers between devices, turn(): lax.all_to_all(block, 'chan', split_axis=0, concat_axis=0, tiled=True)  19.2 us
    ppermute x8, starting transfers between devices, from_sibling(): return lax.ppermute(block, 'acol', [(1 - core, core) for core in cores])  18.4 us
    ppermute x8, starting transfers between devices, from_ahead(): lax.ppermute(block, 'arow', [((i + distance) % size, i) for i in range(si...  12.9 us
    pallas_call x1, Pallas kernels, halves(): pl.pallas_call(cut_kernel, out_shape=(half, half), grid=(channels // step...  3.79 us
    all_to_all x2, waiting for transfers between devices, turn(): lax.all_to_all(block, 'chan', split_axis=0, concat_axis=0, tiled=True)  3.13 us
  transfers between devices with their start and end apart: 18, of which 9 were waited for; matrix products, arithmetic and copies ran while one was open for 0% of the time, Pallas kernels for 11%

profile of v1, /device:TPU:1, one launch (start us, length us, event | category | flops | bytes accessed | tf_op | source)
XLA Modules:
  0.0 132.2 jit_solution(14382158914167426191)
XLA Ops:
  0.6 3.8 %shard_map.30 = (bf16[32,16,1024]{2,1,0:T(8,128)(2,1)}, bf16[32,16,1024]{2,1,0:T(8,128)(2,1)}) custom-call(bf16[32,1,16,2048]{3,2,1,0:T(8,128)(2,1)} %voltages.1), custom_call_target="tpu_custom_call" | custom-call | tf_op jit(solution)/shard_map/pallas_call | solution.py:39
  4.4 11.9 %all-to-all-start.1 = ((bf16[32,16,1024]{2,1,0:T(8,128)(2,1)}), bf16[32,16,1024]{2,1,0:T(8,128)(2,1)S(1)}, u32[]{:S(2)}, u32[]{:S(2)}) async-start(bf16[32,16,1024]{2,1,0:T(8,128)(2,1)} %get-tuple-element.22), calls=%async_computation.1 | async-start | bytes 2097152 | tf_op jit(solution)/shard_map/all_to_all | solution.py:22
  16.3 2.8 %collective-permute-start = (bf16[32,16,1024]{2,1,0:T(8,128)(2,1)}, bf16[32,16,1024]{2,1,0:T(8,128)(2,1)}, u32[]{:S(2)}, u32[]{:S(2)}) collective-permute-start(bf16[32,16,1024]{2,1,0:T(8,128)(2,1)} %get-tuple-element.21), channel_id=1, source_target_pairs={{2,0},{4,2},{6,4},{0,6},{3,1},{5,3},{7,5},{1,7},{10,8},{12,10},{14... | collective-permute-start | bytes 3145736 | tf_op jit(solution)/shard_map/ppermute | solution.py:14
  19.1 21.8 %collective-permute-done = bf16[32,16,1024]{2,1,0:T(8,128)(2,1)} collective-permute-done((bf16[32,16,1024]{2,1,0:T(8,128)(2,1)}, bf16[32,16,1024]{2,1,0:T(8,128)(2,1)}, u32[]{:S(2)}, u32[]{:S(2)}) %collective-permute-start) | collective-permute-done | bytes 1048608 | tf_op jit(solution)/shard_map/ppermute | solution.py:14
  40.9 1.6 %all-to-all-done.1 = bf16[32,16,1024]{2,1,0:T(8,128)(2,1)S(1)} async-done(((bf16[32,16,1024]{2,1,0:T(8,128)(2,1)}), bf16[32,16,1024]{2,1,0:T(8,128)(2,1)S(1)}, u32[]{:S(2)}, u32[]{:S(2)}) %all-to-all-start.1) | async-done | bytes 1048608 | tf_op jit(solution)/shard_map/all_to_all | solution.py:22
  42.5 7.4 %all-to-all-start = ((bf16[32,16,1024]{2,1,0:T(8,128)(2,1)}), bf16[32,16,1024]{2,1,0:T(8,128)(2,1)S(1)}, u32[]{:S(2)}, u32[]{:S(2)}) async-start(bf16[32,16,1024]{2,1,0:T(8,128)(2,1)} %collective-permute-done), calls=%async_computation | async-start | bytes 2097152 | tf_op jit(solution)/shard_map/all_to_all | solution.py:22
  49.9 0.8 collective-permute-start.3
  50.8 2.7 %collective-permute-start.1 = (bf16[304,1024]{1,0:T(8,128)(2,1)S(1)}, bf16[304,1024]{1,0:T(8,128)(2,1)}, u32[]{:S(2)}, u32[]{:S(2)}) collective-permute-start(bf16[304,1024]{1,0:T(8,128)(2,1)S(1)} %bitcast.12), channel_id=1, source_target_pairs={{2,0},{4,2},{6,4},{0,6},{3,1},{5,3},{7,5},{1,7},{10,8},{12,10},{14... | collective-permute-start | bytes 1867784 | tf_op jit(solution)/shard_map/ppermute | solution.py:14
  53.5 4.7 %collective-permute-start.6 = (bf16[512,1024]{1,0:T(8,128)(2,1)S(1)}, bf16[512,1024]{1,0:T(8,128)(2,1)S(1)}, u32[]{:S(2)}, u32[]{:S(2)}) collective-permute-start(bf16[512,1024]{1,0:T(8,128)(2,1)S(1)} %bitcast.6), channel_id=1, source_target_pairs={{1,0},{3,2},{5,4},{7,6},{9,8},{11,10},{13,12},{15,14},{17,16},{19,... | collective-permute-start | bytes 3145736 | tf_op jit(solution)/shard_map/ppermute | solution.py:18
  58.2 2.9 %collective-permute-done.3 = bf16[208,1024]{1,0:T(8,128)(2,1)S(1)} collective-permute-done((bf16[208,1024]{1,0:T(8,128)(2,1)S(1)}, bf16[208,1024]{1,0:T(8,128)(2,1)S(1)}, u32[]{:S(2)}, u32[]{:S(2)}) %collective-permute-start.3) | collective-permute-done | bytes 426016 | tf_op jit(solution)/shard_map/ppermute | solution.py:14
  61.1 0.0 collective-permute-start.4
  61.1 3.3 %collective-permute-done.1.down_1 = bf16[304,1024]{1,0:T(8,128)(2,1)} collective-permute-done((bf16[304,1024]{1,0:T(8,128)(2,1)S(1)}, bf16[304,1024]{1,0:T(8,128)(2,1)}, u32[]{:S(2)}, u32[]{:S(2)}) %collective-permute-start.1) | collective-permute-done | bytes 622624 | tf_op jit(solution)/shard_map/ppermute | solution.py:14
  64.4 3.4 %collective-permute-start.7 = (bf16[304,1024]{1,0:T(8,128)(2,1)}, bf16[304,1024]{1,0:T(8,128)(2,1)}, u32[]{:S(2)}, u32[]{:S(2)}) collective-permute-start(bf16[304,1024]{1,0:T(8,128)(2,1)} %collective-permute-done.1.down_1), channel_id=1, source_target_pairs={{1,0},{0,1},{3,2},{2,3},{5,4},{4,5},{7,6},{6,7},{9,8},{8,9},{11,10... | collective-permute-start | bytes 1867784 | tf_op jit(solution)/shard_map/ppermute | solution.py:18
  67.8 3.5 %collective-permute-start.2 = (bf16[304,1024]{1,0:T(8,128)(2,1)}, bf16[304,1024]{1,0:T(8,128)(2,1)}, u32[]{:S(2)}, u32[]{:S(2)}) collective-permute-start(bf16[304,1024]{1,0:T(8,128)(2,1)} %collective-permute-done.1.down_1), channel_id=1, source_target_pairs={{2,0},{4,2},{6,4},{0,6},{3,1},{5,3},{7,5},{1,7},{10,8},{12,10},{14... | collective-permute-start | bytes 1867784 | tf_op jit(solution)/shard_map/ppermute | solution.py:14
  71.3 0.0 collective-permute-done.4.up_2
  71.3 1.3 collective-permute-start.8
  72.6 0.1 collective-permute-start.5
  72.7 1.6 %all-to-all-done = bf16[32,16,1024]{2,1,0:T(8,128)(2,1)S(1)} async-done(((bf16[32,16,1024]{2,1,0:T(8,128)(2,1)}), bf16[32,16,1024]{2,1,0:T(8,128)(2,1)S(1)}, u32[]{:S(2)}, u32[]{:S(2)}) %all-to-all-start) | async-done | bytes 1048608 | tf_op jit(solution)/shard_map/all_to_all | solution.py:22
  74.2 10.8 %collective-permute-done.2.down_2 = bf16[304,1024]{1,0:T(8,128)(2,1)} collective-permute-done((bf16[304,1024]{1,0:T(8,128)(2,1)}, bf16[304,1024]{1,0:T(8,128)(2,1)}, u32[]{:S(2)}, u32[]{:S(2)}) %collective-permute-start.2) | collective-permute-done | bytes 622624 | tf_op jit(solution)/shard_map/ppermute | solution.py:14
  85.1 1.3 %collective-permute-start.11 = (bf16[512,1024]{1,0:T(8,128)(2,1)S(1)}, bf16[512,1024]{1,0:T(8,128)(2,1)}, u32[]{:S(2)}, u32[]{:S(2)}) collective-permute-start(bf16[512,1024]{1,0:T(8,128)(2,1)S(1)} %bitcast.8), channel_id=1, source_target_pairs={{1,0},{0,1},{3,2},{2,3},{5,4},{4,5},{7,6},{6,7},{9,8},{8,9},{11,10... | collective-permute-start | bytes 3145736 | tf_op jit(solution)/shard_map/ppermute | solution.py:18
  86.4 2.9 %collective-permute-start.10 = (bf16[512,1024]{1,0:T(8,128)(2,1)S(1)}, bf16[512,1024]{1,0:T(8,128)(2,1)}, u32[]{:S(2)}, u32[]{:S(2)}) collective-permute-start(bf16[512,1024]{1,0:T(8,128)(2,1)S(1)} %bitcast.9), channel_id=1, source_target_pairs={{2,0},{4,2},{6,4},{0,6},{3,1},{5,3},{7,5},{1,7},{10,8},{12,10},{14... | collective-permute-start | bytes 3145736 | tf_op jit(solution)/shard_map/ppermute | solution.py:14
  89.3 1.3 collective-permute-start.13
  90.6 2.0 %collective-permute-start.12 = (bf16[208,1024]{1,0:T(8,128)(2,1)}, bf16[208,1024]{1,0:T(8,128)(2,1)}, u32[]{:S(2)}, u32[]{:S(2)}) collective-permute-start(bf16[208,1024]{1,0:T(8,128)(2,1)} %collective-permute-done.5.up_3), channel_id=1, source_target_pairs={{1,0},{0,1},{3,2},{2,3},{5,4},{4,5},{7,6},{6,7},{9,8},{8,9},{11,10... | collective-permute-start | bytes 1277960 | tf_op jit(solution)/shard_map/ppermute | solution.py:18
  92.6 0.1 pad_add_fusion.place
  92.7 1.7 %collective-permute-done.12.sib_up_3 = bf16[208,1024]{1,0:T(8,128)(2,1)} collective-permute-done((bf16[208,1024]{1,0:T(8,128)(2,1)}, bf16[208,1024]{1,0:T(8,128)(2,1)}, u32[]{:S(2)}, u32[]{:S(2)}) %collective-permute-start.12) | collective-permute-done | bytes 426016 | tf_op jit(solution)/shard_map/ppermute | solution.py:18
  94.3 6.8 %shard_map.31 = (f32[1,2,1,4,512,512]{5,4,3,2,1,0:T(8,128)S(1)}, f32[1,2,1,256,512]{4,3,2,1,0:T(8,128)S(1)}) custom-call(s32[2]{0:T(128)S(1)} %pad_add_fusion.place, bf16[512,1024]{1,0:T(8,128)(2,1)S(1)} %bitcast.7, bf16[304,1024]{1,0:T(8,128)(2,1)} %collective-permute-done.1.down_1, bf16[208,1024]{1,0:T(8,128)(2,1)} %collective-permute-done.5.up_3, ...), custom_call_target="tpu_custom_call" | custom-call | tf_op jit(solution)/shard_map/pallas_call | solution.py:219
  101.1 10.7 %collective-permute-done.10.beyond_at = bf16[512,1024]{1,0:T(8,128)(2,1)} collective-permute-done((bf16[512,1024]{1,0:T(8,128)(2,1)S(1)}, bf16[512,1024]{1,0:T(8,128)(2,1)}, u32[]{:S(2)}, u32[]{:S(2)}) %collective-permute-start.10) | collective-permute-done | bytes 1048608 | tf_op jit(solution)/shard_map/ppermute | solution.py:14
  111.8 3.2 %collective-permute-done.9.own_at = bf16[512,1024]{1,0:T(8,128)(2,1)} collective-permute-done((bf16[512,1024]{1,0:T(8,128)(2,1)S(1)}, bf16[512,1024]{1,0:T(8,128)(2,1)}, u32[]{:S(2)}, u32[]{:S(2)}) %collective-permute-start.9) | collective-permute-done | bytes 1048608 | tf_op jit(solution)/shard_map/ppermute | solution.py:14
  115.0 1.3 collective-permute-start.15
  116.3 3.2 %collective-permute-start.14 = (bf16[512,1024]{1,0:T(8,128)(2,1)}, bf16[512,1024]{1,0:T(8,128)(2,1)S(1)}, u32[]{:S(2)}, u32[]{:S(2)}) collective-permute-start(bf16[512,1024]{1,0:T(8,128)(2,1)} %collective-permute-done.9.own_at), channel_id=1, source_target_pairs={{1,0},{3,2},{5,4},{7,6},{9,8},{11,10},{13,12},{15,14},{17,16},{19,... | collective-permute-start | bytes 3145736 | tf_op jit(solution)/shard_map/ppermute | solution.py:18
  119.5 8.2 %shard_map.32 = (f32[1,2,1,4,512,512]{5,4,3,2,1,0:T(8,128)}, f32[1,2,1,256,512]{4,3,2,1,0:T(8,128)}) custom-call(s32[2]{0:T(128)S(1)} %pad_add_fusion.place, bf16[512,1024]{1,0:T(8,128)(2,1)} %collective-permute-done.9.own_at, bf16[512,1024]{1,0:T(8,128)(2,1)S(1)} %bitcast.11, bf16[512,1024]{1,0:T(8,128)(2,1)} %collective-permute-done.10.beyond_at, ...), custom_call_target="tpu_custom_call" | custom-call | flops 4294967296 | bytes 8388608 | tf_op jit(solution)/shard_map/pallas_call | solution.py:219
  127.7 4.4 %shard_map.33 = f32[1,2,1,4,512,512]{5,4,3,2,1,0:T(8,128)} custom-call(s32[2]{0:T(128)S(1)} %pad_add_fusion.place, bf16[512,1024]{1,0:T(8,128)(2,1)} %collective-permute-done.9.own_at, bf16[512,1024]{1,0:T(8,128)(2,1)S(1)} %collective-permute-done.14.sib_own_at, ...), custom_call_target="tpu_custom_call", output_to_operand_aliasing={{}: (5, {})} | custom-call | flops 1073741824 | bytes 2097152 | tf_op jit(solution)/shard_map/pallas_call | solution.py:219
  (11 shorter events, 0.1 us)
Async XLA Ops:
  4.4 38.1 %all-to-all-start.1 = ((bf16[32,16,1024]{2,1,0:T(8,128)(2,1)}), bf16[32,16,1024]{2,1,0:T(8,128)(2,1)S(1)}, u32[]{:S(2)}, u32[]{:S(2)}) async-start(bf16[32,16,1024]{2,1,0:T(8,128)(2,1)} %get-tuple-element.22), calls=%async_computation.1 | async-start | bytes 2097152 | tf_op jit(solution)/shard_map/all_to_all | solution.py:22
  16.3 24.6 %collective-permute-start = (bf16[32,16,1024]{2,1,0:T(8,128)(2,1)}, bf16[32,16,1024]{2,1,0:T(8,128)(2,1)}, u32[]{:S(2)}, u32[]{:S(2)}) collective-permute-start(bf16[32,16,1024]{2,1,0:T(8,128)(2,1)} %get-tuple-element.21), channel_id=1, source_target_pairs={{2,0},{4,2},{6,4},{0,6},{3,1},{5,3},{7,5},{1,7},{10,8},{12,10},{14... | collective-permute-start | bytes 3145736 | tf_op jit(solution)/shard_map/ppermute | solution.py:14
  42.5 31.7 %all-to-all-start = ((bf16[32,16,1024]{2,1,0:T(8,128)(2,1)}), bf16[32,16,1024]{2,1,0:T(8,128)(2,1)S(1)}, u32[]{:S(2)}, u32[]{:S(2)}) async-start(bf16[32,16,1024]{2,1,0:T(8,128)(2,1)} %collective-permute-done), calls=%async_computation | async-start | bytes 2097152 | tf_op jit(solution)/shard_map/all_to_all | solution.py:22
  49.9 11.2 %collective-permute-start.3 = (bf16[208,1024]{1,0:T(8,128)(2,1)S(1)}, bf16[208,1024]{1,0:T(8,128)(2,1)S(1)}, u32[]{:S(2)}, u32[]{:S(2)}) collective-permute-start(bf16[208,1024]{1,0:T(8,128)(2,1)S(1)} %bitcast.13), channel_id=1, source_target_pairs={{6,0},{0,2},{2,4},{4,6},{7,1},{1,3},{3,5},{5,7},{14,8},{8,10},{10,... | collective-permute-start | bytes 1277960 | tf_op jit(solution)/shard_map/ppermute | solution.py:14
  50.8 13.6 %collective-permute-start.1 = (bf16[304,1024]{1,0:T(8,128)(2,1)S(1)}, bf16[304,1024]{1,0:T(8,128)(2,1)}, u32[]{:S(2)}, u32[]{:S(2)}) collective-permute-start(bf16[304,1024]{1,0:T(8,128)(2,1)S(1)} %bitcast.12), channel_id=1, source_target_pairs={{2,0},{4,2},{6,4},{0,6},{3,1},{5,3},{7,5},{1,7},{10,8},{12,10},{14... | collective-permute-start | bytes 1867784 | tf_op jit(solution)/shard_map/ppermute | solution.py:14
  53.5 19.1 %collective-permute-start.6 = (bf16[512,1024]{1,0:T(8,128)(2,1)S(1)}, bf16[512,1024]{1,0:T(8,128)(2,1)S(1)}, u32[]{:S(2)}, u32[]{:S(2)}) collective-permute-start(bf16[512,1024]{1,0:T(8,128)(2,1)S(1)} %bitcast.6), channel_id=1, source_target_pairs={{1,0},{3,2},{5,4},{7,6},{9,8},{11,10},{13,12},{15,14},{17,16},{19,... | collective-permute-start | bytes 3145736 | tf_op jit(solution)/shard_map/ppermute | solution.py:18
  61.1 10.2 %collective-permute-start.4 = (bf16[208,1024]{1,0:T(8,128)(2,1)S(1)}, bf16[208,1024]{1,0:T(8,128)(2,1)}, u32[]{:S(2)}, u32[]{:S(2)}) collective-permute-start(bf16[208,1024]{1,0:T(8,128)(2,1)S(1)} %collective-permute-done.3), channel_id=1, source_target_pairs={{6,0},{0,2},{2,4},{4,6},{7,1},{1,3},{3,5},{5,7},{14,8},{8,10},{10,... | collective-permute-start | bytes 1277960 | tf_op jit(solution)/shard_map/ppermute | solution.py:14
  64.4 9.8 %collective-permute-start.7 = (bf16[304,1024]{1,0:T(8,128)(2,1)}, bf16[304,1024]{1,0:T(8,128)(2,1)}, u32[]{:S(2)}, u32[]{:S(2)}) collective-permute-start(bf16[304,1024]{1,0:T(8,128)(2,1)} %collective-permute-done.1.down_1), channel_id=1, source_target_pairs={{1,0},{0,1},{3,2},{2,3},{5,4},{4,5},{7,6},{6,7},{9,8},{8,9},{11,10... | collective-permute-start | bytes 1867784 | tf_op jit(solution)/shard_map/ppermute | solution.py:18
  67.8 17.3 %collective-permute-start.2 = (bf16[304,1024]{1,0:T(8,128)(2,1)}, bf16[304,1024]{1,0:T(8,128)(2,1)}, u32[]{:S(2)}, u32[]{:S(2)}) collective-permute-start(bf16[304,1024]{1,0:T(8,128)(2,1)} %collective-permute-done.1.down_1), channel_id=1, source_target_pairs={{2,0},{4,2},{6,4},{0,6},{3,1},{5,3},{7,5},{1,7},{10,8},{12,10},{14... | collective-permute-start | bytes 1867784 | tf_op jit(solution)/shard_map/ppermute | solution.py:14
  71.3 13.8 %collective-permute-start.8 = (bf16[208,1024]{1,0:T(8,128)(2,1)}, bf16[208,1024]{1,0:T(8,128)(2,1)}, u32[]{:S(2)}, u32[]{:S(2)}) collective-permute-start(bf16[208,1024]{1,0:T(8,128)(2,1)} %collective-permute-done.4.up_2), channel_id=1, source_target_pairs={{0,1},{2,3},{4,5},{6,7},{8,9},{10,11},{12,13},{14,15},{16,17},{18,... | collective-permute-start | bytes 1277960 | tf_op jit(solution)/shard_map/ppermute | solution.py:18
  72.6 12.5 %collective-permute-start.5 = (bf16[208,1024]{1,0:T(8,128)(2,1)}, bf16[208,1024]{1,0:T(8,128)(2,1)}, u32[]{:S(2)}, u32[]{:S(2)}) collective-permute-start(bf16[208,1024]{1,0:T(8,128)(2,1)} %collective-permute-done.4.up_2), channel_id=1, source_target_pairs={{6,0},{0,2},{2,4},{4,6},{7,1},{1,3},{3,5},{5,7},{14,8},{8,10},{10,... | collective-permute-start | bytes 1277960 | tf_op jit(solution)/shard_map/ppermute | solution.py:14
  85.1 16.0 %collective-permute-start.11 = (bf16[512,1024]{1,0:T(8,128)(2,1)S(1)}, bf16[512,1024]{1,0:T(8,128)(2,1)}, u32[]{:S(2)}, u32[]{:S(2)}) collective-permute-start(bf16[512,1024]{1,0:T(8,128)(2,1)S(1)} %bitcast.8), channel_id=1, source_target_pairs={{1,0},{0,1},{3,2},{2,3},{5,4},{4,5},{7,6},{6,7},{9,8},{8,9},{11,10... | collective-permute-start | bytes 3145736 | tf_op jit(solution)/shard_map/ppermute | solution.py:18
  86.4 25.4 %collective-permute-start.10 = (bf16[512,1024]{1,0:T(8,128)(2,1)S(1)}, bf16[512,1024]{1,0:T(8,128)(2,1)}, u32[]{:S(2)}, u32[]{:S(2)}) collective-permute-start(bf16[512,1024]{1,0:T(8,128)(2,1)S(1)} %bitcast.9), channel_id=1, source_target_pairs={{2,0},{4,2},{6,4},{0,6},{3,1},{5,3},{7,5},{1,7},{10,8},{12,10},{14... | collective-permute-start | bytes 3145736 | tf_op jit(solution)/shard_map/ppermute | solution.py:14
  89.3 25.7 %collective-permute-start.9 = (bf16[512,1024]{1,0:T(8,128)(2,1)S(1)}, bf16[512,1024]{1,0:T(8,128)(2,1)}, u32[]{:S(2)}, u32[]{:S(2)}) collective-permute-start(bf16[512,1024]{1,0:T(8,128)(2,1)S(1)} %bitcast.10), channel_id=1, source_target_pairs={{6,0},{0,2},{2,4},{4,6},{7,1},{1,3},{3,5},{5,7},{14,8},{8,10},{10,... | collective-permute-start | bytes 3145736 | tf_op jit(solution)/shard_map/ppermute | solution.py:14
  89.3 5.0 %collective-permute-start.13 = (bf16[304,1024]{1,0:T(8,128)(2,1)}, bf16[304,1024]{1,0:T(8,128)(2,1)}, u32[]{:S(2)}, u32[]{:S(2)}) collective-permute-start(bf16[304,1024]{1,0:T(8,128)(2,1)} %collective-permute-done.2.down_2), channel_id=1, source_target_pairs={{0,1},{2,3},{4,5},{6,7},{8,9},{10,11},{12,13},{14,15},{16,17},{18,... | collective-permute-start | bytes 1867784 | tf_op jit(solution)/shard_map/ppermute | solution.py:18
  90.6 3.7 %collective-permute-start.12 = (bf16[208,1024]{1,0:T(8,128)(2,1)}, bf16[208,1024]{1,0:T(8,128)(2,1)}, u32[]{:S(2)}, u32[]{:S(2)}) collective-permute-start(bf16[208,1024]{1,0:T(8,128)(2,1)} %collective-permute-done.5.up_3), channel_id=1, source_target_pairs={{1,0},{0,1},{3,2},{2,3},{5,4},{4,5},{7,6},{6,7},{9,8},{8,9},{11,10... | collective-permute-start | bytes 1277960 | tf_op jit(solution)/shard_map/ppermute | solution.py:18
  115.0 12.7 %collective-permute-start.15 = (bf16[512,1024]{1,0:T(8,128)(2,1)}, bf16[512,1024]{1,0:T(8,128)(2,1)S(1)}, u32[]{:S(2)}, u32[]{:S(2)}) collective-permute-start(bf16[512,1024]{1,0:T(8,128)(2,1)} %collective-permute-done.10.beyond_at), channel_id=1, source_target_pairs={{0,1},{2,3},{4,5},{6,7},{8,9},{10,11},{12,13},{14,15},{16,17},{18,... | collective-permute-start | bytes 3145736 | tf_op jit(solution)/shard_map/ppermute | solution.py:18
  116.3 11.4 %collective-permute-start.14 = (bf16[512,1024]{1,0:T(8,128)(2,1)}, bf16[512,1024]{1,0:T(8,128)(2,1)S(1)}, u32[]{:S(2)}, u32[]{:S(2)}) collective-permute-start(bf16[512,1024]{1,0:T(8,128)(2,1)} %collective-permute-done.9.own_at), channel_id=1, source_target_pairs={{1,0},{3,2},{5,4},{7,6},{9,8},{11,10},{13,12},{15,14},{17,16},{19,... | collective-permute-start | bytes 3145736 | tf_op jit(solution)/shard_map/ppermute | solution.py:18

commit v2 on v1

--- a/solution.py
+++ b/solution.py
@@ -23,26 +23,25 @@
     return turned.reshape(-1, block.shape[-1])
 
 
-def cut_kernel(voltages, early, late):
-    width = voltages.shape[-1] // 2
-    cut = width // 2
-    for part in range(2):
-        to = pl.ds(part * cut, cut)
-        early[:, :, to] = voltages[:, 0, :, pl.ds(part * width, cut)]
-        late[:, :, to] = voltages[:, 0, :, pl.ds(part * width + cut, cut)]
-
-
-def halves(voltages):
+def cut_kernel(real, imaginary, half):
+    cut = real.shape[-1]
+    half[:, :, :cut] = real[:, 0]
+    half[:, :, cut:] = imaginary[:, 0]
+
+
+def half_of(voltages, number):
     channels, _, rows, span = voltages.shape
-    step = channels // 4
-    half = jax.ShapeDtypeStruct((channels, rows, span // 2), voltages.dtype)
+    step, cut = channels // 2, span // 4
     return pl.pallas_call(
         cut_kernel,
-        out_shape=(half, half),
+        out_shape=jax.ShapeDtypeStruct((channels, rows, span // 2), voltages.dtype),
         grid=(channels // step,),
-        in_specs=[pl.BlockSpec((step, 1, rows, span), lambda i: (i, 0, 0, 0))],
-        out_specs=[pl.BlockSpec((step, rows, span // 2), lambda i: (i, 0, 0))] * 2,
-    )(voltages)
+        in_specs=[
+            pl.BlockSpec((step, 1, rows, cut), lambda i, part=part: (i, 0, 0, 2 * part + number))
+            for part in range(2)
+        ],
+        out_specs=pl.BlockSpec((step, rows, span // 2), lambda i: (i, 0, 0)),
+    )(voltages, voltages)
 
 
 def quadrature(rows):
@@ -133,19 +132,21 @@
 
 
 def late_kernel(
-    place, own_at, ahead_at, beyond_at, sib_ahead_at, band_in, far_in, band, far_at,
-    swapped, own, ahead, beyond, sib_ahead, far, sems,
+    place, band_in, far_in, own_at, ahead_at, beyond_at, sib_ahead_at, band, far_at, left,
+    ahead, beyond, sib_ahead, far, sems,
 ):
     core, upper = place[0], place[1]
     step = pl.program_id(0)
-    last = pl.num_programs(0) - 1
+    rows = ahead.shape[0]
+    own, swapped = left.at[pl.ds(0, rows)], left.at[pl.ds(rows, rows)]
     pairs = ((own_at, own), (beyond_at, beyond), (ahead_at, ahead), (sib_ahead_at, sib_ahead))
     loads = [pltpu.make_async_copy(*pair, sems.at[i]) for i, pair in enumerate(pairs)]
     store = pltpu.make_async_copy(far, far_at.at[0, :, 0], sems.at[4])
 
     def tile(slot, columns):
-        for part, left in enumerate((own, swapped)):
-            band[0, part, 0, 0] = times(left[...], columns[...]) + band_in[0, part, 0, slot]
+        product = times(left[...], columns[...])
+        band[0, 0, 0, 0] = product[:rows] + band_in[0, 0, 0, slot]
+        band[0, 1, 0, 0] = product[rows:] + band_in[0, 1, 0, slot]
 
     @pl.when(step == 0)
     def _():
@@ -154,6 +155,9 @@
         loads[0].wait()
         swapped[...] = quadrature(own[...])
         tile(0, own)
+
+    @pl.when(step == 1)
+    def _():
         loads[1].wait()
 
         def put(part, product):
@@ -161,72 +165,54 @@
 
         far_tile(upper, own, swapped, beyond, put)
         store.start()
-
-    @pl.when(step == 1)
-    def _():
         loads[2].wait()
         tile(2, ahead)
 
-    @pl.when(step == last)
+    @pl.when(step == 2)
     def _():
         loads[3].wait()
         tile(3 - 2 * core, sib_ahead)
         store.wait()
 
 
-def last_kernel(
-    place, own_at, sib_own_at, sib_beyond_at, band_in, band_part, band, swapped, own, columns, sems
-):
+def last_kernel(place, left, sib_own, sib_beyond, band_in, band_part, band):
     core, half = place[0], pl.program_id(0)
     slot = 1 + 2 * core
     rows = band.shape[4]
-    here = pl.ds(pl.multiple_of(half * rows, rows), rows)
-
-    @pl.when(half == 0)
-    def _():
-        load = pltpu.make_async_copy(own_at, own, sems.at[0])
-        load.start()
-        for chosen, source in ((core == 0, sib_own_at), (core != 0, sib_beyond_at)):
-
-            @pl.when(chosen)
-            def _(source=source):
-                other = pltpu.make_async_copy(source, columns, sems.at[1])
-                other.start()
-                other.wait()
-
-        load.wait()
-        swapped[...] = quadrature(own[...])
-
-    for part, left in enumerate((own, swapped)):
-        band[0, part, 0, 0] = (
-            times(left[here, :], columns[...]) + band_in[0, part, 0, slot, here, :]
-        )
+
+    for chosen, columns in ((core == 0, sib_own), (core != 0, sib_beyond)):
+
+        @pl.when(chosen)
+        def _(columns=columns):
+            for part in range(2):
+                here = pl.ds(pl.multiple_of(half * rows, rows), rows)
+                there = pl.ds(pl.multiple_of((2 * part + half) * rows, rows), rows)
+                band[0, part, 0, 0] = (
+                    times(left[there, :], columns[...]) + band_in[0, part, 0, slot, here, :]
+                )
 
 
 IN_VMEM = pl.BlockSpec(memory_space=pltpu.VMEM)
 
 
-def call(kernel, grid, place, blocks, sums, outs, specs, alias, tiles, scratch):
-    rows, span = blocks[0].shape
-    sums = [pltpu.with_memory_space_constraint(total, pltpu.VMEM) for total in sums]
-    ins = [pl.BlockSpec(memory_space=pl.ANY)] * len(blocks) + [IN_VMEM] * len(sums)
-    operands = [*blocks, *sums]
-    aliases = {}
-    if alias is not None:
-        aliases = {1 + len(operands): 0}
-        operands.append(alias)
-        ins.append(pl.BlockSpec(memory_space=pl.ANY))
+IN_PLACE = pl.BlockSpec(memory_space=pl.ANY)
+
+
+def call(kernel, grid, place, blocks, inside, outs, specs, aliases, tiles, scratch):
+    rows, span = outs[0].shape[-1], 1024
+    inside = [pltpu.with_memory_space_constraint(block, pltpu.VMEM) for block in inside]
+    operands = [*inside, *blocks]
     return pl.pallas_call(
         kernel,
         out_shape=outs,
         grid_spec=pltpu.PrefetchScalarGridSpec(
             num_scalar_prefetch=1,
             grid=grid,
-            in_specs=ins,
+            in_specs=[IN_VMEM] * len(inside) + [IN_PLACE] * len(blocks),
             out_specs=specs,
-            scratch_shapes=[pltpu.VMEM((rows, span), jnp.bfloat16), *scratch],
+            scratch_shapes=scratch,
         ),
-        input_output_aliases=aliases,
+        input_output_aliases={1 + key: value for key, value in aliases.items()},
         cost_estimate=pl.CostEstimate(
             flops=tiles * 4 * rows * rows * span,
             bytes_accessed=tiles * 8 * rows * rows,
@@ -241,7 +227,7 @@
     upper = lax.axis_index("arow") // (lax.axis_size("arow") // 2)
     place = jnp.stack([core, upper]).astype(jnp.int32)
 
-    early, late = halves(voltages)
+    early, late = half_of(voltages, 0), half_of(voltages, 1)
     late_hub = from_ahead(late, 1)
     own = turn(early)
     late_ahead = turn(late_hub)
@@ -255,8 +241,8 @@
     sib_own = from_sibling(own, (0,))
     sib_down_1 = from_sibling(down_1)
     sib_up_2 = from_sibling(up_2, (1,))
-    late_ahead, down_1, down_2, up_2, up_3, sib_own, sib_down_1, sib_up_2 = lax.optimization_barrier(
-        (late_ahead, down_1, down_2, up_2, up_3, sib_own, sib_down_1, sib_up_2)
+    late_ahead, down_1, up_2, sib_own, sib_down_1, sib_up_2 = lax.optimization_barrier(
+        (late_ahead, down_1, up_2, sib_own, sib_down_1, sib_up_2)
     )
     late_own = from_ahead(late_ahead, -1)
     late_beyond = from_ahead(late_ahead, 1)
@@ -272,8 +258,7 @@
         early_kernel, (1,), place,
         (own, down_1, up_3, down_2, up_2, sib_own, sib_down_1, sib_up_3, sib_down_2, sib_up_2), (),
         [pltpu.VMEM(band_shape, jnp.float32), pltpu.VMEM(far_shape, jnp.float32)],
-        [IN_VMEM, IN_VMEM], None, 0,
-        (block, block, block, block, block, pltpu.SemaphoreType.DMA((9,))),
+        [IN_VMEM, IN_VMEM], {}, 2, [block] * 6 + [pltpu.SemaphoreType.DMA((9,))],
     )
     late_own, late_beyond, late_sib_ahead, band_sum, far_sum = lax.optimization_barrier(
         (late_own, late_beyond, late_sib_ahead, band_sum, far_sum)
@@ -282,9 +267,10 @@
     late_sib_beyond = from_sibling(late_beyond, (1,))
     band_out = jax.ShapeDtypeStruct(band_shape, jnp.float32)
     far_out = jax.ShapeDtypeStruct(far_shape, jnp.float32)
-    band, far = call(
+    band, far, left = call(
         late_kernel, (3,), place, (late_own, late_ahead, late_beyond, late_sib_ahead),
-        (band_sum, far_sum), [band_out, far_out],
+        (band_sum, far_sum),
+        [band_out, far_out, pltpu.VMEM((2 * rows, late_own.shape[1]), late_own.dtype)],
         [
             pl.BlockSpec(
                 (1, 2, 1, 1, rows, rows),
@@ -294,23 +280,23 @@
                     0, 0,
                 ),
             ),
-            pl.BlockSpec(memory_space=pl.ANY),
+            IN_PLACE,
+            IN_VMEM,
         ],
-        None, 4,
-        (
-            block, block, block, block,
-            pltpu.VMEM((2, rows // 2, rows), jnp.float32), pltpu.SemaphoreType.DMA((5,)),
-        ),
+        {}, 4,
+        [block] * 3
+        + [pltpu.VMEM((2, rows // 2, rows), jnp.float32), pltpu.SemaphoreType.DMA((5,))],
     )
     (band,) = call(
-        last_kernel, (2,), place, (late_own, late_sib_own, late_sib_beyond), (band_sum,), [band_out],
+        last_kernel, (2,), place, (band,), (left, late_sib_own, late_sib_beyond, band_sum),
+        [band_out],
         [
             pl.BlockSpec(
                 (1, 2, 1, 1, rows // 2, rows),
                 lambda half, place: (0, 0, 0, 1 + 2 * place[0], half, 0),
             )
         ],
-        band, 1, (block, block, pltpu.SemaphoreType.DMA((2,))),
+        {4: 0}, 1, [],
     )
     return band, far
 

time: 133 us -> 126 us (0.947)
  waiting for transfers between devices: 57.5 us -> 40.8 us
  starting transfers between devices: 50.5 us -> 62.1 us
    ppermute x8, waiting for transfers between devices: 52.7 us -> 35.1 us  [from_ahead(): lax.ppermute(block, 'arow', [((i + distance) % size, i) for i in range(si...]
    ppermute x8, starting transfers between devices: 18.4 us -> 30.1 us  [from_sibling(): return lax.ppermute(block, 'acol', [(1 - core, core) for core in cores])]
    ppermute x8, waiting for transfers between devices: 1.68 us -> 4.92 us  [from_sibling(): return lax.ppermute(block, 'acol', [(1 - core, core) for core in cores])]
    all_to_all x2, waiting for transfers between devices: 3.13 us -> 0.8 us  [turn(): lax.all_to_all(block, 'chan', split_axis=0, concat_axis=0, tiled=True)]
    ppermute x8, starting transfers between devices: 12.9 us -> 11.3 us  [from_ahead(): lax.ppermute(block, 'arow', [((i + distance) % size, i) for i in range(si...]
    all_to_all x2, starting transfers between devices: 19.2 us -> 20.8 us  [turn(): lax.all_to_all(block, 'chan', split_axis=0, concat_axis=0, tiled=True)]
    pallas_call x3, Pallas kernels: 19.3 us -> 17.8 us  [call(): pl.pallas_call(kernel, out_shape=outs, grid_spec=pltpu.PrefetchScalarGrid...]
    pallas_call x1 -> x2, Pallas kernels: 3.79 us -> 4.1 us  [half_of(): pl.pallas_call(cut_kernel, out_shape=jax.ShapeDtypeStruct((channels, rows...]
  transfers between devices with their start and end apart: 18 -> 18, of which waited for: 9 -> 10; matrix products, arithmetic and copies ran while one was open for 0% -> 0% of each run, Pallas kernels for 11% -> 13%
where the time goes in v2:
time: 126 us
  starting transfers between devices  62.1 us (49%)
  waiting for transfers between devices  40.8 us (32%)
  Pallas kernels  21.9 us (17%)
    ppermute x8, waiting for transfers between devices, from_ahead(): lax.ppermute(block, 'arow', [((i + distance) % size, i) for i in range(si...  35.1 us
    ppermute x8, starting transfers between devices, from_sibling(): return lax.ppermute(block, 'acol', [(1 - core, core) for core in cores])  30.1 us
    all_to_all x2, starting transfers between devices, turn(): lax.all_to_all(block, 'chan', split_axis=0, concat_axis=0, tiled=True)  20.8 us
    pallas_call x3, Pallas kernels, call(): pl.pallas_call(kernel, out_shape=outs, grid_spec=pltpu.PrefetchScalarGrid...  17.8 us
    ppermute x8, starting transfers between devices, from_ahead(): lax.ppermute(block, 'arow', [((i + distance) % size, i) for i in range(si...  11.3 us
    ppermute x8, waiting for transfers between devices, from_sibling(): return lax.ppermute(block, 'acol', [(1 - core, core) for core in cores])  4.92 us
    pallas_call x2, Pallas kernels, half_of(): pl.pallas_call(cut_kernel, out_shape=jax.ShapeDtypeStruct((channels, rows...  4.1 us
  transfers between devices with their start and end apart: 18, of which 10 were waited for; matrix products, arithmetic and copies ran while one was open for 0% of the time, Pallas kernels for 13%

profile of v2, /device:TPU:1, one launch (start us, length us, event | category | flops | bytes accessed | tf_op | source)
XLA Modules:
  0.0 125.8 jit_solution(10276696070319806645)
XLA Ops:
  0.6 2.1 %shard_map.31 = bf16[32,16,1024]{2,1,0:T(8,128)(2,1)} custom-call(bf16[32,1,16,2048]{3,2,1,0:T(8,128)(2,1)} %imaginary.3, bf16[32,1,16,2048]{3,2,1,0:T(8,128)(2,1)} %imaginary.3), custom_call_target="tpu_custom_call" | custom-call | tf_op jit(solution)/shard_map/pallas_call | solution.py:35
  2.7 11.9 %all-to-all-start.1 = ((bf16[32,16,1024]{2,1,0:T(8,128)(2,1)}), bf16[32,16,1024]{2,1,0:T(8,128)(2,1)S(1)}, u32[]{:S(2)}, u32[]{:S(2)}) async-start(bf16[32,16,1024]{2,1,0:T(8,128)(2,1)} %shard_map.31), calls=%async_computation.1 | async-start | bytes 2097152 | tf_op jit(solution)/shard_map/all_to_all | solution.py:22
  14.6 2.1 %shard_map.30 = bf16[32,16,1024]{2,1,0:T(8,128)(2,1)} custom-call(bf16[32,1,16,2048]{3,2,1,0:T(8,128)(2,1)} %imaginary.3, bf16[32,1,16,2048]{3,2,1,0:T(8,128)(2,1)} %imaginary.3), custom_call_target="tpu_custom_call" | custom-call | tf_op jit(solution)/shard_map/pallas_call | solution.py:35
  16.6 2.7 %collective-permute-start = (bf16[32,16,1024]{2,1,0:T(8,128)(2,1)}, bf16[32,16,1024]{2,1,0:T(8,128)(2,1)}, u32[]{:S(2)}, u32[]{:S(2)}) collective-permute-start(bf16[32,16,1024]{2,1,0:T(8,128)(2,1)} %shard_map.30), channel_id=1, source_target_pairs={{2,0},{4,2},{6,4},{0,6},{3,1},{5,3},{7,5},{1,7},{10,8},{12,10},{14... | collective-permute-start | bytes 3145736 | tf_op jit(solution)/shard_map/ppermute | solution.py:14
  19.3 21.8 %collective-permute-done = bf16[32,16,1024]{2,1,0:T(8,128)(2,1)} collective-permute-done((bf16[32,16,1024]{2,1,0:T(8,128)(2,1)}, bf16[32,16,1024]{2,1,0:T(8,128)(2,1)}, u32[]{:S(2)}, u32[]{:S(2)}) %collective-permute-start) | collective-permute-done | bytes 1048608 | tf_op jit(solution)/shard_map/ppermute | solution.py:14
  41.2 8.9 %all-to-all-start = ((bf16[32,16,1024]{2,1,0:T(8,128)(2,1)}), bf16[32,16,1024]{2,1,0:T(8,128)(2,1)S(1)}, u32[]{:S(2)}, u32[]{:S(2)}) async-start(bf16[32,16,1024]{2,1,0:T(8,128)(2,1)} %collective-permute-done), calls=%async_computation | async-start | bytes 2097152 | tf_op jit(solution)/shard_map/all_to_all | solution.py:22
  50.1 0.8 collective-permute-start.2
  51.0 2.7 %collective-permute-start.1 = (bf16[304,1024]{1,0:T(8,128)(2,1)S(1)}, bf16[304,1024]{1,0:T(8,128)(2,1)}, u32[]{:S(2)}, u32[]{:S(2)}) collective-permute-start(bf16[304,1024]{1,0:T(8,128)(2,1)S(1)} %bitcast.12), channel_id=1, source_target_pairs={{2,0},{4,2},{6,4},{0,6},{3,1},{5,3},{7,5},{1,7},{10,8},{12,10},{14... | collective-permute-start | bytes 1867784 | tf_op jit(solution)/shard_map/ppermute | solution.py:14
  53.8 4.7 %collective-permute-start.4 = (bf16[512,1024]{1,0:T(8,128)(2,1)S(1)}, bf16[512,1024]{1,0:T(8,128)(2,1)S(1)}, u32[]{:S(2)}, u32[]{:S(2)}) collective-permute-start(bf16[512,1024]{1,0:T(8,128)(2,1)S(1)} %bitcast.6), channel_id=1, source_target_pairs={{1,0},{3,2},{5,4},{7,6},{9,8},{11,10},{13,12},{15,14},{17,16},{19,... | collective-permute-start | bytes 3145736 | tf_op jit(solution)/shard_map/ppermute | solution.py:18
  58.5 2.9 %collective-permute-done.2 = bf16[208,1024]{1,0:T(8,128)(2,1)S(1)} collective-permute-done((bf16[208,1024]{1,0:T(8,128)(2,1)S(1)}, bf16[208,1024]{1,0:T(8,128)(2,1)S(1)}, u32[]{:S(2)}, u32[]{:S(2)}) %collective-permute-start.2) | collective-permute-done | bytes 426016 | tf_op jit(solution)/shard_map/ppermute | solution.py:14
  61.3 3.3 %collective-permute-done.1.down_1 = bf16[304,1024]{1,0:T(8,128)(2,1)} collective-permute-done((bf16[304,1024]{1,0:T(8,128)(2,1)S(1)}, bf16[304,1024]{1,0:T(8,128)(2,1)}, u32[]{:S(2)}, u32[]{:S(2)}) %collective-permute-start.1) | collective-permute-done | bytes 622624 | tf_op jit(solution)/shard_map/ppermute | solution.py:14
  64.7 3.4 %collective-permute-start.5 = (bf16[304,1024]{1,0:T(8,128)(2,1)}, bf16[304,1024]{1,0:T(8,128)(2,1)}, u32[]{:S(2)}, u32[]{:S(2)}) collective-permute-start(bf16[304,1024]{1,0:T(8,128)(2,1)} %collective-permute-done.1.down_1), channel_id=1, source_target_pairs={{1,0},{0,1},{3,2},{2,3},{5,4},{4,5},{7,6},{6,7},{9,8},{8,9},{11,10... | collective-permute-start | bytes 1867784 | tf_op jit(solution)/shard_map/ppermute | solution.py:18
  68.0 2.8 %collective-permute-done.3.up_2 = bf16[208,1024]{1,0:T(8,128)(2,1)} collective-permute-done((bf16[208,1024]{1,0:T(8,128)(2,1)S(1)}, bf16[208,1024]{1,0:T(8,128)(2,1)}, u32[]{:S(2)}, u32[]{:S(2)}) %collective-permute-start.3) | collective-permute-done | bytes 426016 | tf_op jit(solution)/shard_map/ppermute | solution.py:14
  70.9 1.3 %collective-permute-start.6 = (bf16[208,1024]{1,0:T(8,128)(2,1)}, bf16[208,1024]{1,0:T(8,128)(2,1)}, u32[]{:S(2)}, u32[]{:S(2)}) collective-permute-start(bf16[208,1024]{1,0:T(8,128)(2,1)} %collective-permute-done.3.up_2), channel_id=1, source_target_pairs={{0,1},{2,3},{4,5},{6,7},{8,9},{10,11},{12,13},{14,15},{16,17},{18,... | collective-permute-start | bytes 1277960 | tf_op jit(solution)/shard_map/ppermute | solution.py:18
  72.1 0.8 collective-permute-start.11
  72.9 0.8 collective-permute-start.10
  73.7 0.8 all-to-all-done
  74.5 3.2 %collective-permute-done.6.sib_up_2 = bf16[208,1024]{1,0:T(8,128)(2,1)} collective-permute-done((bf16[208,1024]{1,0:T(8,128)(2,1)}, bf16[208,1024]{1,0:T(8,128)(2,1)}, u32[]{:S(2)}, u32[]{:S(2)}) %collective-permute-start.6) | collective-permute-done | bytes 426016 | tf_op jit(solution)/shard_map/ppermute | solution.py:18
  77.7 1.5 %collective-permute-start.9 = (bf16[512,1024]{1,0:T(8,128)(2,1)S(1)}, bf16[512,1024]{1,0:T(8,128)(2,1)}, u32[]{:S(2)}, u32[]{:S(2)}) collective-permute-start(bf16[512,1024]{1,0:T(8,128)(2,1)S(1)} %bitcast.8), channel_id=1, source_target_pairs={{1,0},{0,1},{3,2},{2,3},{5,4},{4,5},{7,6},{6,7},{9,8},{8,9},{11,10... | collective-permute-start | bytes 3145736 | tf_op jit(solution)/shard_map/ppermute | solution.py:18
  79.2 3.4 %collective-permute-start.8 = (bf16[512,1024]{1,0:T(8,128)(2,1)S(1)}, bf16[512,1024]{1,0:T(8,128)(2,1)}, u32[]{:S(2)}, u32[]{:S(2)}) collective-permute-start(bf16[512,1024]{1,0:T(8,128)(2,1)S(1)} %bitcast.9), channel_id=1, source_target_pairs={{2,0},{4,2},{6,4},{0,6},{3,1},{5,3},{7,5},{1,7},{10,8},{12,10},{14... | collective-permute-start | bytes 3145736 | tf_op jit(solution)/shard_map/ppermute | solution.py:14
  82.6 0.7 collective-permute-done.11.down_2
  83.4 1.3 %collective-permute-start.13 = (bf16[304,1024]{1,0:T(8,128)(2,1)}, bf16[304,1024]{1,0:T(8,128)(2,1)}, u32[]{:S(2)}, u32[]{:S(2)}) collective-permute-start(bf16[304,1024]{1,0:T(8,128)(2,1)} %collective-permute-done.11.down_2), channel_id=1, source_target_pairs={{0,1},{2,3},{4,5},{6,7},{8,9},{10,11},{12,13},{14,15},{16,17},{18,... | collective-permute-start | bytes 1867784 | tf_op jit(solution)/shard_map/ppermute | solution.py:18
  84.7 11.7 %collective-permute-start.12 = (bf16[208,1024]{1,0:T(8,128)(2,1)}, bf16[208,1024]{1,0:T(8,128)(2,1)}, u32[]{:S(2)}, u32[]{:S(2)}) collective-permute-start(bf16[208,1024]{1,0:T(8,128)(2,1)} %collective-permute-done.10.up_3), channel_id=1, source_target_pairs={{1,0},{0,1},{3,2},{2,3},{5,4},{4,5},{7,6},{6,7},{9,8},{8,9},{11,10... | collective-permute-start | bytes 1277960 | tf_op jit(solution)/shard_map/ppermute | solution.py:18
  96.4 0.1 pad_add_fusion.place
  96.4 1.7 %collective-permute-done.12.sib_up_3 = bf16[208,1024]{1,0:T(8,128)(2,1)} collective-permute-done((bf16[208,1024]{1,0:T(8,128)(2,1)}, bf16[208,1024]{1,0:T(8,128)(2,1)}, u32[]{:S(2)}, u32[]{:S(2)}) %collective-permute-start.12) | collective-permute-done | bytes 426016 | tf_op jit(solution)/shard_map/ppermute | solution.py:18
  98.1 6.8 %shard_map.32 = (f32[1,2,1,4,512,512]{5,4,3,2,1,0:T(8,128)S(1)}, f32[1,2,1,256,512]{4,3,2,1,0:T(8,128)S(1)}) custom-call(s32[2]{0:T(128)S(1)} %pad_add_fusion.place, bf16[512,1024]{1,0:T(8,128)(2,1)S(1)} %bitcast.7, bf16[304,1024]{1,0:T(8,128)(2,1)} %collective-permute-done.1.down_1, bf16[208,1024]{1,0:T(8,128)(2,1)} %collective-permute-done.10.up_3, ...), custom_call_target="tpu_custom_call" | custom-call | flops 2147483648 | bytes 4194304 | tf_op jit(solution)/shard_map/pallas_call | solution.py:205
  104.9 0.9 collective-permute-done.8.beyond_at
  105.8 2.6 %collective-permute-done.7.own_at = bf16[512,1024]{1,0:T(8,128)(2,1)} collective-permute-done((bf16[512,1024]{1,0:T(8,128)(2,1)S(1)}, bf16[512,1024]{1,0:T(8,128)(2,1)}, u32[]{:S(2)}, u32[]{:S(2)}) %collective-permute-start.7) | collective-permute-done | bytes 1048608 | tf_op jit(solution)/shard_map/ppermute | solution.py:14
  108.4 5.0 %collective-permute-start.14 = (bf16[512,1024]{1,0:T(8,128)(2,1)}, bf16[512,1024]{1,0:T(8,128)(2,1)S(1)}, u32[]{:S(2)}, u32[]{:S(2)}) collective-permute-start(bf16[512,1024]{1,0:T(8,128)(2,1)} %collective-permute-done.7.own_at), channel_id=1, source_target_pairs={{1,0},{3,2},{5,4},{7,6},{9,8},{11,10},{13,12},{15,14},{17,16},{19,... | collective-permute-start | bytes 3145736 | tf_op jit(solution)/shard_map/ppermute | solution.py:18
  113.4 1.3 %collective-permute-start.15 = (bf16[512,1024]{1,0:T(8,128)(2,1)}, bf16[512,1024]{1,0:T(8,128)(2,1)S(1)}, u32[]{:S(2)}, u32[]{:S(2)}) collective-permute-start(bf16[512,1024]{1,0:T(8,128)(2,1)} %collective-permute-done.8.beyond_at), channel_id=1, source_target_pairs={{0,1},{2,3},{4,5},{6,7},{8,9},{10,11},{12,13},{14,15},{16,17},{18,... | collective-permute-start | bytes 3145736 | tf_op jit(solution)/shard_map/ppermute | solution.py:18
  114.7 7.9 %shard_map.33 = (f32[1,2,1,4,512,512]{5,4,3,2,1,0:T(8,128)}, f32[1,2,1,256,512]{4,3,2,1,0:T(8,128)}, bf16[1024,1024]{1,0:T(8,128)(2,1)S(1)}) custom-call(s32[2]{0:T(128)S(1)} %pad_add_fusion.place, f32[1,2,1,4,512,512]{5,4,3,2,1,0:T(8,128)S(1)} %get-tuple-element.26.band_in, f32[1,2,1,256,512]{4,3,2,1,0:T(8,128)S(1)} %get-tuple-element.27.far_in, ...), custom_call_target="tpu_custom_call" | custom-call | flops 4294967296 | bytes 8388608 | tf_op jit(solution)/shard_map/pallas_call | solution.py:205
  122.7 3.1 %shard_map.34 = f32[1,2,1,4,512,512]{5,4,3,2,1,0:T(8,128)} custom-call(s32[2]{0:T(128)S(1)} %pad_add_fusion.place, bf16[1024,1024]{1,0:T(8,128)(2,1)S(1)} %get-tuple-element.31.left, bf16[512,1024]{1,0:T(8,128)(2,1)S(1)} %collective-permute-done.14.sib_own, bf16[512,1024]{1,0:T(8,128)(2,1)S(1)} %collective-permute-done.15.sib_beyond, ...), custom_call_target="tpu_custom_call", output_to_operand_aliasing={{}: (5, {})} | custom-call | flops 1073741824 | bytes 2097152 | tf_op jit(solution)/shard_map/pallas_call | solution.py:205
  (12 shorter events, 0.1 us)
Async XLA Ops:
  2.7 38.5 %all-to-all-start.1 = ((bf16[32,16,1024]{2,1,0:T(8,128)(2,1)}), bf16[32,16,1024]{2,1,0:T(8,128)(2,1)S(1)}, u32[]{:S(2)}, u32[]{:S(2)}) async-start(bf16[32,16,1024]{2,1,0:T(8,128)(2,1)} %shard_map.31), calls=%async_computation.1 | async-start | bytes 2097152 | tf_op jit(solution)/shard_map/all_to_all | solution.py:22
  16.6 24.6 %collective-permute-start = (bf16[32,16,1024]{2,1,0:T(8,128)(2,1)}, bf16[32,16,1024]{2,1,0:T(8,128)(2,1)}, u32[]{:S(2)}, u32[]{:S(2)}) collective-permute-start(bf16[32,16,1024]{2,1,0:T(8,128)(2,1)} %shard_map.30), channel_id=1, source_target_pairs={{2,0},{4,2},{6,4},{0,6},{3,1},{5,3},{7,5},{1,7},{10,8},{12,10},{14... | collective-permute-start | bytes 3145736 | tf_op jit(solution)/shard_map/ppermute | solution.py:14
  41.2 33.3 %all-to-all-start = ((bf16[32,16,1024]{2,1,0:T(8,128)(2,1)}), bf16[32,16,1024]{2,1,0:T(8,128)(2,1)S(1)}, u32[]{:S(2)}, u32[]{:S(2)}) async-start(bf16[32,16,1024]{2,1,0:T(8,128)(2,1)} %collective-permute-done), calls=%async_computation | async-start | bytes 2097152 | tf_op jit(solution)/shard_map/all_to_all | solution.py:22
  50.1 11.2 %collective-permute-start.2 = (bf16[208,1024]{1,0:T(8,128)(2,1)S(1)}, bf16[208,1024]{1,0:T(8,128)(2,1)S(1)}, u32[]{:S(2)}, u32[]{:S(2)}) collective-permute-start(bf16[208,1024]{1,0:T(8,128)(2,1)S(1)} %bitcast.13), channel_id=1, source_target_pairs={{6,0},{0,2},{2,4},{4,6},{7,1},{1,3},{3,5},{5,7},{14,8},{8,10},{10,... | collective-permute-start | bytes 1277960 | tf_op jit(solution)/shard_map/ppermute | solution.py:14
  51.0 13.6 %collective-permute-start.1 = (bf16[304,1024]{1,0:T(8,128)(2,1)S(1)}, bf16[304,1024]{1,0:T(8,128)(2,1)}, u32[]{:S(2)}, u32[]{:S(2)}) collective-permute-start(bf16[304,1024]{1,0:T(8,128)(2,1)S(1)} %bitcast.12), channel_id=1, source_target_pairs={{2,0},{4,2},{6,4},{0,6},{3,1},{5,3},{7,5},{1,7},{10,8},{12,10},{14... | collective-permute-start | bytes 1867784 | tf_op jit(solution)/shard_map/ppermute | solution.py:14
  53.8 20.7 %collective-permute-start.4 = (bf16[512,1024]{1,0:T(8,128)(2,1)S(1)}, bf16[512,1024]{1,0:T(8,128)(2,1)S(1)}, u32[]{:S(2)}, u32[]{:S(2)}) collective-permute-start(bf16[512,1024]{1,0:T(8,128)(2,1)S(1)} %bitcast.6), channel_id=1, source_target_pairs={{1,0},{3,2},{5,4},{7,6},{9,8},{11,10},{13,12},{15,14},{17,16},{19,... | collective-permute-start | bytes 3145736 | tf_op jit(solution)/shard_map/ppermute | solution.py:18
  61.3 9.5 %collective-permute-start.3 = (bf16[208,1024]{1,0:T(8,128)(2,1)S(1)}, bf16[208,1024]{1,0:T(8,128)(2,1)}, u32[]{:S(2)}, u32[]{:S(2)}) collective-permute-start(bf16[208,1024]{1,0:T(8,128)(2,1)S(1)} %collective-permute-done.2), channel_id=1, source_target_pairs={{6,0},{0,2},{2,4},{4,6},{7,1},{1,3},{3,5},{5,7},{14,8},{8,10},{10,... | collective-permute-start | bytes 1277960 | tf_op jit(solution)/shard_map/ppermute | solution.py:14
  64.7 9.8 %collective-permute-start.5 = (bf16[304,1024]{1,0:T(8,128)(2,1)}, bf16[304,1024]{1,0:T(8,128)(2,1)}, u32[]{:S(2)}, u32[]{:S(2)}) collective-permute-start(bf16[304,1024]{1,0:T(8,128)(2,1)} %collective-permute-done.1.down_1), channel_id=1, source_target_pairs={{1,0},{0,1},{3,2},{2,3},{5,4},{4,5},{7,6},{6,7},{9,8},{8,9},{11,10... | collective-permute-start | bytes 1867784 | tf_op jit(solution)/shard_map/ppermute | solution.py:18
  70.9 6.9 %collective-permute-start.6 = (bf16[208,1024]{1,0:T(8,128)(2,1)}, bf16[208,1024]{1,0:T(8,128)(2,1)}, u32[]{:S(2)}, u32[]{:S(2)}) collective-permute-start(bf16[208,1024]{1,0:T(8,128)(2,1)} %collective-permute-done.3.up_2), channel_id=1, source_target_pairs={{0,1},{2,3},{4,5},{6,7},{8,9},{10,11},{12,13},{14,15},{16,17},{18,... | collective-permute-start | bytes 1277960 | tf_op jit(solution)/shard_map/ppermute | solution.py:18
  72.1 11.2 %collective-permute-start.11 = (bf16[304,1024]{1,0:T(8,128)(2,1)}, bf16[304,1024]{1,0:T(8,128)(2,1)}, u32[]{:S(2)}, u32[]{:S(2)}) collective-permute-start(bf16[304,1024]{1,0:T(8,128)(2,1)} %collective-permute-done.1.down_1), channel_id=1, source_target_pairs={{2,0},{4,2},{6,4},{0,6},{3,1},{5,3},{7,5},{1,7},{10,8},{12,10},{14... | collective-permute-start | bytes 1867784 | tf_op jit(solution)/shard_map/ppermute | solution.py:14
  72.9 11.7 %collective-permute-start.10 = (bf16[208,1024]{1,0:T(8,128)(2,1)}, bf16[208,1024]{1,0:T(8,128)(2,1)}, u32[]{:S(2)}, u32[]{:S(2)}) collective-permute-start(bf16[208,1024]{1,0:T(8,128)(2,1)} %collective-permute-done.3.up_2), channel_id=1, source_target_pairs={{6,0},{0,2},{2,4},{4,6},{7,1},{1,3},{3,5},{5,7},{14,8},{8,10},{10,... | collective-permute-start | bytes 1277960 | tf_op jit(solution)/shard_map/ppermute | solution.py:14
  77.7 27.2 %collective-permute-start.9 = (bf16[512,1024]{1,0:T(8,128)(2,1)S(1)}, bf16[512,1024]{1,0:T(8,128)(2,1)}, u32[]{:S(2)}, u32[]{:S(2)}) collective-permute-start(bf16[512,1024]{1,0:T(8,128)(2,1)S(1)} %bitcast.8), channel_id=1, source_target_pairs={{1,0},{0,1},{3,2},{2,3},{5,4},{4,5},{7,6},{6,7},{9,8},{8,9},{11,10... | collective-permute-start | bytes 3145736 | tf_op jit(solution)/shard_map/ppermute | solution.py:18
  79.2 26.6 %collective-permute-start.8 = (bf16[512,1024]{1,0:T(8,128)(2,1)S(1)}, bf16[512,1024]{1,0:T(8,128)(2,1)}, u32[]{:S(2)}, u32[]{:S(2)}) collective-permute-start(bf16[512,1024]{1,0:T(8,128)(2,1)S(1)} %bitcast.9), channel_id=1, source_target_pairs={{2,0},{4,2},{6,4},{0,6},{3,1},{5,3},{7,5},{1,7},{10,8},{12,10},{14... | collective-permute-start | bytes 3145736 | tf_op jit(solution)/shard_map/ppermute | solution.py:14
  82.6 25.8 %collective-permute-start.7 = (bf16[512,1024]{1,0:T(8,128)(2,1)S(1)}, bf16[512,1024]{1,0:T(8,128)(2,1)}, u32[]{:S(2)}, u32[]{:S(2)}) collective-permute-start(bf16[512,1024]{1,0:T(8,128)(2,1)S(1)} %bitcast.10), channel_id=1, source_target_pairs={{6,0},{0,2},{2,4},{4,6},{7,1},{1,3},{3,5},{5,7},{14,8},{8,10},{10,... | collective-permute-start | bytes 3145736 | tf_op jit(solution)/shard_map/ppermute | solution.py:14
  83.4 14.8 %collective-permute-start.13 = (bf16[304,1024]{1,0:T(8,128)(2,1)}, bf16[304,1024]{1,0:T(8,128)(2,1)}, u32[]{:S(2)}, u32[]{:S(2)}) collective-permute-start(bf16[304,1024]{1,0:T(8,128)(2,1)} %collective-permute-done.11.down_2), channel_id=1, source_target_pairs={{0,1},{2,3},{4,5},{6,7},{8,9},{10,11},{12,13},{14,15},{16,17},{18,... | collective-permute-start | bytes 1867784 | tf_op jit(solution)/shard_map/ppermute | solution.py:18
  84.7 13.5 %collective-permute-start.12 = (bf16[208,1024]{1,0:T(8,128)(2,1)}, bf16[208,1024]{1,0:T(8,128)(2,1)}, u32[]{:S(2)}, u32[]{:S(2)}) collective-permute-start(bf16[208,1024]{1,0:T(8,128)(2,1)} %collective-permute-done.10.up_3), channel_id=1, source_target_pairs={{1,0},{0,1},{3,2},{2,3},{5,4},{4,5},{7,6},{6,7},{9,8},{8,9},{11,10... | collective-permute-start | bytes 1277960 | tf_op jit(solution)/shard_map/ppermute | solution.py:18
  108.4 14.2 %collective-permute-start.14 = (bf16[512,1024]{1,0:T(8,128)(2,1)}, bf16[512,1024]{1,0:T(8,128)(2,1)S(1)}, u32[]{:S(2)}, u32[]{:S(2)}) collective-permute-start(bf16[512,1024]{1,0:T(8,128)(2,1)} %collective-permute-done.7.own_at), channel_id=1, source_target_pairs={{1,0},{3,2},{5,4},{7,6},{9,8},{11,10},{13,12},{15,14},{17,16},{19,... | collective-permute-start | bytes 3145736 | tf_op jit(solution)/shard_map/ppermute | solution.py:18
  113.4 9.2 %collective-permute-start.15 = (bf16[512,1024]{1,0:T(8,128)(2,1)}, bf16[512,1024]{1,0:T(8,128)(2,1)S(1)}, u32[]{:S(2)}, u32[]{:S(2)}) collective-permute-start(bf16[512,1024]{1,0:T(8,128)(2,1)} %collective-permute-done.8.beyond_at), channel_id=1, source_target_pairs={{0,1},{2,3},{4,5},{6,7},{8,9},{10,11},{12,13},{14,15},{16,17},{18,... | collective-permute-start | bytes 3145736 | tf_op jit(solution)/shard_map/ppermute | solution.py:18

commit v3 on v2

--- a/solution.py
+++ b/solution.py
@@ -12,6 +12,16 @@
 def from_ahead(block, distance):
     size = lax.axis_size("arow")
     return lax.ppermute(block, "arow", [((i + distance) % size, i) for i in range(size)])
+
+
+def from_both_sides(block, core_ahead):
+    size, cores = lax.axis_size("arow"), lax.axis_size("acol")
+    route = [
+        (((i + (1 if core == core_ahead else -1)) % size) * cores + core, i * cores + core)
+        for i in range(size)
+        for core in range(cores)
+    ]
+    return lax.ppermute(block, ("arow", "acol"), route)
 
 
 def from_sibling(block, cores=(0, 1)):
@@ -132,16 +142,21 @@
 
 
 def late_kernel(
-    place, band_in, far_in, own_at, ahead_at, beyond_at, sib_ahead_at, band, far_at, left,
-    ahead, beyond, sib_ahead, far, sems,
+    place, band_in, far_in, first, second, ahead_at, sib_ahead_at, sib_first, band, far_at, left,
+    ahead, beyond, sib_ahead, other, far, sems,
 ):
     core, upper = place[0], place[1]
     step = pl.program_id(0)
     rows = ahead.shape[0]
     own, swapped = left.at[pl.ds(0, rows)], left.at[pl.ds(rows, rows)]
-    pairs = ((own_at, own), (beyond_at, beyond), (ahead_at, ahead), (sib_ahead_at, sib_ahead))
-    loads = [pltpu.make_async_copy(*pair, sems.at[i]) for i, pair in enumerate(pairs)]
-    store = pltpu.make_async_copy(far, far_at.at[0, :, 0], sems.at[4])
+
+    def load(number, source, target):
+        return pltpu.make_async_copy(source, target, sems.at[number])
+
+    loads = [
+        load(2, ahead_at, ahead), load(3, sib_ahead_at, sib_ahead), load(4, sib_first, other)
+    ]
+    store = pltpu.make_async_copy(far, far_at.at[0, :, 0], sems.at[5])
 
     def tile(slot, columns):
         product = times(left[...], columns[...])
@@ -150,46 +165,44 @@
 
     @pl.when(step == 0)
     def _():
-        for load in loads:
-            load.start()
-        loads[0].wait()
+        @pl.when(core == 0)
+        def _():
+            load(0, second, own).start()
+            load(1, first, beyond).start()
+
+        @pl.when(core != 0)
+        def _():
+            load(0, first, own).start()
+            load(1, second, beyond).start()
+
+        for copy in loads:
+            copy.start()
+        load(0, first, own).wait()
         swapped[...] = quadrature(own[...])
         tile(0, own)
 
     @pl.when(step == 1)
     def _():
-        loads[1].wait()
+        load(1, second, beyond).wait()
 
         def put(part, product):
             far[part] = product + far_in[0, part, 0]
 
         far_tile(upper, own, swapped, beyond, put)
         store.start()
+        loads[0].wait()
+        tile(2, ahead)
+
+    @pl.when(step == 2)
+    def _():
+        loads[1].wait()
+        tile(3 - 2 * core, sib_ahead)
+
+    @pl.when(step == 3)
+    def _():
         loads[2].wait()
-        tile(2, ahead)
-
-    @pl.when(step == 2)
-    def _():
-        loads[3].wait()
-        tile(3 - 2 * core, sib_ahead)
+        tile(1 + 2 * core, other)
         store.wait()
-
-
-def last_kernel(place, left, sib_own, sib_beyond, band_in, band_part, band):
-    core, half = place[0], pl.program_id(0)
-    slot = 1 + 2 * core
-    rows = band.shape[4]
-
-    for chosen, columns in ((core == 0, sib_own), (core != 0, sib_beyond)):
-
-        @pl.when(chosen)
-        def _(columns=columns):
-            for part in range(2):
-                here = pl.ds(pl.multiple_of(half * rows, rows), rows)
-                there = pl.ds(pl.multiple_of((2 * part + half) * rows, rows), rows)
-                band[0, part, 0, 0] = (
-                    times(left[there, :], columns[...]) + band_in[0, part, 0, slot, here, :]
-                )
 
 
 IN_VMEM = pl.BlockSpec(memory_space=pltpu.VMEM)
@@ -244,8 +257,7 @@
     late_ahead, down_1, up_2, sib_own, sib_down_1, sib_up_2 = lax.optimization_barrier(
         (late_ahead, down_1, up_2, sib_own, sib_down_1, sib_up_2)
     )
-    late_own = from_ahead(late_ahead, -1)
-    late_beyond = from_ahead(late_ahead, 1)
+    late_first = from_both_sides(late_ahead, 0)
     late_sib_ahead = from_sibling(late_ahead)
 
     sib_up_3 = from_sibling(up_3)
@@ -260,43 +272,33 @@
         [pltpu.VMEM(band_shape, jnp.float32), pltpu.VMEM(far_shape, jnp.float32)],
         [IN_VMEM, IN_VMEM], {}, 2, [block] * 6 + [pltpu.SemaphoreType.DMA((9,))],
     )
-    late_own, late_beyond, late_sib_ahead, band_sum, far_sum = lax.optimization_barrier(
-        (late_own, late_beyond, late_sib_ahead, band_sum, far_sum)
-    )
-    late_sib_own = from_sibling(late_own, (0,))
-    late_sib_beyond = from_sibling(late_beyond, (1,))
+    late_ahead, late_sib_ahead, late_first, band_sum, far_sum = lax.optimization_barrier(
+        (late_ahead, late_sib_ahead, late_first, band_sum, far_sum)
+    )
+    late_second = from_both_sides(late_ahead, 1)
+    late_sib_first = from_sibling(late_first)
     band_out = jax.ShapeDtypeStruct(band_shape, jnp.float32)
     far_out = jax.ShapeDtypeStruct(far_shape, jnp.float32)
-    band, far, left = call(
-        late_kernel, (3,), place, (late_own, late_ahead, late_beyond, late_sib_ahead),
-        (band_sum, far_sum),
-        [band_out, far_out, pltpu.VMEM((2 * rows, late_own.shape[1]), late_own.dtype)],
+    band, far = call(
+        late_kernel, (4,), place,
+        (late_first, late_second, late_ahead, late_sib_ahead, late_sib_first),
+        (band_sum, far_sum), [band_out, far_out],
         [
             pl.BlockSpec(
                 (1, 2, 1, 1, rows, rows),
                 lambda step, place: (
                     0, 0, 0,
-                    jnp.where(step == 0, 0, jnp.where(step == 1, 2, 3 - 2 * place[0])),
+                    jnp.where(
+                        step < 2, 2 * step, jnp.where(step == 2, 3 - 2 * place[0], 1 + 2 * place[0])
+                    ),
                     0, 0,
                 ),
             ),
             IN_PLACE,
-            IN_VMEM,
         ],
-        {}, 4,
-        [block] * 3
-        + [pltpu.VMEM((2, rows // 2, rows), jnp.float32), pltpu.SemaphoreType.DMA((5,))],
-    )
-    (band,) = call(
-        last_kernel, (2,), place, (band,), (left, late_sib_own, late_sib_beyond, band_sum),
-        [band_out],
-        [
-            pl.BlockSpec(
-                (1, 2, 1, 1, rows // 2, rows),
-                lambda half, place: (0, 0, 0, 1 + 2 * place[0], half, 0),
-            )
-        ],
-        {4: 0}, 1, [],
+        {}, 5,
+        [pltpu.VMEM((2 * rows, late_ahead.shape[1]), late_ahead.dtype)] + [block] * 4
+        + [pltpu.VMEM((2, rows // 2, rows), jnp.float32), pltpu.SemaphoreType.DMA((6,))],
     )
     return band, far
 

time: 126 us -> 124 us (0.984)
  starting transfers between devices: 62.1 us -> 53.3 us
  waiting for transfers between devices: 40.8 us -> 49.5 us
  Pallas kernels: 21.9 us -> 20.1 us
    ppermute x0 -> x2, waiting for transfers between devices: none -> 11.4 us  [from_both_sides(): return lax.ppermute(block, ('arow', 'acol'), route)]
    ppermute x8 -> x7, starting transfers between devices: 30.1 us -> 23.1 us  [from_sibling(): return lax.ppermute(block, 'acol', [(1 - core, core) for core in cores])]
    ppermute x8 -> x6, waiting for transfers between devices: 35.1 us -> 31.4 us  [from_ahead(): lax.ppermute(block, 'arow', [((i + distance) % size, i) for i in range(si...]
    ppermute x8 -> x6, starting transfers between devices: 11.3 us -> 7.86 us  [from_ahead(): lax.ppermute(block, 'arow', [((i + distance) % size, i) for i in range(si...]
    pallas_call x3 -> x2, Pallas kernels: 17.8 us -> 16 us  [call(): pl.pallas_call(kernel, out_shape=outs, grid_spec=pltpu.PrefetchScalarGrid...]
    ppermute x0 -> x2, starting transfers between devices: none -> 1.5 us  [from_both_sides(): return lax.ppermute(block, ('arow', 'acol'), route)]
    ppermute x8 -> x7, waiting for transfers between devices: 4.92 us -> 5.92 us  [from_sibling(): return lax.ppermute(block, 'acol', [(1 - core, core) for core in cores])]
  transfers between devices with their start and end apart: 18 -> 17, of which waited for: 10 -> 10; matrix products, arithmetic and copies ran while one was open for 0% -> 0% of each run, Pallas kernels for 13% -> 7%
where the time goes in v3:
time: 124 us
  starting transfers between devices  53.3 us (43%)
  waiting for transfers between devices  49.5 us (40%)
  Pallas kernels  20.1 us (16%)
    ppermute x6, waiting for transfers between devices, from_ahead(): lax.ppermute(block, 'arow', [((i + distance) % size, i) for i in range(si...  31.4 us
    ppermute x7, starting transfers between devices, from_sibling(): return lax.ppermute(block, 'acol', [(1 - core, core) for core in cores])  23.1 us
    all_to_all x2, starting transfers between devices, turn(): lax.all_to_all(block, 'chan', split_axis=0, concat_axis=0, tiled=True)  20.8 us
    pallas_call x2, Pallas kernels, call(): pl.pallas_call(kernel, out_shape=outs, grid_spec=pltpu.PrefetchScalarGrid...  16 us
    ppermute x2, waiting for transfers between devices, from_both_sides(): return lax.ppermute(block, ('arow', 'acol'), route)  11.4 us
    ppermute x6, starting transfers between devices, from_ahead(): lax.ppermute(block, 'arow', [((i + distance) % size, i) for i in range(si...  7.86 us
    ppermute x7, waiting for transfers between devices, from_sibling(): return lax.ppermute(block, 'acol', [(1 - core, core) for core in cores])  5.92 us
    pallas_call x2, Pallas kernels, half_of(): pl.pallas_call(cut_kernel, out_shape=jax.ShapeDtypeStruct((channels, rows...  4.1 us
  transfers between devices with their start and end apart: 17, of which 10 were waited for; matrix products, arithmetic and copies ran while one was open for 0% of the time, Pallas kernels for 7%

profile of v3, /device:TPU:1, one launch (start us, length us, event | category | flops | bytes accessed | tf_op | source)
XLA Modules:
  0.0 123.9 jit_solution(17381255019191298198)
XLA Ops:
  0.6 2.1 %shard_map.31 = bf16[32,16,1024]{2,1,0:T(8,128)(2,1)} custom-call(bf16[32,1,16,2048]{3,2,1,0:T(8,128)(2,1)} %imaginary.3, bf16[32,1,16,2048]{3,2,1,0:T(8,128)(2,1)} %imaginary.3), custom_call_target="tpu_custom_call" | custom-call | tf_op jit(solution)/shard_map/pallas_call | solution.py:45
  2.7 11.9 %all-to-all-start.1 = ((bf16[32,16,1024]{2,1,0:T(8,128)(2,1)}), bf16[32,16,1024]{2,1,0:T(8,128)(2,1)S(1)}, u32[]{:S(2)}, u32[]{:S(2)}) async-start(bf16[32,16,1024]{2,1,0:T(8,128)(2,1)} %shard_map.31), calls=%async_computation.1 | async-start | bytes 2097152 | tf_op jit(solution)/shard_map/all_to_all | solution.py:32
  14.6 2.1 %shard_map.30 = bf16[32,16,1024]{2,1,0:T(8,128)(2,1)} custom-call(bf16[32,1,16,2048]{3,2,1,0:T(8,128)(2,1)} %imaginary.3, bf16[32,1,16,2048]{3,2,1,0:T(8,128)(2,1)} %imaginary.3), custom_call_target="tpu_custom_call" | custom-call | tf_op jit(solution)/shard_map/pallas_call | solution.py:45
  16.6 2.7 %collective-permute-start = (bf16[32,16,1024]{2,1,0:T(8,128)(2,1)}, bf16[32,16,1024]{2,1,0:T(8,128)(2,1)}, u32[]{:S(2)}, u32[]{:S(2)}) collective-permute-start(bf16[32,16,1024]{2,1,0:T(8,128)(2,1)} %shard_map.30), channel_id=1, source_target_pairs={{2,0},{4,2},{6,4},{0,6},{3,1},{5,3},{7,5},{1,7},{10,8},{12,10},{14... | collective-permute-start | bytes 3145736 | tf_op jit(solution)/shard_map/ppermute | solution.py:14
  19.3 21.8 %collective-permute-done = bf16[32,16,1024]{2,1,0:T(8,128)(2,1)} collective-permute-done((bf16[32,16,1024]{2,1,0:T(8,128)(2,1)}, bf16[32,16,1024]{2,1,0:T(8,128)(2,1)}, u32[]{:S(2)}, u32[]{:S(2)}) %collective-permute-start) | collective-permute-done | bytes 1048608 | tf_op jit(solution)/shard_map/ppermute | solution.py:14
  41.2 8.9 %all-to-all-start = ((bf16[32,16,1024]{2,1,0:T(8,128)(2,1)}), bf16[32,16,1024]{2,1,0:T(8,128)(2,1)S(1)}, u32[]{:S(2)}, u32[]{:S(2)}) async-start(bf16[32,16,1024]{2,1,0:T(8,128)(2,1)} %collective-permute-done), calls=%async_computation | async-start | bytes 2097152 | tf_op jit(solution)/shard_map/all_to_all | solution.py:32
  50.1 0.8 collective-permute-start.2
  51.0 2.7 %collective-permute-start.1 = (bf16[304,1024]{1,0:T(8,128)(2,1)S(1)}, bf16[304,1024]{1,0:T(8,128)(2,1)}, u32[]{:S(2)}, u32[]{:S(2)}) collective-permute-start(bf16[304,1024]{1,0:T(8,128)(2,1)S(1)} %bitcast.12), channel_id=1, source_target_pairs={{2,0},{4,2},{6,4},{0,6},{3,1},{5,3},{7,5},{1,7},{10,8},{12,10},{14... | collective-permute-start | bytes 1867784 | tf_op jit(solution)/shard_map/ppermute | solution.py:14
  53.8 4.7 %collective-permute-start.4 = (bf16[512,1024]{1,0:T(8,128)(2,1)S(1)}, bf16[512,1024]{1,0:T(8,128)(2,1)S(1)}, u32[]{:S(2)}, u32[]{:S(2)}) collective-permute-start(bf16[512,1024]{1,0:T(8,128)(2,1)S(1)} %bitcast.6), channel_id=1, source_target_pairs={{1,0},{3,2},{5,4},{7,6},{9,8},{11,10},{13,12},{15,14},{17,16},{19,... | collective-permute-start | bytes 3145736 | tf_op jit(solution)/shard_map/ppermute | solution.py:28
  58.5 2.9 %collective-permute-done.2 = bf16[208,1024]{1,0:T(8,128)(2,1)S(1)} collective-permute-done((bf16[208,1024]{1,0:T(8,128)(2,1)S(1)}, bf16[208,1024]{1,0:T(8,128)(2,1)S(1)}, u32[]{:S(2)}, u32[]{:S(2)}) %collective-permute-start.2) | collective-permute-done | bytes 426016 | tf_op jit(solution)/shard_map/ppermute | solution.py:14
  61.3 0.0 collective-permute-start.3
  61.3 3.3 %collective-permute-done.1.down_1 = bf16[304,1024]{1,0:T(8,128)(2,1)} collective-permute-done((bf16[304,1024]{1,0:T(8,128)(2,1)S(1)}, bf16[304,1024]{1,0:T(8,128)(2,1)}, u32[]{:S(2)}, u32[]{:S(2)}) %collective-permute-start.1) | collective-permute-done | bytes 622624 | tf_op jit(solution)/shard_map/ppermute | solution.py:14
  64.7 3.4 %collective-permute-start.5 = (bf16[304,1024]{1,0:T(8,128)(2,1)}, bf16[304,1024]{1,0:T(8,128)(2,1)}, u32[]{:S(2)}, u32[]{:S(2)}) collective-permute-start(bf16[304,1024]{1,0:T(8,128)(2,1)} %collective-permute-done.1.down_1), channel_id=1, source_target_pairs={{1,0},{0,1},{3,2},{2,3},{5,4},{4,5},{7,6},{6,7},{9,8},{8,9},{11,10... | collective-permute-start | bytes 1867784 | tf_op jit(solution)/shard_map/ppermute | solution.py:28
  68.0 2.8 %collective-permute-done.3.up_2 = bf16[208,1024]{1,0:T(8,128)(2,1)} collective-permute-done((bf16[208,1024]{1,0:T(8,128)(2,1)S(1)}, bf16[208,1024]{1,0:T(8,128)(2,1)}, u32[]{:S(2)}, u32[]{:S(2)}) %collective-permute-start.3) | collective-permute-done | bytes 426016 | tf_op jit(solution)/shard_map/ppermute | solution.py:14
  70.9 1.3 %collective-permute-start.6 = (bf16[208,1024]{1,0:T(8,128)(2,1)}, bf16[208,1024]{1,0:T(8,128)(2,1)}, u32[]{:S(2)}, u32[]{:S(2)}) collective-permute-start(bf16[208,1024]{1,0:T(8,128)(2,1)} %collective-permute-done.3.up_2), channel_id=1, source_target_pairs={{0,1},{2,3},{4,5},{6,7},{8,9},{10,11},{12,13},{14,15},{16,17},{18,... | collective-permute-start | bytes 1277960 | tf_op jit(solution)/shard_map/ppermute | solution.py:28
  72.1 0.8 collective-permute-start.10
  72.9 0.8 collective-permute-start.9
  73.7 0.8 all-to-all-done
  74.5 3.2 %collective-permute-done.6.sib_up_2 = bf16[208,1024]{1,0:T(8,128)(2,1)} collective-permute-done((bf16[208,1024]{1,0:T(8,128)(2,1)}, bf16[208,1024]{1,0:T(8,128)(2,1)}, u32[]{:S(2)}, u32[]{:S(2)}) %collective-permute-start.6) | collective-permute-done | bytes 426016 | tf_op jit(solution)/shard_map/ppermute | solution.py:28
  77.7 0.0 collective-permute-start.8
  77.7 5.1 %collective-permute-start.7 = (bf16[512,1024]{1,0:T(8,128)(2,1)S(1)}, bf16[512,1024]{1,0:T(8,128)(2,1)}, u32[]{:S(2)}, u32[]{:S(2)}) collective-permute-start(bf16[512,1024]{1,0:T(8,128)(2,1)S(1)} %bitcast.9), channel_id=1, source_target_pairs={{1,0},{0,1},{3,2},{2,3},{5,4},{4,5},{7,6},{6,7},{9,8},{8,9},{11,10... | collective-permute-start | bytes 3145736 | tf_op jit(solution)/shard_map/ppermute | solution.py:28
  82.9 0.5 collective-permute-done.10.down_2
  83.4 1.3 %collective-permute-start.12 = (bf16[304,1024]{1,0:T(8,128)(2,1)}, bf16[304,1024]{1,0:T(8,128)(2,1)}, u32[]{:S(2)}, u32[]{:S(2)}) collective-permute-start(bf16[304,1024]{1,0:T(8,128)(2,1)} %collective-permute-done.10.down_2), channel_id=1, source_target_pairs={{0,1},{2,3},{4,5},{6,7},{8,9},{10,11},{12,13},{14,15},{16,17},{18,... | collective-permute-start | bytes 1867784 | tf_op jit(solution)/shard_map/ppermute | solution.py:28
  84.7 6.9 %collective-permute-start.11 = (bf16[208,1024]{1,0:T(8,128)(2,1)}, bf16[208,1024]{1,0:T(8,128)(2,1)}, u32[]{:S(2)}, u32[]{:S(2)}) collective-permute-start(bf16[208,1024]{1,0:T(8,128)(2,1)} %collective-permute-done.9.up_3), channel_id=1, source_target_pairs={{1,0},{0,1},{3,2},{2,3},{5,4},{4,5},{7,6},{6,7},{9,8},{8,9},{11,10... | collective-permute-start | bytes 1277960 | tf_op jit(solution)/shard_map/ppermute | solution.py:28
  91.5 0.1 pad_add_fusion.place
  91.6 1.7 %collective-permute-done.11.sib_up_3 = bf16[208,1024]{1,0:T(8,128)(2,1)} collective-permute-done((bf16[208,1024]{1,0:T(8,128)(2,1)}, bf16[208,1024]{1,0:T(8,128)(2,1)}, u32[]{:S(2)}, u32[]{:S(2)}) %collective-permute-start.11) | collective-permute-done | bytes 426016 | tf_op jit(solution)/shard_map/ppermute | solution.py:28
  93.3 6.8 %shard_map.32 = (f32[1,2,1,4,512,512]{5,4,3,2,1,0:T(8,128)S(1)}, f32[1,2,1,256,512]{4,3,2,1,0:T(8,128)S(1)}) custom-call(s32[2]{0:T(128)S(1)} %pad_add_fusion.place, bf16[512,1024]{1,0:T(8,128)(2,1)S(1)} %bitcast.7, bf16[304,1024]{1,0:T(8,128)(2,1)} %collective-permute-done.1.down_1, bf16[208,1024]{1,0:T(8,128)(2,1)} %collective-permute-done.9.up_3, ...), custom_call_target="tpu_custom_call" | custom-call | flops 2147483648 | bytes 4194304 | tf_op jit(solution)/shard_map/pallas_call | solution.py:218
  100.1 0.5 collective-permute-start.14
  100.6 1.5 %collective-permute-start.13 = (bf16[512,1024]{1,0:T(8,128)(2,1)S(1)}, bf16[512,1024]{1,0:T(8,128)(2,1)S(1)}, u32[]{:S(2)}, u32[]{:S(2)}) collective-permute-start(bf16[512,1024]{1,0:T(8,128)(2,1)S(1)} %bitcast.10), channel_id=1, source_target_pairs={{6,0},{3,1},{0,2},{5,3},{2,4},{7,5},{4,6},{1,7},{14,8},{11,9},{8,1... | collective-permute-start | bytes 3145736 | tf_op jit(solution)/shard_map/ppermute | solution.py:24
  102.1 1.0 collective-permute-done.14.sib_first
  103.1 11.4 %collective-permute-done.13.second = bf16[512,1024]{1,0:T(8,128)(2,1)S(1)} collective-permute-done((bf16[512,1024]{1,0:T(8,128)(2,1)S(1)}, bf16[512,1024]{1,0:T(8,128)(2,1)S(1)}, u32[]{:S(2)}, u32[]{:S(2)}) %collective-permute-start.13) | collective-permute-done | bytes 1048608 | tf_op jit(solution)/shard_map/ppermute | solution.py:24
  114.6 9.2 %shard_map.33 = (f32[1,2,1,4,512,512]{5,4,3,2,1,0:T(8,128)}, f32[1,2,1,256,512]{4,3,2,1,0:T(8,128)}) custom-call(s32[2]{0:T(128)S(1)} %pad_add_fusion.place, f32[1,2,1,4,512,512]{5,4,3,2,1,0:T(8,128)S(1)} %get-tuple-element.23.band_in, f32[1,2,1,256,512]{4,3,2,1,0:T(8,128)S(1)} %get-tuple-element.24.far_in, bf16[512,1024]{1,0:T(8,128)(2,1)} %collective-permute-done.8.first, ...), custom_call_target="tpu_custom_call" | custom-call | flops 5368709120 | bytes 10485760 | tf_op jit(solution)/shard_map/pallas_call | solution.py:218
  (9 shorter events, 0.1 us)
Async XLA Ops:
  2.7 38.5 %all-to-all-start.1 = ((bf16[32,16,1024]{2,1,0:T(8,128)(2,1)}), bf16[32,16,1024]{2,1,0:T(8,128)(2,1)S(1)}, u32[]{:S(2)}, u32[]{:S(2)}) async-start(bf16[32,16,1024]{2,1,0:T(8,128)(2,1)} %shard_map.31), calls=%async_computation.1 | async-start | bytes 2097152 | tf_op jit(solution)/shard_map/all_to_all | solution.py:32
  16.6 24.6 %collective-permute-start = (bf16[32,16,1024]{2,1,0:T(8,128)(2,1)}, bf16[32,16,1024]{2,1,0:T(8,128)(2,1)}, u32[]{:S(2)}, u32[]{:S(2)}) collective-permute-start(bf16[32,16,1024]{2,1,0:T(8,128)(2,1)} %shard_map.30), channel_id=1, source_target_pairs={{2,0},{4,2},{6,4},{0,6},{3,1},{5,3},{7,5},{1,7},{10,8},{12,10},{14... | collective-permute-start | bytes 3145736 | tf_op jit(solution)/shard_map/ppermute | solution.py:14
  41.2 33.3 %all-to-all-start = ((bf16[32,16,1024]{2,1,0:T(8,128)(2,1)}), bf16[32,16,1024]{2,1,0:T(8,128)(2,1)S(1)}, u32[]{:S(2)}, u32[]{:S(2)}) async-start(bf16[32,16,1024]{2,1,0:T(8,128)(2,1)} %collective-permute-done), calls=%async_computation | async-start | bytes 2097152 | tf_op jit(solution)/shard_map/all_to_all | solution.py:32
  50.1 11.2 %collective-permute-start.2 = (bf16[208,1024]{1,0:T(8,128)(2,1)S(1)}, bf16[208,1024]{1,0:T(8,128)(2,1)S(1)}, u32[]{:S(2)}, u32[]{:S(2)}) collective-permute-start(bf16[208,1024]{1,0:T(8,128)(2,1)S(1)} %bitcast.13), channel_id=1, source_target_pairs={{6,0},{0,2},{2,4},{4,6},{7,1},{1,3},{3,5},{5,7},{14,8},{8,10},{10,... | collective-permute-start | bytes 1277960 | tf_op jit(solution)/shard_map/ppermute | solution.py:14
  51.0 13.6 %collective-permute-start.1 = (bf16[304,1024]{1,0:T(8,128)(2,1)S(1)}, bf16[304,1024]{1,0:T(8,128)(2,1)}, u32[]{:S(2)}, u32[]{:S(2)}) collective-permute-start(bf16[304,1024]{1,0:T(8,128)(2,1)S(1)} %bitcast.12), channel_id=1, source_target_pairs={{2,0},{4,2},{6,4},{0,6},{3,1},{5,3},{7,5},{1,7},{10,8},{12,10},{14... | collective-permute-start | bytes 1867784 | tf_op jit(solution)/shard_map/ppermute | solution.py:14
  53.8 20.7 %collective-permute-start.4 = (bf16[512,1024]{1,0:T(8,128)(2,1)S(1)}, bf16[512,1024]{1,0:T(8,128)(2,1)S(1)}, u32[]{:S(2)}, u32[]{:S(2)}) collective-permute-start(bf16[512,1024]{1,0:T(8,128)(2,1)S(1)} %bitcast.6), channel_id=1, source_target_pairs={{1,0},{3,2},{5,4},{7,6},{9,8},{11,10},{13,12},{15,14},{17,16},{19,... | collective-permute-start | bytes 3145736 | tf_op jit(solution)/shard_map/ppermute | solution.py:28
  61.3 9.5 %collective-permute-start.3 = (bf16[208,1024]{1,0:T(8,128)(2,1)S(1)}, bf16[208,1024]{1,0:T(8,128)(2,1)}, u32[]{:S(2)}, u32[]{:S(2)}) collective-permute-start(bf16[208,1024]{1,0:T(8,128)(2,1)S(1)} %collective-permute-done.2), channel_id=1, source_target_pairs={{6,0},{0,2},{2,4},{4,6},{7,1},{1,3},{3,5},{5,7},{14,8},{8,10},{10,... | collective-permute-start | bytes 1277960 | tf_op jit(solution)/shard_map/ppermute | solution.py:14
  64.7 9.8 %collective-permute-start.5 = (bf16[304,1024]{1,0:T(8,128)(2,1)}, bf16[304,1024]{1,0:T(8,128)(2,1)}, u32[]{:S(2)}, u32[]{:S(2)}) collective-permute-start(bf16[304,1024]{1,0:T(8,128)(2,1)} %collective-permute-done.1.down_1), channel_id=1, source_target_pairs={{1,0},{0,1},{3,2},{2,3},{5,4},{4,5},{7,6},{6,7},{9,8},{8,9},{11,10... | collective-permute-start | bytes 1867784 | tf_op jit(solution)/shard_map/ppermute | solution.py:28
  70.9 6.9 %collective-permute-start.6 = (bf16[208,1024]{1,0:T(8,128)(2,1)}, bf16[208,1024]{1,0:T(8,128)(2,1)}, u32[]{:S(2)}, u32[]{:S(2)}) collective-permute-start(bf16[208,1024]{1,0:T(8,128)(2,1)} %collective-permute-done.3.up_2), channel_id=1, source_target_pairs={{0,1},{2,3},{4,5},{6,7},{8,9},{10,11},{12,13},{14,15},{16,17},{18,... | collective-permute-start | bytes 1277960 | tf_op jit(solution)/shard_map/ppermute | solution.py:28
  72.1 11.2 %collective-permute-start.10 = (bf16[304,1024]{1,0:T(8,128)(2,1)}, bf16[304,1024]{1,0:T(8,128)(2,1)}, u32[]{:S(2)}, u32[]{:S(2)}) collective-permute-start(bf16[304,1024]{1,0:T(8,128)(2,1)} %collective-permute-done.1.down_1), channel_id=1, source_target_pairs={{2,0},{4,2},{6,4},{0,6},{3,1},{5,3},{7,5},{1,7},{10,8},{12,10},{14... | collective-permute-start | bytes 1867784 | tf_op jit(solution)/shard_map/ppermute | solution.py:14
  72.9 11.8 %collective-permute-start.9 = (bf16[208,1024]{1,0:T(8,128)(2,1)}, bf16[208,1024]{1,0:T(8,128)(2,1)}, u32[]{:S(2)}, u32[]{:S(2)}) collective-permute-start(bf16[208,1024]{1,0:T(8,128)(2,1)} %collective-permute-done.3.up_2), channel_id=1, source_target_pairs={{6,0},{0,2},{2,4},{4,6},{7,1},{1,3},{3,5},{5,7},{14,8},{8,10},{10,... | collective-permute-start | bytes 1277960 | tf_op jit(solution)/shard_map/ppermute | solution.py:14
  77.7 22.3 %collective-permute-start.8 = (bf16[512,1024]{1,0:T(8,128)(2,1)S(1)}, bf16[512,1024]{1,0:T(8,128)(2,1)}, u32[]{:S(2)}, u32[]{:S(2)}) collective-permute-start(bf16[512,1024]{1,0:T(8,128)(2,1)S(1)} %bitcast.8), channel_id=1, source_target_pairs={{2,0},{7,1},{4,2},{1,3},{6,4},{3,5},{0,6},{5,7},{10,8},{15,9},{12,... | collective-permute-start | bytes 3145736 | tf_op jit(solution)/shard_map/ppermute | solution.py:24
  77.7 22.3 %collective-permute-start.7 = (bf16[512,1024]{1,0:T(8,128)(2,1)S(1)}, bf16[512,1024]{1,0:T(8,128)(2,1)}, u32[]{:S(2)}, u32[]{:S(2)}) collective-permute-start(bf16[512,1024]{1,0:T(8,128)(2,1)S(1)} %bitcast.9), channel_id=1, source_target_pairs={{1,0},{0,1},{3,2},{2,3},{5,4},{4,5},{7,6},{6,7},{9,8},{8,9},{11,10... | collective-permute-start | bytes 3145736 | tf_op jit(solution)/shard_map/ppermute | solution.py:28
  83.4 9.9 %collective-permute-start.12 = (bf16[304,1024]{1,0:T(8,128)(2,1)}, bf16[304,1024]{1,0:T(8,128)(2,1)}, u32[]{:S(2)}, u32[]{:S(2)}) collective-permute-start(bf16[304,1024]{1,0:T(8,128)(2,1)} %collective-permute-done.10.down_2), channel_id=1, source_target_pairs={{0,1},{2,3},{4,5},{6,7},{8,9},{10,11},{12,13},{14,15},{16,17},{18,... | collective-permute-start | bytes 1867784 | tf_op jit(solution)/shard_map/ppermute | solution.py:28
  84.7 8.6 %collective-permute-start.11 = (bf16[208,1024]{1,0:T(8,128)(2,1)}, bf16[208,1024]{1,0:T(8,128)(2,1)}, u32[]{:S(2)}, u32[]{:S(2)}) collective-permute-start(bf16[208,1024]{1,0:T(8,128)(2,1)} %collective-permute-done.9.up_3), channel_id=1, source_target_pairs={{1,0},{0,1},{3,2},{2,3},{5,4},{4,5},{7,6},{6,7},{9,8},{8,9},{11,10... | collective-permute-start | bytes 1277960 | tf_op jit(solution)/shard_map/ppermute | solution.py:28
  100.1 3.0 %collective-permute-start.14 = (bf16[512,1024]{1,0:T(8,128)(2,1)}, bf16[512,1024]{1,0:T(8,128)(2,1)S(1)}, u32[]{:S(2)}, u32[]{:S(2)}) collective-permute-start(bf16[512,1024]{1,0:T(8,128)(2,1)} %collective-permute-done.8.first), channel_id=1, source_target_pairs={{1,0},{0,1},{3,2},{2,3},{5,4},{4,5},{7,6},{6,7},{9,8},{8,9},{11,10... | collective-permute-start | bytes 3145736 | tf_op jit(solution)/shard_map/ppermute | solution.py:28
  100.6 13.9 %collective-permute-start.13 = (bf16[512,1024]{1,0:T(8,128)(2,1)S(1)}, bf16[512,1024]{1,0:T(8,128)(2,1)S(1)}, u32[]{:S(2)}, u32[]{:S(2)}) collective-permute-start(bf16[512,1024]{1,0:T(8,128)(2,1)S(1)} %bitcast.10), channel_id=1, source_target_pairs={{6,0},{3,1},{0,2},{5,3},{2,4},{7,5},{4,6},{1,7},{14,8},{11,9},{8,1... | collective-permute-start | bytes 3145736 | tf_op jit(solution)/shard_map/ppermute | solution.py:24

commit v4 on v3

--- a/solution.py
+++ b/solution.py
@@ -260,8 +260,13 @@
     late_first = from_both_sides(late_ahead, 0)
     late_sib_ahead = from_sibling(late_ahead)
 
+    late_ahead, late_first, up_3, down_2 = lax.optimization_barrier(
+        (late_ahead, late_first, up_3, down_2)
+    )
     sib_up_3 = from_sibling(up_3)
     sib_down_2 = from_sibling(down_2, (1,))
+    late_second = from_both_sides(late_ahead, 1)
+    late_sib_first = from_sibling(late_first)
 
     rows = own.shape[0]
     block = pltpu.VMEM(own.shape, own.dtype)
@@ -272,11 +277,6 @@
         [pltpu.VMEM(band_shape, jnp.float32), pltpu.VMEM(far_shape, jnp.float32)],
         [IN_VMEM, IN_VMEM], {}, 2, [block] * 6 + [pltpu.SemaphoreType.DMA((9,))],
     )
-    late_ahead, late_sib_ahead, late_first, band_sum, far_sum = lax.optimization_barrier(
-        (late_ahead, late_sib_ahead, late_first, band_sum, far_sum)
-    )
-    late_second = from_both_sides(late_ahead, 1)
-    late_sib_first = from_sibling(late_first)
     band_out = jax.ShapeDtypeStruct(band_shape, jnp.float32)
     far_out = jax.ShapeDtypeStruct(far_shape, jnp.float32)
     band, far = call(

time: 124 us -> 131 us (1.056)
  waiting for transfers between devices: 49.5 us -> 55.1 us
    ppermute x6, waiting for transfers between devices: 31.4 us -> 47.9 us  [from_ahead(): lax.ppermute(block, 'arow', [((i + distance) % size, i) for i in range(si...]
    ppermute x2, waiting for transfers between devices: 11.4 us -> 0.01 us  [from_both_sides(): return lax.ppermute(block, ('arow', 'acol'), route)]
    ppermute x2, starting transfers between devices: 1.5 us -> 3.41 us  [from_both_sides(): return lax.ppermute(block, ('arow', 'acol'), route)]
    ppermute x7, starting transfers between devices: 23.1 us -> 21.4 us  [from_sibling(): return lax.ppermute(block, 'acol', [(1 - core, core) for core in cores])]
    all_to_all x2, waiting for transfers between devices: 0.8 us -> 2.33 us  [turn(): lax.all_to_all(block, 'chan', split_axis=0, concat_axis=0, tiled=True)]
  transfers between devices with their start and end apart: 17 -> 17, of which waited for: 10 -> 9; matrix products, arithmetic and copies ran while one was open for 0% -> 0% of each run, Pallas kernels for 7% -> 7%
where the time goes in v4:
time: 131 us
  waiting for transfers between devices  55.1 us (42%)
  starting transfers between devices  54.6 us (42%)
  Pallas kernels  20.1 us (15%)
    ppermute x6, waiting for transfers between devices, from_ahead(): lax.ppermute(block, 'arow', [((i + distance) % size, i) for i in range(si...  47.9 us
    ppermute x7, starting transfers between devices, from_sibling(): return lax.ppermute(block, 'acol', [(1 - core, core) for core in cores])  21.4 us
    all_to_all x2, starting transfers between devices, turn(): lax.all_to_all(block, 'chan', split_axis=0, concat_axis=0, tiled=True)  20.8 us
    pallas_call x2, Pallas kernels, call(): pl.pallas_call(kernel, out_shape=outs, grid_spec=pltpu.PrefetchScalarGrid...  16 us
    ppermute x6, starting transfers between devices, from_ahead(): lax.ppermute(block, 'arow', [((i + distance) % size, i) for i in range(si...  8.99 us
    ppermute x7, waiting for transfers between devices, from_sibling(): return lax.ppermute(block, 'acol', [(1 - core, core) for core in cores])  4.92 us
    pallas_call x2, Pallas kernels, half_of(): pl.pallas_call(cut_kernel, out_shape=jax.ShapeDtypeStruct((channels, rows...  4.1 us
    ppermute x2, starting transfers between devices, from_both_sides(): return lax.ppermute(block, ('arow', 'acol'), route)  3.41 us
  transfers between devices with their start and end apart: 17, of which 9 were waited for; matrix products, arithmetic and copies ran while one was open for 0% of the time, Pallas kernels for 7%

profile of v4, /device:TPU:1, one launch (start us, length us, event | category | flops | bytes accessed | tf_op | source)
XLA Modules:
  0.0 130.8 jit_solution(10600187654273232927)
XLA Ops:
  0.6 2.1 %shard_map.30 = bf16[32,16,1024]{2,1,0:T(8,128)(2,1)} custom-call(bf16[32,1,16,2048]{3,2,1,0:T(8,128)(2,1)} %imaginary.3, bf16[32,1,16,2048]{3,2,1,0:T(8,128)(2,1)} %imaginary.3), custom_call_target="tpu_custom_call" | custom-call | tf_op jit(solution)/shard_map/pallas_call | solution.py:45
  2.7 11.9 %all-to-all-start = ((bf16[32,16,1024]{2,1,0:T(8,128)(2,1)}), bf16[32,16,1024]{2,1,0:T(8,128)(2,1)S(1)}, u32[]{:S(2)}, u32[]{:S(2)}) async-start(bf16[32,16,1024]{2,1,0:T(8,128)(2,1)} %shard_map.30), calls=%async_computation | async-start | bytes 2097152 | tf_op jit(solution)/shard_map/all_to_all | solution.py:32
  14.6 2.1 %shard_map.31 = bf16[32,16,1024]{2,1,0:T(8,128)(2,1)} custom-call(bf16[32,1,16,2048]{3,2,1,0:T(8,128)(2,1)} %imaginary.3, bf16[32,1,16,2048]{3,2,1,0:T(8,128)(2,1)} %imaginary.3), custom_call_target="tpu_custom_call" | custom-call | tf_op jit(solution)/shard_map/pallas_call | solution.py:45
  16.6 2.7 %collective-permute-start = (bf16[32,16,1024]{2,1,0:T(8,128)(2,1)}, bf16[32,16,1024]{2,1,0:T(8,128)(2,1)}, u32[]{:S(2)}, u32[]{:S(2)}) collective-permute-start(bf16[32,16,1024]{2,1,0:T(8,128)(2,1)} %shard_map.31), channel_id=1, source_target_pairs={{2,0},{4,2},{6,4},{0,6},{3,1},{5,3},{7,5},{1,7},{10,8},{12,10},{14... | collective-permute-start | bytes 3145736 | tf_op jit(solution)/shard_map/ppermute | solution.py:14
  19.3 21.8 %collective-permute-done = bf16[32,16,1024]{2,1,0:T(8,128)(2,1)} collective-permute-done((bf16[32,16,1024]{2,1,0:T(8,128)(2,1)}, bf16[32,16,1024]{2,1,0:T(8,128)(2,1)}, u32[]{:S(2)}, u32[]{:S(2)}) %collective-permute-start) | collective-permute-done | bytes 1048608 | tf_op jit(solution)/shard_map/ppermute | solution.py:14
  41.2 8.9 %all-to-all-start.1 = ((bf16[32,16,1024]{2,1,0:T(8,128)(2,1)}), bf16[32,16,1024]{2,1,0:T(8,128)(2,1)S(1)}, u32[]{:S(2)}, u32[]{:S(2)}) async-start(bf16[32,16,1024]{2,1,0:T(8,128)(2,1)} %collective-permute-done), calls=%async_computation.1 | async-start | bytes 2097152 | tf_op jit(solution)/shard_map/all_to_all | solution.py:32
  50.1 0.8 collective-permute-start.2
  51.0 2.7 %collective-permute-start.1 = (bf16[304,1024]{1,0:T(8,128)(2,1)S(1)}, bf16[304,1024]{1,0:T(8,128)(2,1)}, u32[]{:S(2)}, u32[]{:S(2)}) collective-permute-start(bf16[304,1024]{1,0:T(8,128)(2,1)S(1)} %bitcast.12), channel_id=1, source_target_pairs={{2,0},{4,2},{6,4},{0,6},{3,1},{5,3},{7,5},{1,7},{10,8},{12,10},{14... | collective-permute-start | bytes 1867784 | tf_op jit(solution)/shard_map/ppermute | solution.py:14
  53.8 4.7 %collective-permute-start.4 = (bf16[512,1024]{1,0:T(8,128)(2,1)S(1)}, bf16[512,1024]{1,0:T(8,128)(2,1)S(1)}, u32[]{:S(2)}, u32[]{:S(2)}) collective-permute-start(bf16[512,1024]{1,0:T(8,128)(2,1)S(1)} %bitcast.6), channel_id=1, source_target_pairs={{1,0},{3,2},{5,4},{7,6},{9,8},{11,10},{13,12},{15,14},{17,16},{19,... | collective-permute-start | bytes 3145736 | tf_op jit(solution)/shard_map/ppermute | solution.py:28
  58.5 2.9 %collective-permute-done.2 = bf16[208,1024]{1,0:T(8,128)(2,1)S(1)} collective-permute-done((bf16[208,1024]{1,0:T(8,128)(2,1)S(1)}, bf16[208,1024]{1,0:T(8,128)(2,1)S(1)}, u32[]{:S(2)}, u32[]{:S(2)}) %collective-permute-start.2) | collective-permute-done | bytes 426016 | tf_op jit(solution)/shard_map/ppermute | solution.py:14
  61.3 0.0 collective-permute-start.3
  61.3 3.3 %collective-permute-done.1.down_1 = bf16[304,1024]{1,0:T(8,128)(2,1)} collective-permute-done((bf16[304,1024]{1,0:T(8,128)(2,1)S(1)}, bf16[304,1024]{1,0:T(8,128)(2,1)}, u32[]{:S(2)}, u32[]{:S(2)}) %collective-permute-start.1) | collective-permute-done | bytes 622624 | tf_op jit(solution)/shard_map/ppermute | solution.py:14
  64.7 3.4 %collective-permute-start.5 = (bf16[304,1024]{1,0:T(8,128)(2,1)}, bf16[304,1024]{1,0:T(8,128)(2,1)}, u32[]{:S(2)}, u32[]{:S(2)}) collective-permute-start(bf16[304,1024]{1,0:T(8,128)(2,1)} %collective-permute-done.1.down_1), channel_id=1, source_target_pairs={{1,0},{0,1},{3,2},{2,3},{5,4},{4,5},{7,6},{6,7},{9,8},{8,9},{11,10... | collective-permute-start | bytes 1867784 | tf_op jit(solution)/shard_map/ppermute | solution.py:28
  68.0 2.8 %collective-permute-done.3.up_2 = bf16[208,1024]{1,0:T(8,128)(2,1)} collective-permute-done((bf16[208,1024]{1,0:T(8,128)(2,1)S(1)}, bf16[208,1024]{1,0:T(8,128)(2,1)}, u32[]{:S(2)}, u32[]{:S(2)}) %collective-permute-start.3) | collective-permute-done | bytes 426016 | tf_op jit(solution)/shard_map/ppermute | solution.py:14
  70.9 1.3 collective-permute-start.6
  72.2 2.3 %all-to-all-done.1 = bf16[32,16,1024]{2,1,0:T(8,128)(2,1)S(1)} async-done(((bf16[32,16,1024]{2,1,0:T(8,128)(2,1)}), bf16[32,16,1024]{2,1,0:T(8,128)(2,1)S(1)}, u32[]{:S(2)}, u32[]{:S(2)}) %all-to-all-start.1) | async-done | bytes 1048608 | tf_op jit(solution)/shard_map/all_to_all | solution.py:32
  74.5 0.0 collective-permute-done.5.sib_down_1
  74.5 3.2 %collective-permute-done.6.sib_up_2 = bf16[208,1024]{1,0:T(8,128)(2,1)} collective-permute-done((bf16[208,1024]{1,0:T(8,128)(2,1)}, bf16[208,1024]{1,0:T(8,128)(2,1)}, u32[]{:S(2)}, u32[]{:S(2)}) %collective-permute-start.6) | collective-permute-done | bytes 426016 | tf_op jit(solution)/shard_map/ppermute | solution.py:28
  77.7 0.0 collective-permute-start.7
  77.7 2.7 %collective-permute-start.9 = (bf16[304,1024]{1,0:T(8,128)(2,1)}, bf16[304,1024]{1,0:T(8,128)(2,1)}, u32[]{:S(2)}, u32[]{:S(2)}) collective-permute-start(bf16[304,1024]{1,0:T(8,128)(2,1)} %collective-permute-done.1.down_1), channel_id=1, source_target_pairs={{2,0},{4,2},{6,4},{0,6},{3,1},{5,3},{7,5},{1,7},{10,8},{12,10},{14... | collective-permute-start | bytes 1867784 | tf_op jit(solution)/shard_map/ppermute | solution.py:14
  80.4 4.4 %collective-permute-start.13 = (bf16[512,1024]{1,0:T(8,128)(2,1)S(1)}, bf16[512,1024]{1,0:T(8,128)(2,1)}, u32[]{:S(2)}, u32[]{:S(2)}) collective-permute-start(bf16[512,1024]{1,0:T(8,128)(2,1)S(1)} %bitcast.9), channel_id=1, source_target_pairs={{1,0},{0,1},{3,2},{2,3},{5,4},{4,5},{7,6},{6,7},{9,8},{8,9},{11,10... | collective-permute-start | bytes 3145736 | tf_op jit(solution)/shard_map/ppermute | solution.py:28
  84.8 7.6 %collective-permute-done.9.down_2 = bf16[304,1024]{1,0:T(8,128)(2,1)} collective-permute-done((bf16[304,1024]{1,0:T(8,128)(2,1)}, bf16[304,1024]{1,0:T(8,128)(2,1)}, u32[]{:S(2)}, u32[]{:S(2)}) %collective-permute-start.9) | collective-permute-done | bytes 622624 | tf_op jit(solution)/shard_map/ppermute | solution.py:14
  92.4 9.4 %collective-permute-done.8.up_3 = bf16[208,1024]{1,0:T(8,128)(2,1)} collective-permute-done((bf16[208,1024]{1,0:T(8,128)(2,1)}, bf16[208,1024]{1,0:T(8,128)(2,1)}, u32[]{:S(2)}, u32[]{:S(2)}) %collective-permute-start.8) | collective-permute-done | bytes 426016 | tf_op jit(solution)/shard_map/ppermute | solution.py:14
  101.8 4.4 %collective-permute-start.14 = (bf16[512,1024]{1,0:T(8,128)(2,1)}, bf16[512,1024]{1,0:T(8,128)(2,1)}, u32[]{:S(2)}, u32[]{:S(2)}) collective-permute-start(bf16[512,1024]{1,0:T(8,128)(2,1)} %collective-permute-done.7.first), channel_id=1, source_target_pairs={{1,0},{0,1},{3,2},{2,3},{5,4},{4,5},{7,6},{6,7},{9,8},{8,9},{11,10... | collective-permute-start | bytes 3145736 | tf_op jit(solution)/shard_map/ppermute | solution.py:28
  106.2 3.4 %collective-permute-start.12 = (bf16[512,1024]{1,0:T(8,128)(2,1)S(1)}, bf16[512,1024]{1,0:T(8,128)(2,1)}, u32[]{:S(2)}, u32[]{:S(2)}) collective-permute-start(bf16[512,1024]{1,0:T(8,128)(2,1)S(1)} %bitcast.10), channel_id=1, source_target_pairs={{6,0},{3,1},{0,2},{5,3},{2,4},{7,5},{4,6},{1,7},{14,8},{11,9},{8,1... | collective-permute-start | bytes 3145736 | tf_op jit(solution)/shard_map/ppermute | solution.py:24
  109.6 1.3 collective-permute-start.11
  110.9 2.0 %collective-permute-start.10 = (bf16[208,1024]{1,0:T(8,128)(2,1)}, bf16[208,1024]{1,0:T(8,128)(2,1)}, u32[]{:S(2)}, u32[]{:S(2)}) collective-permute-start(bf16[208,1024]{1,0:T(8,128)(2,1)} %collective-permute-done.8.up_3), channel_id=1, source_target_pairs={{1,0},{0,1},{3,2},{2,3},{5,4},{4,5},{7,6},{6,7},{9,8},{8,9},{11,10... | collective-permute-start | bytes 1277960 | tf_op jit(solution)/shard_map/ppermute | solution.py:28
  112.9 0.1 pad_add_fusion.place
  113.0 1.7 %collective-permute-done.10.sib_up_3 = bf16[208,1024]{1,0:T(8,128)(2,1)} collective-permute-done((bf16[208,1024]{1,0:T(8,128)(2,1)}, bf16[208,1024]{1,0:T(8,128)(2,1)}, u32[]{:S(2)}, u32[]{:S(2)}) %collective-permute-start.10) | collective-permute-done | bytes 426016 | tf_op jit(solution)/shard_map/ppermute | solution.py:28
  114.6 0.0 collective-permute-done.11.sib_down_2
  114.6 6.8 %shard_map.32 = (f32[1,2,1,4,512,512]{5,4,3,2,1,0:T(8,128)S(1)}, f32[1,2,1,256,512]{4,3,2,1,0:T(8,128)S(1)}) custom-call(s32[2]{0:T(128)S(1)} %pad_add_fusion.place, bf16[512,1024]{1,0:T(8,128)(2,1)S(1)} %bitcast.7, bf16[304,1024]{1,0:T(8,128)(2,1)} %collective-permute-done.1.down_1, bf16[208,1024]{1,0:T(8,128)(2,1)} %collective-permute-done.8.up_3, ...), custom_call_target="tpu_custom_call" | custom-call | flops 2147483648 | bytes 4194304 | tf_op jit(solution)/shard_map/pallas_call | solution.py:218
  121.4 9.2 %shard_map.33 = (f32[1,2,1,4,512,512]{5,4,3,2,1,0:T(8,128)}, f32[1,2,1,256,512]{4,3,2,1,0:T(8,128)}) custom-call(s32[2]{0:T(128)S(1)} %pad_add_fusion.place, f32[1,2,1,4,512,512]{5,4,3,2,1,0:T(8,128)S(1)} %get-tuple-element.22.band_in, f32[1,2,1,256,512]{4,3,2,1,0:T(8,128)S(1)} %get-tuple-element.23.far_in, bf16[512,1024]{1,0:T(8,128)(2,1)} %collective-permute-done.7.first, ...), custom_call_target="tpu_custom_call" | custom-call | flops 5368709120 | bytes 10485760 | tf_op jit(solution)/shard_map/pallas_call | solution.py:218
  (9 shorter events, 0.1 us)
Async XLA Ops:
  2.7 38.5 %all-to-all-start = ((bf16[32,16,1024]{2,1,0:T(8,128)(2,1)}), bf16[32,16,1024]{2,1,0:T(8,128)(2,1)S(1)}, u32[]{:S(2)}, u32[]{:S(2)}) async-start(bf16[32,16,1024]{2,1,0:T(8,128)(2,1)} %shard_map.30), calls=%async_computation | async-start | bytes 2097152 | tf_op jit(solution)/shard_map/all_to_all | solution.py:32
  16.6 24.6 %collective-permute-start = (bf16[32,16,1024]{2,1,0:T(8,128)(2,1)}, bf16[32,16,1024]{2,1,0:T(8,128)(2,1)}, u32[]{:S(2)}, u32[]{:S(2)}) collective-permute-start(bf16[32,16,1024]{2,1,0:T(8,128)(2,1)} %shard_map.31), channel_id=1, source_target_pairs={{2,0},{4,2},{6,4},{0,6},{3,1},{5,3},{7,5},{1,7},{10,8},{12,10},{14... | collective-permute-start | bytes 3145736 | tf_op jit(solution)/shard_map/ppermute | solution.py:14
  41.2 33.3 %all-to-all-start.1 = ((bf16[32,16,1024]{2,1,0:T(8,128)(2,1)}), bf16[32,16,1024]{2,1,0:T(8,128)(2,1)S(1)}, u32[]{:S(2)}, u32[]{:S(2)}) async-start(bf16[32,16,1024]{2,1,0:T(8,128)(2,1)} %collective-permute-done), calls=%async_computation.1 | async-start | bytes 2097152 | tf_op jit(solution)/shard_map/all_to_all | solution.py:32
  50.1 11.2 %collective-permute-start.2 = (bf16[208,1024]{1,0:T(8,128)(2,1)S(1)}, bf16[208,1024]{1,0:T(8,128)(2,1)S(1)}, u32[]{:S(2)}, u32[]{:S(2)}) collective-permute-start(bf16[208,1024]{1,0:T(8,128)(2,1)S(1)} %bitcast.13), channel_id=1, source_target_pairs={{6,0},{0,2},{2,4},{4,6},{7,1},{1,3},{3,5},{5,7},{14,8},{8,10},{10,... | collective-permute-start | bytes 1277960 | tf_op jit(solution)/shard_map/ppermute | solution.py:14
  51.0 13.6 %collective-permute-start.1 = (bf16[304,1024]{1,0:T(8,128)(2,1)S(1)}, bf16[304,1024]{1,0:T(8,128)(2,1)}, u32[]{:S(2)}, u32[]{:S(2)}) collective-permute-start(bf16[304,1024]{1,0:T(8,128)(2,1)S(1)} %bitcast.12), channel_id=1, source_target_pairs={{2,0},{4,2},{6,4},{0,6},{3,1},{5,3},{7,5},{1,7},{10,8},{12,10},{14... | collective-permute-start | bytes 1867784 | tf_op jit(solution)/shard_map/ppermute | solution.py:14
  53.8 18.4 %collective-permute-start.4 = (bf16[512,1024]{1,0:T(8,128)(2,1)S(1)}, bf16[512,1024]{1,0:T(8,128)(2,1)S(1)}, u32[]{:S(2)}, u32[]{:S(2)}) collective-permute-start(bf16[512,1024]{1,0:T(8,128)(2,1)S(1)} %bitcast.6), channel_id=1, source_target_pairs={{1,0},{3,2},{5,4},{7,6},{9,8},{11,10},{13,12},{15,14},{17,16},{19,... | collective-permute-start | bytes 3145736 | tf_op jit(solution)/shard_map/ppermute | solution.py:28
  61.3 9.5 %collective-permute-start.3 = (bf16[208,1024]{1,0:T(8,128)(2,1)S(1)}, bf16[208,1024]{1,0:T(8,128)(2,1)}, u32[]{:S(2)}, u32[]{:S(2)}) collective-permute-start(bf16[208,1024]{1,0:T(8,128)(2,1)S(1)} %collective-permute-done.2), channel_id=1, source_target_pairs={{6,0},{0,2},{2,4},{4,6},{7,1},{1,3},{3,5},{5,7},{14,8},{8,10},{10,... | collective-permute-start | bytes 1277960 | tf_op jit(solution)/shard_map/ppermute | solution.py:14
  64.7 9.8 %collective-permute-start.5 = (bf16[304,1024]{1,0:T(8,128)(2,1)}, bf16[304,1024]{1,0:T(8,128)(2,1)}, u32[]{:S(2)}, u32[]{:S(2)}) collective-permute-start(bf16[304,1024]{1,0:T(8,128)(2,1)} %collective-permute-done.1.down_1), channel_id=1, source_target_pairs={{1,0},{0,1},{3,2},{2,3},{5,4},{4,5},{7,6},{6,7},{9,8},{8,9},{11,10... | collective-permute-start | bytes 1867784 | tf_op jit(solution)/shard_map/ppermute | solution.py:28
  70.9 6.9 %collective-permute-start.6 = (bf16[208,1024]{1,0:T(8,128)(2,1)}, bf16[208,1024]{1,0:T(8,128)(2,1)}, u32[]{:S(2)}, u32[]{:S(2)}) collective-permute-start(bf16[208,1024]{1,0:T(8,128)(2,1)} %collective-permute-done.3.up_2), channel_id=1, source_target_pairs={{0,1},{2,3},{4,5},{6,7},{8,9},{10,11},{12,13},{14,15},{16,17},{18,... | collective-permute-start | bytes 1277960 | tf_op jit(solution)/shard_map/ppermute | solution.py:28
  77.7 24.1 %collective-permute-start.7 = (bf16[512,1024]{1,0:T(8,128)(2,1)S(1)}, bf16[512,1024]{1,0:T(8,128)(2,1)}, u32[]{:S(2)}, u32[]{:S(2)}) collective-permute-start(bf16[512,1024]{1,0:T(8,128)(2,1)S(1)} %bitcast.8), channel_id=1, source_target_pairs={{2,0},{7,1},{4,2},{1,3},{6,4},{3,5},{0,6},{5,7},{10,8},{15,9},{12,... | collective-permute-start | bytes 3145736 | tf_op jit(solution)/shard_map/ppermute | solution.py:24
  77.7 14.7 %collective-permute-start.9 = (bf16[304,1024]{1,0:T(8,128)(2,1)}, bf16[304,1024]{1,0:T(8,128)(2,1)}, u32[]{:S(2)}, u32[]{:S(2)}) collective-permute-start(bf16[304,1024]{1,0:T(8,128)(2,1)} %collective-permute-done.1.down_1), channel_id=1, source_target_pairs={{2,0},{4,2},{6,4},{0,6},{3,1},{5,3},{7,5},{1,7},{10,8},{12,10},{14... | collective-permute-start | bytes 1867784 | tf_op jit(solution)/shard_map/ppermute | solution.py:14
  80.4 21.4 %collective-permute-start.8 = (bf16[208,1024]{1,0:T(8,128)(2,1)}, bf16[208,1024]{1,0:T(8,128)(2,1)}, u32[]{:S(2)}, u32[]{:S(2)}) collective-permute-start(bf16[208,1024]{1,0:T(8,128)(2,1)} %collective-permute-done.3.up_2), channel_id=1, source_target_pairs={{6,0},{0,2},{2,4},{4,6},{7,1},{1,3},{3,5},{5,7},{14,8},{8,10},{10,... | collective-permute-start | bytes 1277960 | tf_op jit(solution)/shard_map/ppermute | solution.py:14
  80.4 41.0 %collective-permute-start.13 = (bf16[512,1024]{1,0:T(8,128)(2,1)S(1)}, bf16[512,1024]{1,0:T(8,128)(2,1)}, u32[]{:S(2)}, u32[]{:S(2)}) collective-permute-start(bf16[512,1024]{1,0:T(8,128)(2,1)S(1)} %bitcast.9), channel_id=1, source_target_pairs={{1,0},{0,1},{3,2},{2,3},{5,4},{4,5},{7,6},{6,7},{9,8},{8,9},{11,10... | collective-permute-start | bytes 3145736 | tf_op jit(solution)/shard_map/ppermute | solution.py:28
  101.8 19.6 %collective-permute-start.14 = (bf16[512,1024]{1,0:T(8,128)(2,1)}, bf16[512,1024]{1,0:T(8,128)(2,1)}, u32[]{:S(2)}, u32[]{:S(2)}) collective-permute-start(bf16[512,1024]{1,0:T(8,128)(2,1)} %collective-permute-done.7.first), channel_id=1, source_target_pairs={{1,0},{0,1},{3,2},{2,3},{5,4},{4,5},{7,6},{6,7},{9,8},{8,9},{11,10... | collective-permute-start | bytes 3145736 | tf_op jit(solution)/shard_map/ppermute | solution.py:28
  106.2 15.2 %collective-permute-start.12 = (bf16[512,1024]{1,0:T(8,128)(2,1)S(1)}, bf16[512,1024]{1,0:T(8,128)(2,1)}, u32[]{:S(2)}, u32[]{:S(2)}) collective-permute-start(bf16[512,1024]{1,0:T(8,128)(2,1)S(1)} %bitcast.10), channel_id=1, source_target_pairs={{6,0},{3,1},{0,2},{5,3},{2,4},{7,5},{4,6},{1,7},{14,8},{11,9},{8,1... | collective-permute-start | bytes 3145736 | tf_op jit(solution)/shard_map/ppermute | solution.py:24
  109.6 5.0 %collective-permute-start.11 = (bf16[304,1024]{1,0:T(8,128)(2,1)}, bf16[304,1024]{1,0:T(8,128)(2,1)}, u32[]{:S(2)}, u32[]{:S(2)}) collective-permute-start(bf16[304,1024]{1,0:T(8,128)(2,1)} %collective-permute-done.9.down_2), channel_id=1, source_target_pairs={{0,1},{2,3},{4,5},{6,7},{8,9},{10,11},{12,13},{14,15},{16,17},{18,... | collective-permute-start | bytes 1867784 | tf_op jit(solution)/shard_map/ppermute | solution.py:28
  110.9 3.7 %collective-permute-start.10 = (bf16[208,1024]{1,0:T(8,128)(2,1)}, bf16[208,1024]{1,0:T(8,128)(2,1)}, u32[]{:S(2)}, u32[]{:S(2)}) collective-permute-start(bf16[208,1024]{1,0:T(8,128)(2,1)} %collective-permute-done.8.up_3), channel_id=1, source_target_pairs={{1,0},{0,1},{3,2},{2,3},{5,4},{4,5},{7,6},{6,7},{9,8},{8,9},{11,10... | collective-permute-start | bytes 1277960 | tf_op jit(solution)/shard_map/ppermute | solution.py:28

commit v5 on v3

--- a/solution.py
+++ b/solution.py
@@ -80,24 +80,52 @@
         put(1, times(quadrature(lower), own[...]))
 
 
+def ahead_kernel(
+    place, own_at, down_1, up_3, down_2, up_2, tile, far, swapped, own, ahead, beyond, sems
+):
+    upper = place[1]
+    first, second = pl.ds(0, down_1.shape[0]), pl.ds(down_1.shape[0], up_3.shape[0])
+    loads = [
+        pltpu.make_async_copy(own_at, own, sems.at[0]),
+        pltpu.make_async_copy(down_1, ahead.at[first], sems.at[1]),
+        pltpu.make_async_copy(up_3, ahead.at[second], sems.at[2]),
+        pltpu.make_async_copy(down_2, beyond.at[first], sems.at[3]),
+        pltpu.make_async_copy(up_2, beyond.at[second], sems.at[4]),
+    ]
+    for copy in loads:
+        copy.start()
+    loads[0].wait()
+    swapped[...] = quadrature(own[...])
+    for copy in loads[1:3]:
+        copy.wait()
+    for part, left in enumerate((own, swapped)):
+        tile[part] = times(left[...], ahead[...])
+    for copy in loads[3:]:
+        copy.wait()
+
+    def put(part, product):
+        far[0, part, 0] = product
+
+    far_tile(upper, own, swapped, beyond, put)
+
+
 def early_kernel(
-    place, own_at, down_1, up_3, down_2, up_2, sib_own, sib_down_1, sib_up_3, sib_down_2, sib_up_2,
-    band, far, swapped, own, ahead, beyond, sib_ahead, other, sems,
+    place, own_at, sib_own, sib_down_1, sib_up_3, sib_down_2, sib_up_2, band,
+    swapped, own, sib_ahead, other, sems,
 ):
-    core, upper = place[0], place[1]
-    first, second = pl.ds(0, down_1.shape[0]), pl.ds(down_1.shape[0], up_3.shape[0])
+    core = place[0]
+    first = pl.ds(0, sib_down_1.shape[0])
+    second = pl.ds(sib_down_1.shape[0], sib_up_3.shape[0])
 
     def load(number, source, target):
         return pltpu.make_async_copy(source, target, sems.at[number])
 
     own_load = load(0, own_at, own)
-    ahead_loads = [load(1, down_1, ahead.at[first]), load(2, up_3, ahead.at[second])]
-    beyond_loads = [load(3, down_2, beyond.at[first]), load(4, up_2, beyond.at[second])]
-    sib_loads = [load(5, sib_down_1, sib_ahead.at[first]), load(6, sib_up_3, sib_ahead.at[second])]
-    near_load = load(7, sib_own, other)
-    far_loads = [load(7, sib_down_2, other.at[first]), load(8, sib_up_2, other.at[second])]
-
-    for copy in (own_load, *ahead_loads, *beyond_loads, *sib_loads):
+    sib_loads = [load(1, sib_down_1, sib_ahead.at[first]), load(2, sib_up_3, sib_ahead.at[second])]
+    near_load = load(3, sib_own, other)
+    far_loads = [load(3, sib_down_2, other.at[first]), load(4, sib_up_2, other.at[second])]
+
+    for copy in (own_load, *sib_loads):
         copy.start()
 
     @pl.when(core == 0)
@@ -113,18 +141,9 @@
         for part, left in enumerate((own, swapped)):
             band[0, part, 0, slot] = times(left[...], columns[...])
 
-    def put(part, product):
-        far[0, part, 0] = product
-
     own_load.wait()
     swapped[...] = quadrature(own[...])
     tile(0, own)
-    for copy in ahead_loads:
-        copy.wait()
-    tile(2, ahead)
-    for copy in beyond_loads:
-        copy.wait()
-    far_tile(upper, own, swapped, beyond, put)
     for copy in sib_loads:
         copy.wait()
     tile(3 - 2 * core, sib_ahead)
@@ -142,7 +161,7 @@
 
 
 def late_kernel(
-    place, band_in, far_in, first, second, ahead_at, sib_ahead_at, sib_first, band, far_at, left,
+    place, band_in, far_in, ahead_in, first, second, ahead_at, sib_ahead_at, sib_first, band, far_at, left,
     ahead, beyond, sib_ahead, other, far, sems,
 ):
     core, upper = place[0], place[1]
@@ -160,8 +179,9 @@
 
     def tile(slot, columns):
         product = times(left[...], columns[...])
-        band[0, 0, 0, 0] = product[:rows] + band_in[0, 0, 0, slot]
-        band[0, 1, 0, 0] = product[rows:] + band_in[0, 1, 0, slot]
+        for part in range(2):
+            earlier = ahead_in[part] if slot is None else band_in[0, part, 0, slot]
+            band[0, part, 0, 0] = product[part * rows : (part + 1) * rows] + earlier
 
     @pl.when(step == 0)
     def _():
@@ -191,7 +211,7 @@
         far_tile(upper, own, swapped, beyond, put)
         store.start()
         loads[0].wait()
-        tile(2, ahead)
+        tile(None, ahead)
 
     @pl.when(step == 2)
     def _():
@@ -266,23 +286,28 @@
     rows = own.shape[0]
     block = pltpu.VMEM(own.shape, own.dtype)
     band_shape, far_shape = (1, 2, 1, 4, rows, rows), (1, 2, 1, rows // 2, rows)
-    band_sum, far_sum = call(
-        early_kernel, (1,), place,
-        (own, down_1, up_3, down_2, up_2, sib_own, sib_down_1, sib_up_3, sib_down_2, sib_up_2), (),
-        [pltpu.VMEM(band_shape, jnp.float32), pltpu.VMEM(far_shape, jnp.float32)],
-        [IN_VMEM, IN_VMEM], {}, 2, [block] * 6 + [pltpu.SemaphoreType.DMA((9,))],
-    )
-    late_ahead, late_sib_ahead, late_first, band_sum, far_sum = lax.optimization_barrier(
-        (late_ahead, late_sib_ahead, late_first, band_sum, far_sum)
+    ahead_sum, far_sum = call(
+        ahead_kernel, (1,), place, (own, down_1, up_3, down_2, up_2), (),
+        [pltpu.VMEM((2, rows, rows), jnp.float32), pltpu.VMEM(far_shape, jnp.float32)],
+        [IN_VMEM, IN_VMEM], {}, 14, [block] * 4 + [pltpu.SemaphoreType.DMA((5,))],
+    )
+    late_ahead, late_first, ahead_sum, far_sum = lax.optimization_barrier(
+        (late_ahead, late_first, ahead_sum, far_sum)
     )
     late_second = from_both_sides(late_ahead, 1)
     late_sib_first = from_sibling(late_first)
+    (band_sum,) = call(
+        early_kernel, (1,), place,
+        (own, sib_own, sib_down_1, sib_up_3, sib_down_2, sib_up_2), (),
+        [pltpu.VMEM(band_shape, jnp.float32)], [IN_VMEM], {}, 2,
+        [block] * 4 + [pltpu.SemaphoreType.DMA((5,))],
+    )
     band_out = jax.ShapeDtypeStruct(band_shape, jnp.float32)
     far_out = jax.ShapeDtypeStruct(far_shape, jnp.float32)
     band, far = call(
         late_kernel, (4,), place,
         (late_first, late_second, late_ahead, late_sib_ahead, late_sib_first),
-        (band_sum, far_sum), [band_out, far_out],
+        (band_sum, far_sum, ahead_sum), [band_out, far_out],
         [
             pl.BlockSpec(
                 (1, 2, 1, 1, rows, rows),

time: 124 us -> 121 us (0.976)
  starting transfers between devices: 53.3 us -> 48.4 us
    ppermute x7, starting transfers between devices: 23.1 us -> 13.5 us  [from_sibling(): return lax.ppermute(block, 'acol', [(1 - core, core) for core in cores])]
    ppermute x2, starting transfers between devices: 1.5 us -> 4.17 us  [from_both_sides(): return lax.ppermute(block, ('arow', 'acol'), route)]
    ppermute x6, waiting for transfers between devices: 31.4 us -> 33.5 us  [from_ahead(): lax.ppermute(block, 'arow', [((i + distance) % size, i) for i in range(si...]
    ppermute x6, starting transfers between devices: 7.86 us -> 9.92 us  [from_ahead(): lax.ppermute(block, 'arow', [((i + distance) % size, i) for i in range(si...]
    ppermute x2, waiting for transfers between devices: 11.4 us -> 9.94 us  [from_both_sides(): return lax.ppermute(block, ('arow', 'acol'), route)]
    pallas_call x2 -> x3, Pallas kernels: 16 us -> 17.1 us  [call(): pl.pallas_call(kernel, out_shape=outs, grid_spec=pltpu.PrefetchScalarGrid...]
  transfers between devices with their start and end apart: 17 -> 17, of which waited for: 10 -> 9; matrix products, arithmetic and copies ran while one was open for 0% -> 0% of each run, Pallas kernels for 7% -> 9%
where the time goes in v5:
time: 121 us
  waiting for transfers between devices  50.2 us (41%)
  starting transfers between devices  48.4 us (40%)
  Pallas kernels  21.2 us (18%)
    ppermute x6, waiting for transfers between devices, from_ahead(): lax.ppermute(block, 'arow', [((i + distance) % size, i) for i in range(si...  33.5 us
    all_to_all x2, starting transfers between devices, turn(): lax.all_to_all(block, 'chan', split_axis=0, concat_axis=0, tiled=True)  20.8 us
    pallas_call x3, Pallas kernels, call(): pl.pallas_call(kernel, out_shape=outs, grid_spec=pltpu.PrefetchScalarGrid...  17.1 us
    ppermute x7, starting transfers between devices, from_sibling(): return lax.ppermute(block, 'acol', [(1 - core, core) for core in cores])  13.5 us
    ppermute x2, waiting for transfers between devices, from_both_sides(): return lax.ppermute(block, ('arow', 'acol'), route)  9.94 us
    ppermute x6, starting transfers between devices, from_ahead(): lax.ppermute(block, 'arow', [((i + distance) % size, i) for i in range(si...  9.92 us
    ppermute x7, waiting for transfers between devices, from_sibling(): return lax.ppermute(block, 'acol', [(1 - core, core) for core in cores])  5.3 us
    ppermute x2, starting transfers between devices, from_both_sides(): return lax.ppermute(block, ('arow', 'acol'), route)  4.17 us
  transfers between devices with their start and end apart: 17, of which 9 were waited for; matrix products, arithmetic and copies ran while one was open for 0% of the time, Pallas kernels for 9%

profile of v5, /device:TPU:1, one launch (start us, length us, event | category | flops | bytes accessed | tf_op | source)
XLA Modules:
  0.0 120.9 jit_solution(5569626826903086743)
XLA Ops:
  0.6 2.1 %shard_map.30 = bf16[32,16,1024]{2,1,0:T(8,128)(2,1)} custom-call(bf16[32,1,16,2048]{3,2,1,0:T(8,128)(2,1)} %imaginary.3, bf16[32,1,16,2048]{3,2,1,0:T(8,128)(2,1)} %imaginary.3), custom_call_target="tpu_custom_call" | custom-call | tf_op jit(solution)/shard_map/pallas_call | solution.py:45
  2.7 11.9 %all-to-all-start = ((bf16[32,16,1024]{2,1,0:T(8,128)(2,1)}), bf16[32,16,1024]{2,1,0:T(8,128)(2,1)S(1)}, u32[]{:S(2)}, u32[]{:S(2)}) async-start(bf16[32,16,1024]{2,1,0:T(8,128)(2,1)} %shard_map.30), calls=%async_computation | async-start | bytes 2097152 | tf_op jit(solution)/shard_map/all_to_all | solution.py:32
  14.6 2.1 %shard_map.31 = bf16[32,16,1024]{2,1,0:T(8,128)(2,1)} custom-call(bf16[32,1,16,2048]{3,2,1,0:T(8,128)(2,1)} %imaginary.3, bf16[32,1,16,2048]{3,2,1,0:T(8,128)(2,1)} %imaginary.3), custom_call_target="tpu_custom_call" | custom-call | tf_op jit(solution)/shard_map/pallas_call | solution.py:45
  16.6 2.7 %collective-permute-start = (bf16[32,16,1024]{2,1,0:T(8,128)(2,1)}, bf16[32,16,1024]{2,1,0:T(8,128)(2,1)}, u32[]{:S(2)}, u32[]{:S(2)}) collective-permute-start(bf16[32,16,1024]{2,1,0:T(8,128)(2,1)} %shard_map.31), channel_id=1, source_target_pairs={{2,0},{4,2},{6,4},{0,6},{3,1},{5,3},{7,5},{1,7},{10,8},{12,10},{14... | collective-permute-start | bytes 3145736 | tf_op jit(solution)/shard_map/ppermute | solution.py:14
  19.3 21.8 %collective-permute-done = bf16[32,16,1024]{2,1,0:T(8,128)(2,1)} collective-permute-done((bf16[32,16,1024]{2,1,0:T(8,128)(2,1)}, bf16[32,16,1024]{2,1,0:T(8,128)(2,1)}, u32[]{:S(2)}, u32[]{:S(2)}) %collective-permute-start) | collective-permute-done | bytes 1048608 | tf_op jit(solution)/shard_map/ppermute | solution.py:14
  41.2 8.9 %all-to-all-start.1 = ((bf16[32,16,1024]{2,1,0:T(8,128)(2,1)}), bf16[32,16,1024]{2,1,0:T(8,128)(2,1)S(1)}, u32[]{:S(2)}, u32[]{:S(2)}) async-start(bf16[32,16,1024]{2,1,0:T(8,128)(2,1)} %collective-permute-done), calls=%async_computation.1 | async-start | bytes 2097152 | tf_op jit(solution)/shard_map/all_to_all | solution.py:32
  50.1 0.8 collective-permute-start.2
  51.0 2.7 %collective-permute-start.1 = (bf16[304,1024]{1,0:T(8,128)(2,1)S(1)}, bf16[304,1024]{1,0:T(8,128)(2,1)}, u32[]{:S(2)}, u32[]{:S(2)}) collective-permute-start(bf16[304,1024]{1,0:T(8,128)(2,1)S(1)} %bitcast.13), channel_id=1, source_target_pairs={{2,0},{4,2},{6,4},{0,6},{3,1},{5,3},{7,5},{1,7},{10,8},{12,10},{14... | collective-permute-start | bytes 1867784 | tf_op jit(solution)/shard_map/ppermute | solution.py:14
  53.8 4.7 %collective-permute-start.4 = (bf16[512,1024]{1,0:T(8,128)(2,1)S(1)}, bf16[512,1024]{1,0:T(8,128)(2,1)S(1)}, u32[]{:S(2)}, u32[]{:S(2)}) collective-permute-start(bf16[512,1024]{1,0:T(8,128)(2,1)S(1)} %bitcast.6), channel_id=1, source_target_pairs={{1,0},{3,2},{5,4},{7,6},{9,8},{11,10},{13,12},{15,14},{17,16},{19,... | collective-permute-start | bytes 3145736 | tf_op jit(solution)/shard_map/ppermute | solution.py:28
  58.5 2.9 %collective-permute-done.2 = bf16[208,1024]{1,0:T(8,128)(2,1)S(1)} collective-permute-done((bf16[208,1024]{1,0:T(8,128)(2,1)S(1)}, bf16[208,1024]{1,0:T(8,128)(2,1)S(1)}, u32[]{:S(2)}, u32[]{:S(2)}) %collective-permute-start.2) | collective-permute-done | bytes 426016 | tf_op jit(solution)/shard_map/ppermute | solution.py:14
  61.3 0.0 collective-permute-start.3
  61.3 3.3 %collective-permute-done.1.down_1 = bf16[304,1024]{1,0:T(8,128)(2,1)} collective-permute-done((bf16[304,1024]{1,0:T(8,128)(2,1)S(1)}, bf16[304,1024]{1,0:T(8,128)(2,1)}, u32[]{:S(2)}, u32[]{:S(2)}) %collective-permute-start.1) | collective-permute-done | bytes 622624 | tf_op jit(solution)/shard_map/ppermute | solution.py:14
  64.7 3.4 %collective-permute-start.5 = (bf16[304,1024]{1,0:T(8,128)(2,1)}, bf16[304,1024]{1,0:T(8,128)(2,1)}, u32[]{:S(2)}, u32[]{:S(2)}) collective-permute-start(bf16[304,1024]{1,0:T(8,128)(2,1)} %collective-permute-done.1.down_1), channel_id=1, source_target_pairs={{1,0},{0,1},{3,2},{2,3},{5,4},{4,5},{7,6},{6,7},{9,8},{8,9},{11,10... | collective-permute-start | bytes 1867784 | tf_op jit(solution)/shard_map/ppermute | solution.py:28
  68.0 3.5 %collective-permute-start.9 = (bf16[304,1024]{1,0:T(8,128)(2,1)}, bf16[304,1024]{1,0:T(8,128)(2,1)}, u32[]{:S(2)}, u32[]{:S(2)}) collective-permute-start(bf16[304,1024]{1,0:T(8,128)(2,1)} %collective-permute-done.1.down_1), channel_id=1, source_target_pairs={{2,0},{4,2},{6,4},{0,6},{3,1},{5,3},{7,5},{1,7},{10,8},{12,10},{14... | collective-permute-start | bytes 1867784 | tf_op jit(solution)/shard_map/ppermute | solution.py:14
  71.5 1.3 %collective-permute-start.6 = (bf16[208,1024]{1,0:T(8,128)(2,1)}, bf16[208,1024]{1,0:T(8,128)(2,1)}, u32[]{:S(2)}, u32[]{:S(2)}) collective-permute-start(bf16[208,1024]{1,0:T(8,128)(2,1)} %collective-permute-done.3.up_2), channel_id=1, source_target_pairs={{0,1},{2,3},{4,5},{6,7},{8,9},{10,11},{12,13},{14,15},{16,17},{18,... | collective-permute-start | bytes 1277960 | tf_op jit(solution)/shard_map/ppermute | solution.py:28
  72.8 0.1 collective-permute-start.7
  72.9 0.1 pad_add_fusion.place
  73.0 1.5 %all-to-all-done.1 = bf16[32,16,1024]{2,1,0:T(8,128)(2,1)S(1)} async-done(((bf16[32,16,1024]{2,1,0:T(8,128)(2,1)}), bf16[32,16,1024]{2,1,0:T(8,128)(2,1)S(1)}, u32[]{:S(2)}, u32[]{:S(2)}) %all-to-all-start.1) | async-done | bytes 1048608 | tf_op jit(solution)/shard_map/all_to_all | solution.py:32
  74.5 3.2 %collective-permute-done.6.sib_up_2 = bf16[208,1024]{1,0:T(8,128)(2,1)} collective-permute-done((bf16[208,1024]{1,0:T(8,128)(2,1)}, bf16[208,1024]{1,0:T(8,128)(2,1)}, u32[]{:S(2)}, u32[]{:S(2)}) %collective-permute-start.6) | collective-permute-done | bytes 426016 | tf_op jit(solution)/shard_map/ppermute | solution.py:28
  77.7 1.4 %collective-permute-start.13 = (bf16[512,1024]{1,0:T(8,128)(2,1)S(1)}, bf16[512,1024]{1,0:T(8,128)(2,1)S(1)}, u32[]{:S(2)}, u32[]{:S(2)}) collective-permute-start(bf16[512,1024]{1,0:T(8,128)(2,1)S(1)} %bitcast.9), channel_id=1, source_target_pairs={{1,0},{0,1},{3,2},{2,3},{5,4},{4,5},{7,6},{6,7},{9,8},{8,9},{11,10... | collective-permute-start | bytes 3145736 | tf_op jit(solution)/shard_map/ppermute | solution.py:28
  79.1 0.8 collective-permute-start.11
  79.9 5.4 %collective-permute-done.9.down_2 = bf16[304,1024]{1,0:T(8,128)(2,1)} collective-permute-done((bf16[304,1024]{1,0:T(8,128)(2,1)}, bf16[304,1024]{1,0:T(8,128)(2,1)}, u32[]{:S(2)}, u32[]{:S(2)}) %collective-permute-start.9) | collective-permute-done | bytes 622624 | tf_op jit(solution)/shard_map/ppermute | solution.py:14
  85.3 3.9 %shard_map.33 = (f32[2,512,512]{2,1,0:T(8,128)S(1)}, f32[1,2,1,256,512]{4,3,2,1,0:T(8,128)S(1)}) custom-call(s32[2]{0:T(128)S(1)} %pad_add_fusion.place, bf16[512,1024]{1,0:T(8,128)(2,1)S(1)} %bitcast.7, bf16[304,1024]{1,0:T(8,128)(2,1)} %collective-permute-done.1.down_1, bf16[208,1024]{1,0:T(8,128)(2,1)} %collective-permute-done.7.up_3, ...), custom_call_target="tpu_custom_call" | custom-call | flops 15032385536 | bytes 29360128 | tf_op jit(solution)/shard_map/pallas_call | solution.py:238
  89.2 7.9 %collective-permute-done.11.first = bf16[512,1024]{1,0:T(8,128)(2,1)S(1)} collective-permute-done((bf16[512,1024]{1,0:T(8,128)(2,1)S(1)}, bf16[512,1024]{1,0:T(8,128)(2,1)S(1)}, u32[]{:S(2)}, u32[]{:S(2)}) %collective-permute-start.11) | collective-permute-done | bytes 1048608 | tf_op jit(solution)/shard_map/ppermute | solution.py:24
  97.1 0.1 collective-permute-start.14
  97.2 3.4 %collective-permute-start.12 = (bf16[512,1024]{1,0:T(8,128)(2,1)S(1)}, bf16[512,1024]{1,0:T(8,128)(2,1)S(1)}, u32[]{:S(2)}, u32[]{:S(2)}) collective-permute-start(bf16[512,1024]{1,0:T(8,128)(2,1)S(1)} %bitcast.11), channel_id=1, source_target_pairs={{6,0},{3,1},{0,2},{5,3},{2,4},{7,5},{4,6},{1,7},{14,8},{11,9},{8,1... | collective-permute-start | bytes 3145736 | tf_op jit(solution)/shard_map/ppermute | solution.py:24
  100.6 1.3 %collective-permute-start.10 = (bf16[304,1024]{1,0:T(8,128)(2,1)}, bf16[304,1024]{1,0:T(8,128)(2,1)S(1)}, u32[]{:S(2)}, u32[]{:S(2)}) collective-permute-start(bf16[304,1024]{1,0:T(8,128)(2,1)} %collective-permute-done.9.down_2), channel_id=1, source_target_pairs={{0,1},{2,3},{4,5},{6,7},{8,9},{10,11},{12,13},{14,15},{16,17},{18,... | collective-permute-start | bytes 1867784 | tf_op jit(solution)/shard_map/ppermute | solution.py:28
  101.9 1.4 %collective-permute-start.8 = (bf16[208,1024]{1,0:T(8,128)(2,1)}, bf16[208,1024]{1,0:T(8,128)(2,1)S(1)}, u32[]{:S(2)}, u32[]{:S(2)}) collective-permute-start(bf16[208,1024]{1,0:T(8,128)(2,1)} %collective-permute-done.7.up_3), channel_id=1, source_target_pairs={{1,0},{0,1},{3,2},{2,3},{5,4},{4,5},{7,6},{6,7},{9,8},{8,9},{11,10... | collective-permute-start | bytes 1277960 | tf_op jit(solution)/shard_map/ppermute | solution.py:28
  103.4 2.0 %collective-permute-done.8.sib_up_3 = bf16[208,1024]{1,0:T(8,128)(2,1)S(1)} collective-permute-done((bf16[208,1024]{1,0:T(8,128)(2,1)}, bf16[208,1024]{1,0:T(8,128)(2,1)S(1)}, u32[]{:S(2)}, u32[]{:S(2)}) %collective-permute-start.8) | collective-permute-done | bytes 426016 | tf_op jit(solution)/shard_map/ppermute | solution.py:28
  105.4 4.9 %shard_map.32.band_in = f32[1,2,1,4,512,512]{5,4,3,2,1,0:T(8,128)S(1)} custom-call(s32[2]{0:T(128)S(1)} %pad_add_fusion.place, bf16[512,1024]{1,0:T(8,128)(2,1)S(1)} %bitcast.8, bf16[512,1024]{1,0:T(8,128)(2,1)S(1)} %collective-permute-done.4.sib_own, bf16[304,1024]{1,0:T(8,128)(2,1)} %collective-permute-done.5.sib_down_1, ...), custom_call_target="tpu_custom_call" | custom-call | flops 2147483648 | bytes 4194304 | tf_op jit(solution)/shard_map/pallas_call | solution.py:238
  110.3 2.0 %collective-permute-done.12.second = bf16[512,1024]{1,0:T(8,128)(2,1)S(1)} collective-permute-done((bf16[512,1024]{1,0:T(8,128)(2,1)S(1)}, bf16[512,1024]{1,0:T(8,128)(2,1)S(1)}, u32[]{:S(2)}, u32[]{:S(2)}) %collective-permute-start.12) | collective-permute-done | bytes 1048608 | tf_op jit(solution)/shard_map/ppermute | solution.py:24
  112.4 8.3 %shard_map.34 = (f32[1,2,1,4,512,512]{5,4,3,2,1,0:T(8,128)}, f32[1,2,1,256,512]{4,3,2,1,0:T(8,128)}) custom-call(s32[2]{0:T(128)S(1)} %pad_add_fusion.place, f32[1,2,1,4,512,512]{5,4,3,2,1,0:T(8,128)S(1)} %shard_map.32.band_in, f32[1,2,1,256,512]{4,3,2,1,0:T(8,128)S(1)} %get-tuple-element.22.far_in, f32[2,512,512]{2,1,0:T(8,128)S(1)} %get-tuple-element.23.ahead_in, ...), custom_call_target="tpu_custom_call" | custom-call | flops 5368709120 | bytes 10485760 | tf_op jit(solution)/shard_map/pallas_call | solution.py:238
  (10 shorter events, 0.1 us)
Async XLA Ops:
  2.7 38.5 %all-to-all-start = ((bf16[32,16,1024]{2,1,0:T(8,128)(2,1)}), bf16[32,16,1024]{2,1,0:T(8,128)(2,1)S(1)}, u32[]{:S(2)}, u32[]{:S(2)}) async-start(bf16[32,16,1024]{2,1,0:T(8,128)(2,1)} %shard_map.30), calls=%async_computation | async-start | bytes 2097152 | tf_op jit(solution)/shard_map/all_to_all | solution.py:32
  16.6 24.6 %collective-permute-start = (bf16[32,16,1024]{2,1,0:T(8,128)(2,1)}, bf16[32,16,1024]{2,1,0:T(8,128)(2,1)}, u32[]{:S(2)}, u32[]{:S(2)}) collective-permute-start(bf16[32,16,1024]{2,1,0:T(8,128)(2,1)} %shard_map.31), channel_id=1, source_target_pairs={{2,0},{4,2},{6,4},{0,6},{3,1},{5,3},{7,5},{1,7},{10,8},{12,10},{14... | collective-permute-start | bytes 3145736 | tf_op jit(solution)/shard_map/ppermute | solution.py:14
  41.2 33.3 %all-to-all-start.1 = ((bf16[32,16,1024]{2,1,0:T(8,128)(2,1)}), bf16[32,16,1024]{2,1,0:T(8,128)(2,1)S(1)}, u32[]{:S(2)}, u32[]{:S(2)}) async-start(bf16[32,16,1024]{2,1,0:T(8,128)(2,1)} %collective-permute-done), calls=%async_computation.1 | async-start | bytes 2097152 | tf_op jit(solution)/shard_map/all_to_all | solution.py:32
  50.1 11.2 %collective-permute-start.2 = (bf16[208,1024]{1,0:T(8,128)(2,1)S(1)}, bf16[208,1024]{1,0:T(8,128)(2,1)S(1)}, u32[]{:S(2)}, u32[]{:S(2)}) collective-permute-start(bf16[208,1024]{1,0:T(8,128)(2,1)S(1)} %bitcast.14), channel_id=1, source_target_pairs={{6,0},{0,2},{2,4},{4,6},{7,1},{1,3},{3,5},{5,7},{14,8},{8,10},{10,... | collective-permute-start | bytes 1277960 | tf_op jit(solution)/shard_map/ppermute | solution.py:14
  51.0 13.6 %collective-permute-start.1 = (bf16[304,1024]{1,0:T(8,128)(2,1)S(1)}, bf16[304,1024]{1,0:T(8,128)(2,1)}, u32[]{:S(2)}, u32[]{:S(2)}) collective-permute-start(bf16[304,1024]{1,0:T(8,128)(2,1)S(1)} %bitcast.13), channel_id=1, source_target_pairs={{2,0},{4,2},{6,4},{0,6},{3,1},{5,3},{7,5},{1,7},{10,8},{12,10},{14... | collective-permute-start | bytes 1867784 | tf_op jit(solution)/shard_map/ppermute | solution.py:14
  53.8 19.2 %collective-permute-start.4 = (bf16[512,1024]{1,0:T(8,128)(2,1)S(1)}, bf16[512,1024]{1,0:T(8,128)(2,1)S(1)}, u32[]{:S(2)}, u32[]{:S(2)}) collective-permute-start(bf16[512,1024]{1,0:T(8,128)(2,1)S(1)} %bitcast.6), channel_id=1, source_target_pairs={{1,0},{3,2},{5,4},{7,6},{9,8},{11,10},{13,12},{15,14},{17,16},{19,... | collective-permute-start | bytes 3145736 | tf_op jit(solution)/shard_map/ppermute | solution.py:28
  61.3 10.2 %collective-permute-start.3 = (bf16[208,1024]{1,0:T(8,128)(2,1)S(1)}, bf16[208,1024]{1,0:T(8,128)(2,1)}, u32[]{:S(2)}, u32[]{:S(2)}) collective-permute-start(bf16[208,1024]{1,0:T(8,128)(2,1)S(1)} %collective-permute-done.2), channel_id=1, source_target_pairs={{6,0},{0,2},{2,4},{4,6},{7,1},{1,3},{3,5},{5,7},{14,8},{8,10},{10,... | collective-permute-start | bytes 1277960 | tf_op jit(solution)/shard_map/ppermute | solution.py:14
  64.7 9.8 %collective-permute-start.5 = (bf16[304,1024]{1,0:T(8,128)(2,1)}, bf16[304,1024]{1,0:T(8,128)(2,1)}, u32[]{:S(2)}, u32[]{:S(2)}) collective-permute-start(bf16[304,1024]{1,0:T(8,128)(2,1)} %collective-permute-done.1.down_1), channel_id=1, source_target_pairs={{1,0},{0,1},{3,2},{2,3},{5,4},{4,5},{7,6},{6,7},{9,8},{8,9},{11,10... | collective-permute-start | bytes 1867784 | tf_op jit(solution)/shard_map/ppermute | solution.py:28
  68.0 17.3 %collective-permute-start.9 = (bf16[304,1024]{1,0:T(8,128)(2,1)}, bf16[304,1024]{1,0:T(8,128)(2,1)}, u32[]{:S(2)}, u32[]{:S(2)}) collective-permute-start(bf16[304,1024]{1,0:T(8,128)(2,1)} %collective-permute-done.1.down_1), channel_id=1, source_target_pairs={{2,0},{4,2},{6,4},{0,6},{3,1},{5,3},{7,5},{1,7},{10,8},{12,10},{14... | collective-permute-start | bytes 1867784 | tf_op jit(solution)/shard_map/ppermute | solution.py:14
  71.5 6.2 %collective-permute-start.6 = (bf16[208,1024]{1,0:T(8,128)(2,1)}, bf16[208,1024]{1,0:T(8,128)(2,1)}, u32[]{:S(2)}, u32[]{:S(2)}) collective-permute-start(bf16[208,1024]{1,0:T(8,128)(2,1)} %collective-permute-done.3.up_2), channel_id=1, source_target_pairs={{0,1},{2,3},{4,5},{6,7},{8,9},{10,11},{12,13},{14,15},{16,17},{18,... | collective-permute-start | bytes 1277960 | tf_op jit(solution)/shard_map/ppermute | solution.py:28
  72.8 12.5 %collective-permute-start.7 = (bf16[208,1024]{1,0:T(8,128)(2,1)}, bf16[208,1024]{1,0:T(8,128)(2,1)}, u32[]{:S(2)}, u32[]{:S(2)}) collective-permute-start(bf16[208,1024]{1,0:T(8,128)(2,1)} %collective-permute-done.3.up_2), channel_id=1, source_target_pairs={{6,0},{0,2},{2,4},{4,6},{7,1},{1,3},{3,5},{5,7},{14,8},{8,10},{10,... | collective-permute-start | bytes 1277960 | tf_op jit(solution)/shard_map/ppermute | solution.py:14
  77.7 32.6 %collective-permute-start.13 = (bf16[512,1024]{1,0:T(8,128)(2,1)S(1)}, bf16[512,1024]{1,0:T(8,128)(2,1)S(1)}, u32[]{:S(2)}, u32[]{:S(2)}) collective-permute-start(bf16[512,1024]{1,0:T(8,128)(2,1)S(1)} %bitcast.9), channel_id=1, source_target_pairs={{1,0},{0,1},{3,2},{2,3},{5,4},{4,5},{7,6},{6,7},{9,8},{8,9},{11,10... | collective-permute-start | bytes 3145736 | tf_op jit(solution)/shard_map/ppermute | solution.py:28
  79.1 18.0 %collective-permute-start.11 = (bf16[512,1024]{1,0:T(8,128)(2,1)S(1)}, bf16[512,1024]{1,0:T(8,128)(2,1)S(1)}, u32[]{:S(2)}, u32[]{:S(2)}) collective-permute-start(bf16[512,1024]{1,0:T(8,128)(2,1)S(1)} %bitcast.10), channel_id=1, source_target_pairs={{2,0},{7,1},{4,2},{1,3},{6,4},{3,5},{0,6},{5,7},{10,8},{15,9},{12,... | collective-permute-start | bytes 3145736 | tf_op jit(solution)/shard_map/ppermute | solution.py:24
  97.1 13.2 %collective-permute-start.14 = (bf16[512,1024]{1,0:T(8,128)(2,1)S(1)}, bf16[512,1024]{1,0:T(8,128)(2,1)S(1)}, u32[]{:S(2)}, u32[]{:S(2)}) collective-permute-start(bf16[512,1024]{1,0:T(8,128)(2,1)S(1)} %collective-permute-done.11.first), channel_id=1, source_target_pairs={{1,0},{0,1},{3,2},{2,3},{5,4},{4,5},{7,6},{6,7},{9,8},{8,9},{11,10... | collective-permute-start | bytes 3145736 | tf_op jit(solution)/shard_map/ppermute | solution.py:28
  97.2 15.2 %collective-permute-start.12 = (bf16[512,1024]{1,0:T(8,128)(2,1)S(1)}, bf16[512,1024]{1,0:T(8,128)(2,1)S(1)}, u32[]{:S(2)}, u32[]{:S(2)}) collective-permute-start(bf16[512,1024]{1,0:T(8,128)(2,1)S(1)} %bitcast.11), channel_id=1, source_target_pairs={{6,0},{3,1},{0,2},{5,3},{2,4},{7,5},{4,6},{1,7},{14,8},{11,9},{8,1... | collective-permute-start | bytes 3145736 | tf_op jit(solution)/shard_map/ppermute | solution.py:24
  100.6 4.8 %collective-permute-start.10 = (bf16[304,1024]{1,0:T(8,128)(2,1)}, bf16[304,1024]{1,0:T(8,128)(2,1)S(1)}, u32[]{:S(2)}, u32[]{:S(2)}) collective-permute-start(bf16[304,1024]{1,0:T(8,128)(2,1)} %collective-permute-done.9.down_2), channel_id=1, source_target_pairs={{0,1},{2,3},{4,5},{6,7},{8,9},{10,11},{12,13},{14,15},{16,17},{18,... | collective-permute-start | bytes 1867784 | tf_op jit(solution)/shard_map/ppermute | solution.py:28
  101.9 3.5 %collective-permute-start.8 = (bf16[208,1024]{1,0:T(8,128)(2,1)}, bf16[208,1024]{1,0:T(8,128)(2,1)S(1)}, u32[]{:S(2)}, u32[]{:S(2)}) collective-permute-start(bf16[208,1024]{1,0:T(8,128)(2,1)} %collective-permute-done.7.up_3), channel_id=1, source_target_pairs={{1,0},{0,1},{3,2},{2,3},{5,4},{4,5},{7,6},{6,7},{9,8},{8,9},{11,10... | collective-permute-start | bytes 1277960 | tf_op jit(solution)/shard_map/ppermute | solution.py:28

commit v6 on v5

--- a/solution.py
+++ b/solution.py
@@ -81,7 +81,7 @@
 
 
 def ahead_kernel(
-    place, own_at, down_1, up_3, down_2, up_2, tile, far, swapped, own, ahead, beyond, sems
+    place, own_at, down_1, up_3, down_2, up_2, tile, far, ahead, beyond, swapped, own, sems
 ):
     upper = place[1]
     first, second = pl.ds(0, down_1.shape[0]), pl.ds(down_1.shape[0], up_3.shape[0])
@@ -110,53 +110,34 @@
 
 
 def early_kernel(
-    place, own_at, sib_own, sib_down_1, sib_up_3, sib_down_2, sib_up_2, band,
-    swapped, own, sib_ahead, other, sems,
+    place, own_at, sib_own, sib_ahead_at, sib_beyond, band, swapped, own, sib_ahead, other, sems
 ):
     core = place[0]
-    first = pl.ds(0, sib_down_1.shape[0])
-    second = pl.ds(sib_down_1.shape[0], sib_up_3.shape[0])
 
     def load(number, source, target):
         return pltpu.make_async_copy(source, target, sems.at[number])
 
-    own_load = load(0, own_at, own)
-    sib_loads = [load(1, sib_down_1, sib_ahead.at[first]), load(2, sib_up_3, sib_ahead.at[second])]
-    near_load = load(3, sib_own, other)
-    far_loads = [load(3, sib_down_2, other.at[first]), load(4, sib_up_2, other.at[second])]
-
-    for copy in (own_load, *sib_loads):
-        copy.start()
+    load(0, own_at, own).start()
+    load(1, sib_ahead_at, sib_ahead).start()
 
     @pl.when(core == 0)
     def _():
-        near_load.start()
+        load(2, sib_own, other).start()
 
     @pl.when(core != 0)
     def _():
-        for copy in far_loads:
-            copy.start()
+        load(2, sib_beyond, other).start()
 
     def tile(slot, columns):
         for part, left in enumerate((own, swapped)):
             band[0, part, 0, slot] = times(left[...], columns[...])
 
-    own_load.wait()
+    load(0, own_at, own).wait()
     swapped[...] = quadrature(own[...])
     tile(0, own)
-    for copy in sib_loads:
-        copy.wait()
+    load(1, sib_ahead_at, sib_ahead).wait()
     tile(3 - 2 * core, sib_ahead)
-
-    @pl.when(core == 0)
-    def _():
-        near_load.wait()
-
-    @pl.when(core != 0)
-    def _():
-        for copy in far_loads:
-            copy.wait()
-
+    load(2, sib_own, other).wait()
     tile(1 + 2 * core, other)
 
 
@@ -272,35 +253,34 @@
     down_2 = from_ahead(down_1, 1)
     up_3 = from_ahead(up_2, -1)
     sib_own = from_sibling(own, (0,))
-    sib_down_1 = from_sibling(down_1)
-    sib_up_2 = from_sibling(up_2, (1,))
-    late_ahead, down_1, up_2, sib_own, sib_down_1, sib_up_2 = lax.optimization_barrier(
-        (late_ahead, down_1, up_2, sib_own, sib_down_1, sib_up_2)
+    late_ahead, down_1, up_2, sib_own = lax.optimization_barrier(
+        (late_ahead, down_1, up_2, sib_own)
     )
     late_first = from_both_sides(late_ahead, 0)
-    late_sib_ahead = from_sibling(late_ahead)
-
-    sib_up_3 = from_sibling(up_3)
-    sib_down_2 = from_sibling(down_2, (1,))
 
     rows = own.shape[0]
     block = pltpu.VMEM(own.shape, own.dtype)
     band_shape, far_shape = (1, 2, 1, 4, rows, rows), (1, 2, 1, rows // 2, rows)
-    ahead_sum, far_sum = call(
+    ahead_sum, far_sum, ahead, beyond = call(
         ahead_kernel, (1,), place, (own, down_1, up_3, down_2, up_2), (),
-        [pltpu.VMEM((2, rows, rows), jnp.float32), pltpu.VMEM(far_shape, jnp.float32)],
-        [IN_VMEM, IN_VMEM], {}, 14, [block] * 4 + [pltpu.SemaphoreType.DMA((5,))],
-    )
-    late_ahead, late_first, ahead_sum, far_sum = lax.optimization_barrier(
-        (late_ahead, late_first, ahead_sum, far_sum)
+        [
+            pltpu.VMEM((2, rows, rows), jnp.float32), pltpu.VMEM(far_shape, jnp.float32),
+            block, block,
+        ],
+        [IN_VMEM] * 4, {}, 14, [block] * 2 + [pltpu.SemaphoreType.DMA((5,))],
+    )
+    sib_ahead = from_sibling(ahead)
+    sib_beyond = from_sibling(beyond, (1,))
+    late_sib_ahead = from_sibling(late_ahead)
+    late_ahead, late_first, ahead_sum, far_sum, sib_ahead, sib_beyond = lax.optimization_barrier(
+        (late_ahead, late_first, ahead_sum, far_sum, sib_ahead, sib_beyond)
     )
     late_second = from_both_sides(late_ahead, 1)
     late_sib_first = from_sibling(late_first)
     (band_sum,) = call(
-        early_kernel, (1,), place,
-        (own, sib_own, sib_down_1, sib_up_3, sib_down_2, sib_up_2), (),
+        early_kernel, (1,), place, (own, sib_own, sib_ahead, sib_beyond), (),
         [pltpu.VMEM(band_shape, jnp.float32)], [IN_VMEM], {}, 2,
-        [block] * 4 + [pltpu.SemaphoreType.DMA((5,))],
+        [block] * 4 + [pltpu.SemaphoreType.DMA((3,))],
     )
     band_out = jax.ShapeDtypeStruct(band_shape, jnp.float32)
     far_out = jax.ShapeDtypeStruct(far_shape, jnp.float32)

time: 121 us -> 121 us (level)
    ppermute x7 -> x5, starting transfers between devices: 13.5 us -> 16.9 us  [from_sibling(): return lax.ppermute(block, 'acol', [(1 - core, core) for core in cores])]
    ppermute x7 -> x5, waiting for transfers between devices: 5.3 us -> 1.98 us  [from_sibling(): return lax.ppermute(block, 'acol', [(1 - core, core) for core in cores])]
    ppermute x2, starting transfers between devices: 4.17 us -> 1.5 us  [from_both_sides(): return lax.ppermute(block, ('arow', 'acol'), route)]
    all_to_all x2, waiting for transfers between devices: 1.48 us -> 3.55 us  [turn(): lax.all_to_all(block, 'chan', split_axis=0, concat_axis=0, tiled=True)]
    ppermute x6, waiting for transfers between devices: 33.5 us -> 35.1 us  [from_ahead(): lax.ppermute(block, 'arow', [((i + distance) % size, i) for i in range(si...]
    ppermute x2, waiting for transfers between devices: 9.94 us -> 8.37 us  [from_both_sides(): return lax.ppermute(block, ('arow', 'acol'), route)]
  transfers between devices with their start and end apart: 17 -> 15, of which waited for: 9 -> 9; matrix products, arithmetic and copies ran while one was open for 0% -> 0% of each run, Pallas kernels for 9% -> 9%
where the time goes in v6:
time: 121 us; the launch traced here: 120 us
  starting transfers between devices  49 us (40%)
  waiting for transfers between devices  49 us (40%)
  Pallas kernels  21.1 us (17%)
    ppermute x6, waiting for transfers between devices, from_ahead(): lax.ppermute(block, 'arow', [((i + distance) % size, i) for i in range(si...  35.1 us
    all_to_all x2, starting transfers between devices, turn(): lax.all_to_all(block, 'chan', split_axis=0, concat_axis=0, tiled=True)  20.8 us
    pallas_call x3, Pallas kernels, call(): pl.pallas_call(kernel, out_shape=outs, grid_spec=pltpu.PrefetchScalarGrid...  17 us
    ppermute x5, starting transfers between devices, from_sibling(): return lax.ppermute(block, 'acol', [(1 - core, core) for core in cores])  16.9 us
    ppermute x6, starting transfers between devices, from_ahead(): lax.ppermute(block, 'arow', [((i + distance) % size, i) for i in range(si...  9.84 us
    ppermute x2, waiting for transfers between devices, from_both_sides(): return lax.ppermute(block, ('arow', 'acol'), route)  8.37 us
    pallas_call x2, Pallas kernels, half_of(): pl.pallas_call(cut_kernel, out_shape=jax.ShapeDtypeStruct((channels, rows...  4.1 us
    all_to_all x2, waiting for transfers between devices, turn(): lax.all_to_all(block, 'chan', split_axis=0, concat_axis=0, tiled=True)  3.55 us
  transfers between devices with their start and end apart: 15, of which 9 were waited for; matrix products, arithmetic and copies ran while one was open for 0% of the time, Pallas kernels for 9%

profile of v6, /device:TPU:1, one launch (start us, length us, event | category | flops | bytes accessed | tf_op | source)
XLA Modules:
  0.0 120.2 jit_solution(16662837118358008373)
XLA Ops:
  0.6 2.1 %shard_map.30 = bf16[32,16,1024]{2,1,0:T(8,128)(2,1)} custom-call(bf16[32,1,16,2048]{3,2,1,0:T(8,128)(2,1)} %imaginary.3, bf16[32,1,16,2048]{3,2,1,0:T(8,128)(2,1)} %imaginary.3), custom_call_target="tpu_custom_call" | custom-call | tf_op jit(solution)/shard_map/pallas_call | solution.py:45
  2.7 11.9 %all-to-all-start = ((bf16[32,16,1024]{2,1,0:T(8,128)(2,1)}), bf16[32,16,1024]{2,1,0:T(8,128)(2,1)S(1)}, u32[]{:S(2)}, u32[]{:S(2)}) async-start(bf16[32,16,1024]{2,1,0:T(8,128)(2,1)} %shard_map.30), calls=%async_computation | async-start | bytes 2097152 | tf_op jit(solution)/shard_map/all_to_all | solution.py:32
  14.6 2.1 %shard_map.31 = bf16[32,16,1024]{2,1,0:T(8,128)(2,1)} custom-call(bf16[32,1,16,2048]{3,2,1,0:T(8,128)(2,1)} %imaginary.3, bf16[32,1,16,2048]{3,2,1,0:T(8,128)(2,1)} %imaginary.3), custom_call_target="tpu_custom_call" | custom-call | tf_op jit(solution)/shard_map/pallas_call | solution.py:45
  16.6 2.7 %collective-permute-start = (bf16[32,16,1024]{2,1,0:T(8,128)(2,1)}, bf16[32,16,1024]{2,1,0:T(8,128)(2,1)}, u32[]{:S(2)}, u32[]{:S(2)}) collective-permute-start(bf16[32,16,1024]{2,1,0:T(8,128)(2,1)} %shard_map.31), channel_id=1, source_target_pairs={{2,0},{4,2},{6,4},{0,6},{3,1},{5,3},{7,5},{1,7},{10,8},{12,10},{14... | collective-permute-start | bytes 3145736 | tf_op jit(solution)/shard_map/ppermute | solution.py:14
  19.3 21.8 %collective-permute-done = bf16[32,16,1024]{2,1,0:T(8,128)(2,1)} collective-permute-done((bf16[32,16,1024]{2,1,0:T(8,128)(2,1)}, bf16[32,16,1024]{2,1,0:T(8,128)(2,1)}, u32[]{:S(2)}, u32[]{:S(2)}) %collective-permute-start) | collective-permute-done | bytes 1048608 | tf_op jit(solution)/shard_map/ppermute | solution.py:14
  41.2 8.9 %all-to-all-start.1 = ((bf16[32,16,1024]{2,1,0:T(8,128)(2,1)}), bf16[32,16,1024]{2,1,0:T(8,128)(2,1)S(1)}, u32[]{:S(2)}, u32[]{:S(2)}) async-start(bf16[32,16,1024]{2,1,0:T(8,128)(2,1)} %collective-permute-done), calls=%async_computation.1 | async-start | bytes 2097152 | tf_op jit(solution)/shard_map/all_to_all | solution.py:32
  50.1 0.8 collective-permute-start.2
  51.0 2.7 %collective-permute-start.1 = (bf16[304,1024]{1,0:T(8,128)(2,1)S(1)}, bf16[304,1024]{1,0:T(8,128)(2,1)}, u32[]{:S(2)}, u32[]{:S(2)}) collective-permute-start(bf16[304,1024]{1,0:T(8,128)(2,1)S(1)} %bitcast.13), channel_id=1, source_target_pairs={{2,0},{4,2},{6,4},{0,6},{3,1},{5,3},{7,5},{1,7},{10,8},{12,10},{14... | collective-permute-start | bytes 1867784 | tf_op jit(solution)/shard_map/ppermute | solution.py:14
  53.8 4.7 %collective-permute-start.4 = (bf16[512,1024]{1,0:T(8,128)(2,1)S(1)}, bf16[512,1024]{1,0:T(8,128)(2,1)S(1)}, u32[]{:S(2)}, u32[]{:S(2)}) collective-permute-start(bf16[512,1024]{1,0:T(8,128)(2,1)S(1)} %bitcast.6), channel_id=1, source_target_pairs={{1,0},{3,2},{5,4},{7,6},{9,8},{11,10},{13,12},{15,14},{17,16},{19,... | collective-permute-start | bytes 3145736 | tf_op jit(solution)/shard_map/ppermute | solution.py:28
  58.5 2.9 %collective-permute-done.2 = bf16[208,1024]{1,0:T(8,128)(2,1)S(1)} collective-permute-done((bf16[208,1024]{1,0:T(8,128)(2,1)S(1)}, bf16[208,1024]{1,0:T(8,128)(2,1)S(1)}, u32[]{:S(2)}, u32[]{:S(2)}) %collective-permute-start.2) | collective-permute-done | bytes 426016 | tf_op jit(solution)/shard_map/ppermute | solution.py:14
  61.3 0.0 collective-permute-start.3
  61.3 3.3 %collective-permute-done.1.down_1 = bf16[304,1024]{1,0:T(8,128)(2,1)} collective-permute-done((bf16[304,1024]{1,0:T(8,128)(2,1)S(1)}, bf16[304,1024]{1,0:T(8,128)(2,1)}, u32[]{:S(2)}, u32[]{:S(2)}) %collective-permute-start.1) | collective-permute-done | bytes 622624 | tf_op jit(solution)/shard_map/ppermute | solution.py:14
  64.7 3.5 %collective-permute-start.7 = (bf16[304,1024]{1,0:T(8,128)(2,1)}, bf16[304,1024]{1,0:T(8,128)(2,1)}, u32[]{:S(2)}, u32[]{:S(2)}) collective-permute-start(bf16[304,1024]{1,0:T(8,128)(2,1)} %collective-permute-done.1.down_1), channel_id=1, source_target_pairs={{2,0},{4,2},{6,4},{0,6},{3,1},{5,3},{7,5},{1,7},{10,8},{12,10},{14... | collective-permute-start | bytes 1867784 | tf_op jit(solution)/shard_map/ppermute | solution.py:14
  68.2 2.7 %collective-permute-done.3.up_2 = bf16[208,1024]{1,0:T(8,128)(2,1)} collective-permute-done((bf16[208,1024]{1,0:T(8,128)(2,1)S(1)}, bf16[208,1024]{1,0:T(8,128)(2,1)}, u32[]{:S(2)}, u32[]{:S(2)}) %collective-permute-start.3) | collective-permute-done | bytes 426016 | tf_op jit(solution)/shard_map/ppermute | solution.py:14
  70.9 0.0 collective-permute-start.6
  70.9 0.1 pad_add_fusion.place
  70.9 0.0 collective-permute-done.4.sib_own
  70.9 3.5 %all-to-all-done.1 = bf16[32,16,1024]{2,1,0:T(8,128)(2,1)S(1)} async-done(((bf16[32,16,1024]{2,1,0:T(8,128)(2,1)}), bf16[32,16,1024]{2,1,0:T(8,128)(2,1)S(1)}, u32[]{:S(2)}, u32[]{:S(2)}) %all-to-all-start.1) | async-done | bytes 1048608 | tf_op jit(solution)/shard_map/all_to_all | solution.py:32
  74.5 0.8 collective-permute-start.5
  75.2 3.2 %collective-permute-done.7.down_2 = bf16[304,1024]{1,0:T(8,128)(2,1)} collective-permute-done((bf16[304,1024]{1,0:T(8,128)(2,1)}, bf16[304,1024]{1,0:T(8,128)(2,1)}, u32[]{:S(2)}, u32[]{:S(2)}) %collective-permute-start.7) | collective-permute-done | bytes 622624 | tf_op jit(solution)/shard_map/ppermute | solution.py:14
  78.4 1.2 %collective-permute-done.6.up_3 = bf16[208,1024]{1,0:T(8,128)(2,1)} collective-permute-done((bf16[208,1024]{1,0:T(8,128)(2,1)}, bf16[208,1024]{1,0:T(8,128)(2,1)}, u32[]{:S(2)}, u32[]{:S(2)}) %collective-permute-start.6) | collective-permute-done | bytes 426016 | tf_op jit(solution)/shard_map/ppermute | solution.py:14
  79.7 3.9 %shard_map.32 = (f32[2,512,512]{2,1,0:T(8,128)S(1)}, f32[1,2,1,256,512]{4,3,2,1,0:T(8,128)S(1)}, bf16[512,1024]{1,0:T(8,128)(2,1)S(1)}, bf16[512,1024]{1,0:T(8,128)(2,1)S(1)}) custom-call(s32[2]{0:T(128)S(1)} %pad_add_fusion.place, bf16[512,1024]{1,0:T(8,128)(2,1)S(1)} %bitcast.7, bf16[304,1024]{1,0:T(8,128)(2,1)} %collective-permute-done.1.down_1, ...), custom_call_target="tpu_custom_call" | custom-call | flops 15032385536 | bytes 29360128 | tf_op jit(solution)/shard_map/pallas_call | solution.py:219
  83.6 9.5 %collective-permute-start.8 = (bf16[512,1024]{1,0:T(8,128)(2,1)S(1)}, bf16[512,1024]{1,0:T(8,128)(2,1)S(1)}, u32[]{:S(2)}, u32[]{:S(2)}) collective-permute-start(bf16[512,1024]{1,0:T(8,128)(2,1)S(1)} %get-tuple-element.22), channel_id=1, source_target_pairs={{1,0},{0,1},{3,2},{2,3},{5,4},{4,5},{7,6},{6,7},{9,8},{8,9},{11,10... | collective-permute-start | bytes 3145736 | tf_op jit(solution)/shard_map/ppermute | solution.py:28
  93.1 1.3 %collective-permute-start.9 = (bf16[512,1024]{1,0:T(8,128)(2,1)S(1)}, bf16[512,1024]{1,0:T(8,128)(2,1)S(1)}, u32[]{:S(2)}, u32[]{:S(2)}) collective-permute-start(bf16[512,1024]{1,0:T(8,128)(2,1)S(1)} %get-tuple-element.23), channel_id=1, source_target_pairs={{0,1},{2,3},{4,5},{6,7},{8,9},{10,11},{12,13},{14,15},{16,17},{18,... | collective-permute-start | bytes 3145736 | tf_op jit(solution)/shard_map/ppermute | solution.py:28
  94.4 1.3 %collective-permute-start.11 = (bf16[512,1024]{1,0:T(8,128)(2,1)S(1)}, bf16[512,1024]{1,0:T(8,128)(2,1)S(1)}, u32[]{:S(2)}, u32[]{:S(2)}) collective-permute-start(bf16[512,1024]{1,0:T(8,128)(2,1)S(1)} %bitcast.10), channel_id=1, source_target_pairs={{1,0},{0,1},{3,2},{2,3},{5,4},{4,5},{7,6},{6,7},{9,8},{8,9},{11,10... | collective-permute-start | bytes 3145736 | tf_op jit(solution)/shard_map/ppermute | solution.py:28
  95.7 0.0 collective-permute-done.5.first
  95.7 2.0 %collective-permute-done.9.sib_beyond = bf16[512,1024]{1,0:T(8,128)(2,1)S(1)} collective-permute-done((bf16[512,1024]{1,0:T(8,128)(2,1)S(1)}, bf16[512,1024]{1,0:T(8,128)(2,1)S(1)}, u32[]{:S(2)}, u32[]{:S(2)}) %collective-permute-start.9) | collective-permute-done | bytes 1048608 | tf_op jit(solution)/shard_map/ppermute | solution.py:28
  97.7 0.1 collective-permute-start.12
  97.8 0.7 collective-permute-start.10
  98.5 4.8 %shard_map.33.band_in = f32[1,2,1,4,512,512]{5,4,3,2,1,0:T(8,128)S(1)} custom-call(s32[2]{0:T(128)S(1)} %pad_add_fusion.place, bf16[512,1024]{1,0:T(8,128)(2,1)S(1)} %bitcast.8, bf16[512,1024]{1,0:T(8,128)(2,1)S(1)} %collective-permute-done.4.sib_own, bf16[512,1024]{1,0:T(8,128)(2,1)S(1)} %collective-permute-done.8.sib_ahead_at, ...), custom_call_target="tpu_custom_call" | custom-call | flops 2147483648 | bytes 4194304 | tf_op jit(solution)/shard_map/pallas_call | solution.py:219
  103.4 8.4 %collective-permute-done.10.second = bf16[512,1024]{1,0:T(8,128)(2,1)S(1)} collective-permute-done((bf16[512,1024]{1,0:T(8,128)(2,1)S(1)}, bf16[512,1024]{1,0:T(8,128)(2,1)S(1)}, u32[]{:S(2)}, u32[]{:S(2)}) %collective-permute-start.10) | collective-permute-done | bytes 1048608 | tf_op jit(solution)/shard_map/ppermute | solution.py:24
  111.7 8.3 %shard_map.34 = (f32[1,2,1,4,512,512]{5,4,3,2,1,0:T(8,128)}, f32[1,2,1,256,512]{4,3,2,1,0:T(8,128)}) custom-call(s32[2]{0:T(128)S(1)} %pad_add_fusion.place, f32[1,2,1,4,512,512]{5,4,3,2,1,0:T(8,128)S(1)} %shard_map.33.band_in, f32[1,2,1,256,512]{4,3,2,1,0:T(8,128)S(1)} %get-tuple-element.26.far_in, f32[2,512,512]{2,1,0:T(8,128)S(1)} %get-tuple-element.27.ahead_in, ...), custom_call_target="tpu_custom_call" | custom-call | flops 5368709120 | bytes 10485760 | tf_op jit(solution)/shard_map/pallas_call | solution.py:219
  (6 shorter events, 0.1 us)
Async XLA Ops:
  2.7 38.5 %all-to-all-start = ((bf16[32,16,1024]{2,1,0:T(8,128)(2,1)}), bf16[32,16,1024]{2,1,0:T(8,128)(2,1)S(1)}, u32[]{:S(2)}, u32[]{:S(2)}) async-start(bf16[32,16,1024]{2,1,0:T(8,128)(2,1)} %shard_map.30), calls=%async_computation | async-start | bytes 2097152 | tf_op jit(solution)/shard_map/all_to_all | solution.py:32
  16.6 24.6 %collective-permute-start = (bf16[32,16,1024]{2,1,0:T(8,128)(2,1)}, bf16[32,16,1024]{2,1,0:T(8,128)(2,1)}, u32[]{:S(2)}, u32[]{:S(2)}) collective-permute-start(bf16[32,16,1024]{2,1,0:T(8,128)(2,1)} %shard_map.31), channel_id=1, source_target_pairs={{2,0},{4,2},{6,4},{0,6},{3,1},{5,3},{7,5},{1,7},{10,8},{12,10},{14... | collective-permute-start | bytes 3145736 | tf_op jit(solution)/shard_map/ppermute | solution.py:14
  41.2 33.3 %all-to-all-start.1 = ((bf16[32,16,1024]{2,1,0:T(8,128)(2,1)}), bf16[32,16,1024]{2,1,0:T(8,128)(2,1)S(1)}, u32[]{:S(2)}, u32[]{:S(2)}) async-start(bf16[32,16,1024]{2,1,0:T(8,128)(2,1)} %collective-permute-done), calls=%async_computation.1 | async-start | bytes 2097152 | tf_op jit(solution)/shard_map/all_to_all | solution.py:32
  50.1 11.2 %collective-permute-start.2 = (bf16[208,1024]{1,0:T(8,128)(2,1)S(1)}, bf16[208,1024]{1,0:T(8,128)(2,1)S(1)}, u32[]{:S(2)}, u32[]{:S(2)}) collective-permute-start(bf16[208,1024]{1,0:T(8,128)(2,1)S(1)} %bitcast.14), channel_id=1, source_target_pairs={{6,0},{0,2},{2,4},{4,6},{7,1},{1,3},{3,5},{5,7},{14,8},{8,10},{10,... | collective-permute-start | bytes 1277960 | tf_op jit(solution)/shard_map/ppermute | solution.py:14
  51.0 13.6 %collective-permute-start.1 = (bf16[304,1024]{1,0:T(8,128)(2,1)S(1)}, bf16[304,1024]{1,0:T(8,128)(2,1)}, u32[]{:S(2)}, u32[]{:S(2)}) collective-permute-start(bf16[304,1024]{1,0:T(8,128)(2,1)S(1)} %bitcast.13), channel_id=1, source_target_pairs={{2,0},{4,2},{6,4},{0,6},{3,1},{5,3},{7,5},{1,7},{10,8},{12,10},{14... | collective-permute-start | bytes 1867784 | tf_op jit(solution)/shard_map/ppermute | solution.py:14
  53.8 17.2 %collective-permute-start.4 = (bf16[512,1024]{1,0:T(8,128)(2,1)S(1)}, bf16[512,1024]{1,0:T(8,128)(2,1)S(1)}, u32[]{:S(2)}, u32[]{:S(2)}) collective-permute-start(bf16[512,1024]{1,0:T(8,128)(2,1)S(1)} %bitcast.6), channel_id=1, source_target_pairs={{1,0},{3,2},{5,4},{7,6},{9,8},{11,10},{13,12},{15,14},{17,16},{19,... | collective-permute-start | bytes 3145736 | tf_op jit(solution)/shard_map/ppermute | solution.py:28
  61.3 9.5 %collective-permute-start.3 = (bf16[208,1024]{1,0:T(8,128)(2,1)S(1)}, bf16[208,1024]{1,0:T(8,128)(2,1)}, u32[]{:S(2)}, u32[]{:S(2)}) collective-permute-start(bf16[208,1024]{1,0:T(8,128)(2,1)S(1)} %collective-permute-done.2), channel_id=1, source_target_pairs={{6,0},{0,2},{2,4},{4,6},{7,1},{1,3},{3,5},{5,7},{14,8},{8,10},{10,... | collective-permute-start | bytes 1277960 | tf_op jit(solution)/shard_map/ppermute | solution.py:14
  64.7 13.8 %collective-permute-start.7 = (bf16[304,1024]{1,0:T(8,128)(2,1)}, bf16[304,1024]{1,0:T(8,128)(2,1)}, u32[]{:S(2)}, u32[]{:S(2)}) collective-permute-start(bf16[304,1024]{1,0:T(8,128)(2,1)} %collective-permute-done.1.down_1), channel_id=1, source_target_pairs={{2,0},{4,2},{6,4},{0,6},{3,1},{5,3},{7,5},{1,7},{10,8},{12,10},{14... | collective-permute-start | bytes 1867784 | tf_op jit(solution)/shard_map/ppermute | solution.py:14
  70.9 8.8 %collective-permute-start.6 = (bf16[208,1024]{1,0:T(8,128)(2,1)}, bf16[208,1024]{1,0:T(8,128)(2,1)}, u32[]{:S(2)}, u32[]{:S(2)}) collective-permute-start(bf16[208,1024]{1,0:T(8,128)(2,1)} %collective-permute-done.3.up_2), channel_id=1, source_target_pairs={{6,0},{0,2},{2,4},{4,6},{7,1},{1,3},{3,5},{5,7},{14,8},{8,10},{10,... | collective-permute-start | bytes 1277960 | tf_op jit(solution)/shard_map/ppermute | solution.py:14
  74.5 21.2 %collective-permute-start.5 = (bf16[512,1024]{1,0:T(8,128)(2,1)S(1)}, bf16[512,1024]{1,0:T(8,128)(2,1)S(1)}, u32[]{:S(2)}, u32[]{:S(2)}) collective-permute-start(bf16[512,1024]{1,0:T(8,128)(2,1)S(1)} %bitcast.9), channel_id=1, source_target_pairs={{2,0},{7,1},{4,2},{1,3},{6,4},{3,5},{0,6},{5,7},{10,8},{15,9},{12,... | collective-permute-start | bytes 3145736 | tf_op jit(solution)/shard_map/ppermute | solution.py:24
  83.6 12.1 %collective-permute-start.8 = (bf16[512,1024]{1,0:T(8,128)(2,1)S(1)}, bf16[512,1024]{1,0:T(8,128)(2,1)S(1)}, u32[]{:S(2)}, u32[]{:S(2)}) collective-permute-start(bf16[512,1024]{1,0:T(8,128)(2,1)S(1)} %get-tuple-element.22), channel_id=1, source_target_pairs={{1,0},{0,1},{3,2},{2,3},{5,4},{4,5},{7,6},{6,7},{9,8},{8,9},{11,10... | collective-permute-start | bytes 3145736 | tf_op jit(solution)/shard_map/ppermute | solution.py:28
  93.1 4.5 %collective-permute-start.9 = (bf16[512,1024]{1,0:T(8,128)(2,1)S(1)}, bf16[512,1024]{1,0:T(8,128)(2,1)S(1)}, u32[]{:S(2)}, u32[]{:S(2)}) collective-permute-start(bf16[512,1024]{1,0:T(8,128)(2,1)S(1)} %get-tuple-element.23), channel_id=1, source_target_pairs={{0,1},{2,3},{4,5},{6,7},{8,9},{10,11},{12,13},{14,15},{16,17},{18,... | collective-permute-start | bytes 3145736 | tf_op jit(solution)/shard_map/ppermute | solution.py:28
  94.4 9.0 %collective-permute-start.11 = (bf16[512,1024]{1,0:T(8,128)(2,1)S(1)}, bf16[512,1024]{1,0:T(8,128)(2,1)S(1)}, u32[]{:S(2)}, u32[]{:S(2)}) collective-permute-start(bf16[512,1024]{1,0:T(8,128)(2,1)S(1)} %bitcast.10), channel_id=1, source_target_pairs={{1,0},{0,1},{3,2},{2,3},{5,4},{4,5},{7,6},{6,7},{9,8},{8,9},{11,10... | collective-permute-start | bytes 3145736 | tf_op jit(solution)/shard_map/ppermute | solution.py:28
  97.7 5.7 %collective-permute-start.12 = (bf16[512,1024]{1,0:T(8,128)(2,1)S(1)}, bf16[512,1024]{1,0:T(8,128)(2,1)S(1)}, u32[]{:S(2)}, u32[]{:S(2)}) collective-permute-start(bf16[512,1024]{1,0:T(8,128)(2,1)S(1)} %collective-permute-done.5.first), channel_id=1, source_target_pairs={{1,0},{0,1},{3,2},{2,3},{5,4},{4,5},{7,6},{6,7},{9,8},{8,9},{11,10... | collective-permute-start | bytes 3145736 | tf_op jit(solution)/shard_map/ppermute | solution.py:28
  97.8 13.9 %collective-permute-start.10 = (bf16[512,1024]{1,0:T(8,128)(2,1)S(1)}, bf16[512,1024]{1,0:T(8,128)(2,1)S(1)}, u32[]{:S(2)}, u32[]{:S(2)}) collective-permute-start(bf16[512,1024]{1,0:T(8,128)(2,1)S(1)} %bitcast.11), channel_id=1, source_target_pairs={{6,0},{3,1},{0,2},{5,3},{2,4},{7,5},{4,6},{1,7},{14,8},{11,9},{8,1... | collective-permute-start | bytes 3145736 | tf_op jit(solution)/shard_map/ppermute | solution.py:24

commit v7 on v3

--- a/solution.py
+++ b/solution.py
@@ -80,34 +80,43 @@
         put(1, times(quadrature(lower), own[...]))
 
 
+def join_kernel(place, down_1, up_3, down_2, up_2, ahead, beyond, sems):
+    first, second = pl.ds(0, down_1.shape[0]), pl.ds(down_1.shape[0], up_3.shape[0])
+    copies = [
+        pltpu.make_async_copy(down_1, ahead.at[first], sems.at[0]),
+        pltpu.make_async_copy(up_3, ahead.at[second], sems.at[1]),
+        pltpu.make_async_copy(down_2, beyond.at[first], sems.at[2]),
+        pltpu.make_async_copy(up_2, beyond.at[second], sems.at[3]),
+    ]
+    for copy in copies:
+        copy.start()
+    for copy in copies:
+        copy.wait()
+
+
 def early_kernel(
-    place, own_at, down_1, up_3, down_2, up_2, sib_own, sib_down_1, sib_up_3, sib_down_2, sib_up_2,
-    band, far, swapped, own, ahead, beyond, sib_ahead, other, sems,
+    place, own_at, ahead_at, beyond_at, sib_own, sib_ahead_at, sib_beyond, band, far,
+    swapped, own, ahead, beyond, sib_ahead, other, sems,
 ):
     core, upper = place[0], place[1]
-    first, second = pl.ds(0, down_1.shape[0]), pl.ds(down_1.shape[0], up_3.shape[0])
 
     def load(number, source, target):
         return pltpu.make_async_copy(source, target, sems.at[number])
 
-    own_load = load(0, own_at, own)
-    ahead_loads = [load(1, down_1, ahead.at[first]), load(2, up_3, ahead.at[second])]
-    beyond_loads = [load(3, down_2, beyond.at[first]), load(4, up_2, beyond.at[second])]
-    sib_loads = [load(5, sib_down_1, sib_ahead.at[first]), load(6, sib_up_3, sib_ahead.at[second])]
-    near_load = load(7, sib_own, other)
-    far_loads = [load(7, sib_down_2, other.at[first]), load(8, sib_up_2, other.at[second])]
-
-    for copy in (own_load, *ahead_loads, *beyond_loads, *sib_loads):
+    loads = [
+        load(0, own_at, own), load(1, ahead_at, ahead), load(2, beyond_at, beyond),
+        load(3, sib_ahead_at, sib_ahead),
+    ]
+    for copy in loads:
         copy.start()
 
     @pl.when(core == 0)
     def _():
-        near_load.start()
+        load(4, sib_own, other).start()
 
     @pl.when(core != 0)
     def _():
-        for copy in far_loads:
-            copy.start()
+        load(4, sib_beyond, other).start()
 
     def tile(slot, columns):
         for part, left in enumerate((own, swapped)):
@@ -116,28 +125,16 @@
     def put(part, product):
         far[0, part, 0] = product
 
-    own_load.wait()
+    loads[0].wait()
     swapped[...] = quadrature(own[...])
     tile(0, own)
-    for copy in ahead_loads:
-        copy.wait()
+    loads[1].wait()
     tile(2, ahead)
-    for copy in beyond_loads:
-        copy.wait()
+    loads[2].wait()
     far_tile(upper, own, swapped, beyond, put)
-    for copy in sib_loads:
-        copy.wait()
+    loads[3].wait()
     tile(3 - 2 * core, sib_ahead)
-
-    @pl.when(core == 0)
-    def _():
-        near_load.wait()
-
-    @pl.when(core != 0)
-    def _():
-        for copy in far_loads:
-            copy.wait()
-
+    load(4, sib_own, other).wait()
     tile(1 + 2 * core, other)
 
 
@@ -160,8 +157,9 @@
 
     def tile(slot, columns):
         product = times(left[...], columns[...])
-        band[0, 0, 0, 0] = product[:rows] + band_in[0, 0, 0, slot]
-        band[0, 1, 0, 0] = product[rows:] + band_in[0, 1, 0, slot]
+        for part in range(2):
+            here = product[part * rows : (part + 1) * rows]
+            band[0, part, 0, 0] = here + band_in[0, part, 0, slot]
 
     @pl.when(step == 0)
     def _():
@@ -252,31 +250,31 @@
     down_2 = from_ahead(down_1, 1)
     up_3 = from_ahead(up_2, -1)
     sib_own = from_sibling(own, (0,))
-    sib_down_1 = from_sibling(down_1)
-    sib_up_2 = from_sibling(up_2, (1,))
-    late_ahead, down_1, up_2, sib_own, sib_down_1, sib_up_2 = lax.optimization_barrier(
-        (late_ahead, down_1, up_2, sib_own, sib_down_1, sib_up_2)
+    late_ahead, down_1, up_2, sib_own = lax.optimization_barrier(
+        (late_ahead, down_1, up_2, sib_own)
     )
     late_first = from_both_sides(late_ahead, 0)
-    late_sib_ahead = from_sibling(late_ahead)
-
-    sib_up_3 = from_sibling(up_3)
-    sib_down_2 = from_sibling(down_2, (1,))
 
     rows = own.shape[0]
     block = pltpu.VMEM(own.shape, own.dtype)
     band_shape, far_shape = (1, 2, 1, 4, rows, rows), (1, 2, 1, rows // 2, rows)
-    band_sum, far_sum = call(
-        early_kernel, (1,), place,
-        (own, down_1, up_3, down_2, up_2, sib_own, sib_down_1, sib_up_3, sib_down_2, sib_up_2), (),
-        [pltpu.VMEM(band_shape, jnp.float32), pltpu.VMEM(far_shape, jnp.float32)],
-        [IN_VMEM, IN_VMEM], {}, 2, [block] * 6 + [pltpu.SemaphoreType.DMA((9,))],
-    )
-    late_ahead, late_sib_ahead, late_first, band_sum, far_sum = lax.optimization_barrier(
-        (late_ahead, late_sib_ahead, late_first, band_sum, far_sum)
+    ahead, beyond = call(
+        join_kernel, (1,), place, (down_1, up_3, down_2, up_2), (), [block, block],
+        [IN_VMEM] * 2, {}, 4, [pltpu.SemaphoreType.DMA((4,))],
+    )
+    sib_ahead = from_sibling(ahead)
+    sib_beyond = from_sibling(beyond, (1,))
+    late_sib_ahead = from_sibling(late_ahead)
+    late_ahead, late_first, ahead, beyond = lax.optimization_barrier(
+        (late_ahead, late_first, ahead, beyond)
     )
     late_second = from_both_sides(late_ahead, 1)
     late_sib_first = from_sibling(late_first)
+    band_sum, far_sum = call(
+        early_kernel, (1,), place, (own, ahead, beyond, sib_own, sib_ahead, sib_beyond), (),
+        [pltpu.VMEM(band_shape, jnp.float32), pltpu.VMEM(far_shape, jnp.float32)],
+        [IN_VMEM] * 2, {}, 2, [block] * 6 + [pltpu.SemaphoreType.DMA((5,))],
+    )
     band_out = jax.ShapeDtypeStruct(band_shape, jnp.float32)
     far_out = jax.ShapeDtypeStruct(far_shape, jnp.float32)
     band, far = call(

time: 124 us -> 119 us (0.960)
  waiting for transfers between devices: 49.5 us -> 44.6 us
  starting transfers between devices: 53.3 us -> 51.6 us
  Pallas kernels: 20.1 us -> 21.5 us
    ppermute x7 -> x5, starting transfers between devices: 23.1 us -> 16.8 us  [from_sibling(): return lax.ppermute(block, 'acol', [(1 - core, core) for core in cores])]
    ppermute x7 -> x5, waiting for transfers between devices: 5.92 us -> 0.01 us  [from_sibling(): return lax.ppermute(block, 'acol', [(1 - core, core) for core in cores])]
    ppermute x2, waiting for transfers between devices: 11.4 us -> 5.86 us  [from_both_sides(): return lax.ppermute(block, ('arow', 'acol'), route)]
    ppermute x6, waiting for transfers between devices: 31.4 us -> 35.1 us  [from_ahead(): lax.ppermute(block, 'arow', [((i + distance) % size, i) for i in range(si...]
    all_to_all x2, waiting for transfers between devices: 0.8 us -> 3.55 us  [turn(): lax.all_to_all(block, 'chan', split_axis=0, concat_axis=0, tiled=True)]
    ppermute x2, starting transfers between devices: 1.5 us -> 4.17 us  [from_both_sides(): return lax.ppermute(block, ('arow', 'acol'), route)]
    ppermute x6, starting transfers between devices: 7.86 us -> 9.84 us  [from_ahead(): lax.ppermute(block, 'arow', [((i + distance) % size, i) for i in range(si...]
    pallas_call x2 -> x3, Pallas kernels: 16 us -> 17.4 us  [call(): pl.pallas_call(kernel, out_shape=outs, grid_spec=pltpu.PrefetchScalarGrid...]
  transfers between devices with their start and end apart: 17 -> 15, of which waited for: 10 -> 9; matrix products, arithmetic and copies ran while one was open for 0% -> 0% of each run, Pallas kernels for 7% -> 9%
where the time goes in v7:
time: 119 us
  starting transfers between devices  51.6 us (43%)
  waiting for transfers between devices  44.6 us (37%)
  Pallas kernels  21.5 us (18%)
    ppermute x6, waiting for transfers between devices, from_ahead(): lax.ppermute(block, 'arow', [((i + distance) % size, i) for i in range(si...  35.1 us
    all_to_all x2, starting transfers between devices, turn(): lax.all_to_all(block, 'chan', split_axis=0, concat_axis=0, tiled=True)  20.8 us
    pallas_call x3, Pallas kernels, call(): pl.pallas_call(kernel, out_shape=outs, grid_spec=pltpu.PrefetchScalarGrid...  17.4 us
    ppermute x5, starting transfers between devices, from_sibling(): return lax.ppermute(block, 'acol', [(1 - core, core) for core in cores])  16.8 us
    ppermute x6, starting transfers between devices, from_ahead(): lax.ppermute(block, 'arow', [((i + distance) % size, i) for i in range(si...  9.84 us
    ppermute x2, waiting for transfers between devices, from_both_sides(): return lax.ppermute(block, ('arow', 'acol'), route)  5.86 us
    ppermute x2, starting transfers between devices, from_both_sides(): return lax.ppermute(block, ('arow', 'acol'), route)  4.17 us
    pallas_call x2, Pallas kernels, half_of(): pl.pallas_call(cut_kernel, out_shape=jax.ShapeDtypeStruct((channels, rows...  4.1 us
  transfers between devices with their start and end apart: 15, of which 9 were waited for; matrix products, arithmetic and copies ran while one was open for 0% of the time, Pallas kernels for 9%

profile of v7, /device:TPU:1, one launch (start us, length us, event | category | flops | bytes accessed | tf_op | source)
XLA Modules:
  0.0 118.7 jit_solution(12636845759644463553)
XLA Ops:
  0.6 2.1 %shard_map.30 = bf16[32,16,1024]{2,1,0:T(8,128)(2,1)} custom-call(bf16[32,1,16,2048]{3,2,1,0:T(8,128)(2,1)} %imaginary.3, bf16[32,1,16,2048]{3,2,1,0:T(8,128)(2,1)} %imaginary.3), custom_call_target="tpu_custom_call" | custom-call | tf_op jit(solution)/shard_map/pallas_call | solution.py:45
  2.7 11.9 %all-to-all-start = ((bf16[32,16,1024]{2,1,0:T(8,128)(2,1)}), bf16[32,16,1024]{2,1,0:T(8,128)(2,1)S(1)}, u32[]{:S(2)}, u32[]{:S(2)}) async-start(bf16[32,16,1024]{2,1,0:T(8,128)(2,1)} %shard_map.30), calls=%async_computation | async-start | bytes 2097152 | tf_op jit(solution)/shard_map/all_to_all | solution.py:32
  14.6 2.1 %shard_map.31 = bf16[32,16,1024]{2,1,0:T(8,128)(2,1)} custom-call(bf16[32,1,16,2048]{3,2,1,0:T(8,128)(2,1)} %imaginary.3, bf16[32,1,16,2048]{3,2,1,0:T(8,128)(2,1)} %imaginary.3), custom_call_target="tpu_custom_call" | custom-call | tf_op jit(solution)/shard_map/pallas_call | solution.py:45
  16.6 2.7 %collective-permute-start = (bf16[32,16,1024]{2,1,0:T(8,128)(2,1)}, bf16[32,16,1024]{2,1,0:T(8,128)(2,1)}, u32[]{:S(2)}, u32[]{:S(2)}) collective-permute-start(bf16[32,16,1024]{2,1,0:T(8,128)(2,1)} %shard_map.31), channel_id=1, source_target_pairs={{2,0},{4,2},{6,4},{0,6},{3,1},{5,3},{7,5},{1,7},{10,8},{12,10},{14... | collective-permute-start | bytes 3145736 | tf_op jit(solution)/shard_map/ppermute | solution.py:14
  19.3 21.8 %collective-permute-done = bf16[32,16,1024]{2,1,0:T(8,128)(2,1)} collective-permute-done((bf16[32,16,1024]{2,1,0:T(8,128)(2,1)}, bf16[32,16,1024]{2,1,0:T(8,128)(2,1)}, u32[]{:S(2)}, u32[]{:S(2)}) %collective-permute-start) | collective-permute-done | bytes 1048608 | tf_op jit(solution)/shard_map/ppermute | solution.py:14
  41.2 0.0 all-to-all-done
  41.2 8.9 %all-to-all-start.1 = ((bf16[32,16,1024]{2,1,0:T(8,128)(2,1)}), bf16[32,16,1024]{2,1,0:T(8,128)(2,1)S(1)}, u32[]{:S(2)}, u32[]{:S(2)}) async-start(bf16[32,16,1024]{2,1,0:T(8,128)(2,1)} %collective-permute-done), calls=%async_computation.1 | async-start | bytes 2097152 | tf_op jit(solution)/shard_map/all_to_all | solution.py:32
  50.1 0.8 collective-permute-start.2
  51.0 2.7 %collective-permute-start.1 = (bf16[304,1024]{1,0:T(8,128)(2,1)S(1)}, bf16[304,1024]{1,0:T(8,128)(2,1)}, u32[]{:S(2)}, u32[]{:S(2)}) collective-permute-start(bf16[304,1024]{1,0:T(8,128)(2,1)S(1)} %bitcast.12), channel_id=1, source_target_pairs={{2,0},{4,2},{6,4},{0,6},{3,1},{5,3},{7,5},{1,7},{10,8},{12,10},{14... | collective-permute-start | bytes 1867784 | tf_op jit(solution)/shard_map/ppermute | solution.py:14
  53.8 4.7 %collective-permute-start.4 = (bf16[512,1024]{1,0:T(8,128)(2,1)S(1)}, bf16[512,1024]{1,0:T(8,128)(2,1)S(1)}, u32[]{:S(2)}, u32[]{:S(2)}) collective-permute-start(bf16[512,1024]{1,0:T(8,128)(2,1)S(1)} %bitcast.6), channel_id=1, source_target_pairs={{1,0},{3,2},{5,4},{7,6},{9,8},{11,10},{13,12},{15,14},{17,16},{19,... | collective-permute-start | bytes 3145736 | tf_op jit(solution)/shard_map/ppermute | solution.py:28
  58.5 2.9 %collective-permute-done.2 = bf16[208,1024]{1,0:T(8,128)(2,1)S(1)} collective-permute-done((bf16[208,1024]{1,0:T(8,128)(2,1)S(1)}, bf16[208,1024]{1,0:T(8,128)(2,1)S(1)}, u32[]{:S(2)}, u32[]{:S(2)}) %collective-permute-start.2) | collective-permute-done | bytes 426016 | tf_op jit(solution)/shard_map/ppermute | solution.py:14
  61.3 0.0 collective-permute-start.3
  61.3 3.3 %collective-permute-done.1.down_1 = bf16[304,1024]{1,0:T(8,128)(2,1)} collective-permute-done((bf16[304,1024]{1,0:T(8,128)(2,1)S(1)}, bf16[304,1024]{1,0:T(8,128)(2,1)}, u32[]{:S(2)}, u32[]{:S(2)}) %collective-permute-start.1) | collective-permute-done | bytes 622624 | tf_op jit(solution)/shard_map/ppermute | solution.py:14
  64.7 3.5 %collective-permute-start.7 = (bf16[304,1024]{1,0:T(8,128)(2,1)}, bf16[304,1024]{1,0:T(8,128)(2,1)}, u32[]{:S(2)}, u32[]{:S(2)}) collective-permute-start(bf16[304,1024]{1,0:T(8,128)(2,1)} %collective-permute-done.1.down_1), channel_id=1, source_target_pairs={{2,0},{4,2},{6,4},{0,6},{3,1},{5,3},{7,5},{1,7},{10,8},{12,10},{14... | collective-permute-start | bytes 1867784 | tf_op jit(solution)/shard_map/ppermute | solution.py:14
  68.2 2.7 %collective-permute-done.3.up_2 = bf16[208,1024]{1,0:T(8,128)(2,1)} collective-permute-done((bf16[208,1024]{1,0:T(8,128)(2,1)S(1)}, bf16[208,1024]{1,0:T(8,128)(2,1)}, u32[]{:S(2)}, u32[]{:S(2)}) %collective-permute-start.3) | collective-permute-done | bytes 426016 | tf_op jit(solution)/shard_map/ppermute | solution.py:14
  70.9 0.0 collective-permute-start.6
  70.9 0.1 pad_add_fusion.place
  70.9 3.5 %all-to-all-done.1 = bf16[32,16,1024]{2,1,0:T(8,128)(2,1)S(1)} async-done(((bf16[32,16,1024]{2,1,0:T(8,128)(2,1)}), bf16[32,16,1024]{2,1,0:T(8,128)(2,1)S(1)}, u32[]{:S(2)}, u32[]{:S(2)}) %all-to-all-start.1) | async-done | bytes 1048608 | tf_op jit(solution)/shard_map/all_to_all | solution.py:32
  74.5 0.8 collective-permute-start.5
  75.2 3.2 %collective-permute-done.7.down_2 = bf16[304,1024]{1,0:T(8,128)(2,1)} collective-permute-done((bf16[304,1024]{1,0:T(8,128)(2,1)}, bf16[304,1024]{1,0:T(8,128)(2,1)}, u32[]{:S(2)}, u32[]{:S(2)}) %collective-permute-start.7) | collective-permute-done | bytes 622624 | tf_op jit(solution)/shard_map/ppermute | solution.py:14
  78.4 1.2 %collective-permute-done.6.up_3 = bf16[208,1024]{1,0:T(8,128)(2,1)} collective-permute-done((bf16[208,1024]{1,0:T(8,128)(2,1)}, bf16[208,1024]{1,0:T(8,128)(2,1)}, u32[]{:S(2)}, u32[]{:S(2)}) %collective-permute-start.6) | collective-permute-done | bytes 426016 | tf_op jit(solution)/shard_map/ppermute | solution.py:14
  79.7 2.1 %shard_map.32 = (bf16[512,1024]{1,0:T(8,128)(2,1)S(1)}, bf16[512,1024]{1,0:T(8,128)(2,1)S(1)}) custom-call(s32[2]{0:T(128)S(1)} %pad_add_fusion.place, bf16[304,1024]{1,0:T(8,128)(2,1)} %collective-permute-done.1.down_1, bf16[208,1024]{1,0:T(8,128)(2,1)} %collective-permute-done.6.up_3, bf16[304,1024]{1,0:T(8,128)(2,1)} %collective-permute-done.7.down_2, ...), custom_call_target="tpu_custom_call" | custom-call | flops 17179869184 | bytes 33554432 | tf_op jit(solution)/shard_map/pallas_call | solution.py:216
  81.8 9.5 %collective-permute-start.8 = (bf16[512,1024]{1,0:T(8,128)(2,1)S(1)}, bf16[512,1024]{1,0:T(8,128)(2,1)S(1)}, u32[]{:S(2)}, u32[]{:S(2)}) collective-permute-start(bf16[512,1024]{1,0:T(8,128)(2,1)S(1)} %get-tuple-element.19.ahead_at), channel_id=1, source_target_pairs={{1,0},{0,1},{3,2},{2,3},{5,4},{4,5},{7,6},{6,7},{9,8},{8,9},{11,10... | collective-permute-start | bytes 3145736 | tf_op jit(solution)/shard_map/ppermute | solution.py:28
  91.3 1.3 %collective-permute-start.9 = (bf16[512,1024]{1,0:T(8,128)(2,1)S(1)}, bf16[512,1024]{1,0:T(8,128)(2,1)S(1)}, u32[]{:S(2)}, u32[]{:S(2)}) collective-permute-start(bf16[512,1024]{1,0:T(8,128)(2,1)S(1)} %get-tuple-element.20.beyond_at), channel_id=1, source_target_pairs={{0,1},{2,3},{4,5},{6,7},{8,9},{10,11},{12,13},{14,15},{16,17},{18,... | collective-permute-start | bytes 3145736 | tf_op jit(solution)/shard_map/ppermute | solution.py:28
  92.6 1.3 %collective-permute-start.11 = (bf16[512,1024]{1,0:T(8,128)(2,1)S(1)}, bf16[512,1024]{1,0:T(8,128)(2,1)S(1)}, u32[]{:S(2)}, u32[]{:S(2)}) collective-permute-start(bf16[512,1024]{1,0:T(8,128)(2,1)S(1)} %bitcast.9), channel_id=1, source_target_pairs={{1,0},{0,1},{3,2},{2,3},{5,4},{4,5},{7,6},{6,7},{9,8},{8,9},{11,10... | collective-permute-start | bytes 3145736 | tf_op jit(solution)/shard_map/ppermute | solution.py:28
  93.9 1.2 collective-permute-done.5.first
  95.1 0.0 collective-permute-start.12
  95.1 3.4 %collective-permute-start.10 = (bf16[512,1024]{1,0:T(8,128)(2,1)S(1)}, bf16[512,1024]{1,0:T(8,128)(2,1)S(1)}, u32[]{:S(2)}, u32[]{:S(2)}) collective-permute-start(bf16[512,1024]{1,0:T(8,128)(2,1)S(1)} %bitcast.10), channel_id=1, source_target_pairs={{6,0},{3,1},{0,2},{5,3},{2,4},{7,5},{4,6},{1,7},{14,8},{11,9},{8,1... | collective-permute-start | bytes 3145736 | tf_op jit(solution)/shard_map/ppermute | solution.py:24
  98.5 7.0 %shard_map.33 = (f32[1,2,1,4,512,512]{5,4,3,2,1,0:T(8,128)S(1)}, f32[1,2,1,256,512]{4,3,2,1,0:T(8,128)S(1)}) custom-call(s32[2]{0:T(128)S(1)} %pad_add_fusion.place, bf16[512,1024]{1,0:T(8,128)(2,1)S(1)} %bitcast.7, bf16[512,1024]{1,0:T(8,128)(2,1)S(1)} %get-tuple-element.19.ahead_at, bf16[512,1024]{1,0:T(8,128)(2,1)S(1)} %get-tuple-element.20.beyond_at, ...), custom_call_target="tpu_custom_call" | custom-call | flops 2147483648 | bytes 4194304 | tf_op jit(solution)/shard_map/pallas_call | solution.py:216
  105.5 0.0 collective-permute-done.11.sib_ahead_at
  105.6 4.7 %collective-permute-done.10.second = bf16[512,1024]{1,0:T(8,128)(2,1)S(1)} collective-permute-done((bf16[512,1024]{1,0:T(8,128)(2,1)S(1)}, bf16[512,1024]{1,0:T(8,128)(2,1)S(1)}, u32[]{:S(2)}, u32[]{:S(2)}) %collective-permute-start.10) | collective-permute-done | bytes 1048608 | tf_op jit(solution)/shard_map/ppermute | solution.py:24
  110.3 8.3 %shard_map.34 = (f32[1,2,1,4,512,512]{5,4,3,2,1,0:T(8,128)}, f32[1,2,1,256,512]{4,3,2,1,0:T(8,128)}) custom-call(s32[2]{0:T(128)S(1)} %pad_add_fusion.place, f32[1,2,1,4,512,512]{5,4,3,2,1,0:T(8,128)S(1)} %get-tuple-element.22.band_in, f32[1,2,1,256,512]{4,3,2,1,0:T(8,128)S(1)} %get-tuple-element.23.far_in, ...), custom_call_target="tpu_custom_call" | custom-call | flops 5368709120 | bytes 10485760 | tf_op jit(solution)/shard_map/pallas_call | solution.py:216
  (6 shorter events, 0.1 us)
Async XLA Ops:
  2.7 38.5 %all-to-all-start = ((bf16[32,16,1024]{2,1,0:T(8,128)(2,1)}), bf16[32,16,1024]{2,1,0:T(8,128)(2,1)S(1)}, u32[]{:S(2)}, u32[]{:S(2)}) async-start(bf16[32,16,1024]{2,1,0:T(8,128)(2,1)} %shard_map.30), calls=%async_computation | async-start | bytes 2097152 | tf_op jit(solution)/shard_map/all_to_all | solution.py:32
  16.6 24.6 %collective-permute-start = (bf16[32,16,1024]{2,1,0:T(8,128)(2,1)}, bf16[32,16,1024]{2,1,0:T(8,128)(2,1)}, u32[]{:S(2)}, u32[]{:S(2)}) collective-permute-start(bf16[32,16,1024]{2,1,0:T(8,128)(2,1)} %shard_map.31), channel_id=1, source_target_pairs={{2,0},{4,2},{6,4},{0,6},{3,1},{5,3},{7,5},{1,7},{10,8},{12,10},{14... | collective-permute-start | bytes 3145736 | tf_op jit(solution)/shard_map/ppermute | solution.py:14
  41.2 33.3 %all-to-all-start.1 = ((bf16[32,16,1024]{2,1,0:T(8,128)(2,1)}), bf16[32,16,1024]{2,1,0:T(8,128)(2,1)S(1)}, u32[]{:S(2)}, u32[]{:S(2)}) async-start(bf16[32,16,1024]{2,1,0:T(8,128)(2,1)} %collective-permute-done), calls=%async_computation.1 | async-start | bytes 2097152 | tf_op jit(solution)/shard_map/all_to_all | solution.py:32
  50.1 11.2 %collective-permute-start.2 = (bf16[208,1024]{1,0:T(8,128)(2,1)S(1)}, bf16[208,1024]{1,0:T(8,128)(2,1)S(1)}, u32[]{:S(2)}, u32[]{:S(2)}) collective-permute-start(bf16[208,1024]{1,0:T(8,128)(2,1)S(1)} %bitcast.13), channel_id=1, source_target_pairs={{6,0},{0,2},{2,4},{4,6},{7,1},{1,3},{3,5},{5,7},{14,8},{8,10},{10,... | collective-permute-start | bytes 1277960 | tf_op jit(solution)/shard_map/ppermute | solution.py:14
  51.0 13.6 %collective-permute-start.1 = (bf16[304,1024]{1,0:T(8,128)(2,1)S(1)}, bf16[304,1024]{1,0:T(8,128)(2,1)}, u32[]{:S(2)}, u32[]{:S(2)}) collective-permute-start(bf16[304,1024]{1,0:T(8,128)(2,1)S(1)} %bitcast.12), channel_id=1, source_target_pairs={{2,0},{4,2},{6,4},{0,6},{3,1},{5,3},{7,5},{1,7},{10,8},{12,10},{14... | collective-permute-start | bytes 1867784 | tf_op jit(solution)/shard_map/ppermute | solution.py:14
  53.8 17.2 %collective-permute-start.4 = (bf16[512,1024]{1,0:T(8,128)(2,1)S(1)}, bf16[512,1024]{1,0:T(8,128)(2,1)S(1)}, u32[]{:S(2)}, u32[]{:S(2)}) collective-permute-start(bf16[512,1024]{1,0:T(8,128)(2,1)S(1)} %bitcast.6), channel_id=1, source_target_pairs={{1,0},{3,2},{5,4},{7,6},{9,8},{11,10},{13,12},{15,14},{17,16},{19,... | collective-permute-start | bytes 3145736 | tf_op jit(solution)/shard_map/ppermute | solution.py:28
  61.3 9.5 %collective-permute-start.3 = (bf16[208,1024]{1,0:T(8,128)(2,1)S(1)}, bf16[208,1024]{1,0:T(8,128)(2,1)}, u32[]{:S(2)}, u32[]{:S(2)}) collective-permute-start(bf16[208,1024]{1,0:T(8,128)(2,1)S(1)} %collective-permute-done.2), channel_id=1, source_target_pairs={{6,0},{0,2},{2,4},{4,6},{7,1},{1,3},{3,5},{5,7},{14,8},{8,10},{10,... | collective-permute-start | bytes 1277960 | tf_op jit(solution)/shard_map/ppermute | solution.py:14
  64.7 13.8 %collective-permute-start.7 = (bf16[304,1024]{1,0:T(8,128)(2,1)}, bf16[304,1024]{1,0:T(8,128)(2,1)}, u32[]{:S(2)}, u32[]{:S(2)}) collective-permute-start(bf16[304,1024]{1,0:T(8,128)(2,1)} %collective-permute-done.1.down_1), channel_id=1, source_target_pairs={{2,0},{4,2},{6,4},{0,6},{3,1},{5,3},{7,5},{1,7},{10,8},{12,10},{14... | collective-permute-start | bytes 1867784 | tf_op jit(solution)/shard_map/ppermute | solution.py:14
  70.9 8.8 %collective-permute-start.6 = (bf16[208,1024]{1,0:T(8,128)(2,1)}, bf16[208,1024]{1,0:T(8,128)(2,1)}, u32[]{:S(2)}, u32[]{:S(2)}) collective-permute-start(bf16[208,1024]{1,0:T(8,128)(2,1)} %collective-permute-done.3.up_2), channel_id=1, source_target_pairs={{6,0},{0,2},{2,4},{4,6},{7,1},{1,3},{3,5},{5,7},{14,8},{8,10},{10,... | collective-permute-start | bytes 1277960 | tf_op jit(solution)/shard_map/ppermute | solution.py:14
  74.5 20.6 %collective-permute-start.5 = (bf16[512,1024]{1,0:T(8,128)(2,1)S(1)}, bf16[512,1024]{1,0:T(8,128)(2,1)S(1)}, u32[]{:S(2)}, u32[]{:S(2)}) collective-permute-start(bf16[512,1024]{1,0:T(8,128)(2,1)S(1)} %bitcast.8), channel_id=1, source_target_pairs={{2,0},{7,1},{4,2},{1,3},{6,4},{3,5},{0,6},{5,7},{10,8},{15,9},{12,... | collective-permute-start | bytes 3145736 | tf_op jit(solution)/shard_map/ppermute | solution.py:24
  81.8 16.7 %collective-permute-start.8 = (bf16[512,1024]{1,0:T(8,128)(2,1)S(1)}, bf16[512,1024]{1,0:T(8,128)(2,1)S(1)}, u32[]{:S(2)}, u32[]{:S(2)}) collective-permute-start(bf16[512,1024]{1,0:T(8,128)(2,1)S(1)} %get-tuple-element.19.ahead_at), channel_id=1, source_target_pairs={{1,0},{0,1},{3,2},{2,3},{5,4},{4,5},{7,6},{6,7},{9,8},{8,9},{11,10... | collective-permute-start | bytes 3145736 | tf_op jit(solution)/shard_map/ppermute | solution.py:28
  91.3 7.2 %collective-permute-start.9 = (bf16[512,1024]{1,0:T(8,128)(2,1)S(1)}, bf16[512,1024]{1,0:T(8,128)(2,1)S(1)}, u32[]{:S(2)}, u32[]{:S(2)}) collective-permute-start(bf16[512,1024]{1,0:T(8,128)(2,1)S(1)} %get-tuple-element.20.beyond_at), channel_id=1, source_target_pairs={{0,1},{2,3},{4,5},{6,7},{8,9},{10,11},{12,13},{14,15},{16,17},{18,... | collective-permute-start | bytes 3145736 | tf_op jit(solution)/shard_map/ppermute | solution.py:28
  92.6 12.9 %collective-permute-start.11 = (bf16[512,1024]{1,0:T(8,128)(2,1)S(1)}, bf16[512,1024]{1,0:T(8,128)(2,1)S(1)}, u32[]{:S(2)}, u32[]{:S(2)}) collective-permute-start(bf16[512,1024]{1,0:T(8,128)(2,1)S(1)} %bitcast.9), channel_id=1, source_target_pairs={{1,0},{0,1},{3,2},{2,3},{5,4},{4,5},{7,6},{6,7},{9,8},{8,9},{11,10... | collective-permute-start | bytes 3145736 | tf_op jit(solution)/shard_map/ppermute | solution.py:28
  95.1 10.5 %collective-permute-start.12 = (bf16[512,1024]{1,0:T(8,128)(2,1)S(1)}, bf16[512,1024]{1,0:T(8,128)(2,1)S(1)}, u32[]{:S(2)}, u32[]{:S(2)}) collective-permute-start(bf16[512,1024]{1,0:T(8,128)(2,1)S(1)} %collective-permute-done.5.first), channel_id=1, source_target_pairs={{1,0},{0,1},{3,2},{2,3},{5,4},{4,5},{7,6},{6,7},{9,8},{8,9},{11,10... | collective-permute-start | bytes 3145736 | tf_op jit(solution)/shard_map/ppermute | solution.py:28
  95.1 15.2 %collective-permute-start.10 = (bf16[512,1024]{1,0:T(8,128)(2,1)S(1)}, bf16[512,1024]{1,0:T(8,128)(2,1)S(1)}, u32[]{:S(2)}, u32[]{:S(2)}) collective-permute-start(bf16[512,1024]{1,0:T(8,128)(2,1)S(1)} %bitcast.10), channel_id=1, source_target_pairs={{6,0},{3,1},{0,2},{5,3},{2,4},{7,5},{4,6},{1,7},{14,8},{11,9},{8,1... | collective-permute-start | bytes 3145736 | tf_op jit(solution)/shard_map/ppermute | solution.py:24

commit v8 on v7

--- a/solution.py
+++ b/solution.py
@@ -5,7 +5,7 @@
 from jax.experimental.pallas import tpu as pltpu
 from jax.sharding import PartitionSpec as P
 
-DOWN_ROWS = 304
+DOWN_ROWS = 320
 VMEM_BYTES = 28 * 1024 * 1024
 
 
@@ -250,9 +250,7 @@
     down_2 = from_ahead(down_1, 1)
     up_3 = from_ahead(up_2, -1)
     sib_own = from_sibling(own, (0,))
-    late_ahead, down_1, up_2, sib_own = lax.optimization_barrier(
-        (late_ahead, down_1, up_2, sib_own)
-    )
+    late_ahead, down_1, up_2 = lax.optimization_barrier((late_ahead, down_1, up_2))
     late_first = from_both_sides(late_ahead, 0)
 
     rows = own.shape[0]
@@ -265,8 +263,8 @@
     sib_ahead = from_sibling(ahead)
     sib_beyond = from_sibling(beyond, (1,))
     late_sib_ahead = from_sibling(late_ahead)
-    late_ahead, late_first, ahead, beyond = lax.optimization_barrier(
-        (late_ahead, late_first, ahead, beyond)
+    late_ahead, late_first, ahead, beyond, sib_own = lax.optimization_barrier(
+        (late_ahead, late_first, ahead, beyond, sib_own)
     )
     late_second = from_both_sides(late_ahead, 1)
     late_sib_first = from_sibling(late_first)

time: 119 us -> 119 us (level)
    all_to_all x2, waiting for transfers between devices: 3.55 us -> 0.01 us  [turn(): lax.all_to_all(block, 'chan', split_axis=0, concat_axis=0, tiled=True)]
    ppermute x2, waiting for transfers between devices: 5.86 us -> 8.3 us  [from_both_sides(): return lax.ppermute(block, ('arow', 'acol'), route)]
    ppermute x6, waiting for transfers between devices: 35.1 us -> 37.4 us  [from_ahead(): lax.ppermute(block, 'arow', [((i + distance) % size, i) for i in range(si...]
  transfers between devices with their start and end apart: 15 -> 15, of which waited for: 9 -> 8; matrix products, arithmetic and copies ran while one was open for 0% -> 0% of each run, Pallas kernels for 9% -> 9%
where the time goes in v8:
time: 119 us
  starting transfers between devices  50.6 us (43%)
  waiting for transfers between devices  45.7 us (38%)
  Pallas kernels  21.4 us (18%)
    ppermute x6, waiting for transfers between devices, from_ahead(): lax.ppermute(block, 'arow', [((i + distance) % size, i) for i in range(si...  37.4 us
    all_to_all x2, starting transfers between devices, turn(): lax.all_to_all(block, 'chan', split_axis=0, concat_axis=0, tiled=True)  20.8 us
    pallas_call x3, Pallas kernels, call(): pl.pallas_call(kernel, out_shape=outs, grid_spec=pltpu.PrefetchScalarGrid...  17.3 us
    ppermute x5, starting transfers between devices, from_sibling(): return lax.ppermute(block, 'acol', [(1 - core, core) for core in cores])  16.7 us
    ppermute x6, starting transfers between devices, from_ahead(): lax.ppermute(block, 'arow', [((i + distance) % size, i) for i in range(si...  9.83 us
    ppermute x2, waiting for transfers between devices, from_both_sides(): return lax.ppermute(block, ('arow', 'acol'), route)  8.3 us
    pallas_call x2, Pallas kernels, half_of(): pl.pallas_call(cut_kernel, out_shape=jax.ShapeDtypeStruct((channels, rows...  4.1 us
    ppermute x2, starting transfers between devices, from_both_sides(): return lax.ppermute(block, ('arow', 'acol'), route)  3.32 us
  transfers between devices with their start and end apart: 15, of which 8 were waited for; matrix products, arithmetic and copies ran while one was open for 0% of the time, Pallas kernels for 9%

profile of v8, /device:TPU:1, one launch (start us, length us, event | category | flops | bytes accessed | tf_op | source)
XLA Modules:
  0.0 118.8 jit_solution(16528469448047955374)
XLA Ops:
  0.6 2.1 %shard_map.30 = bf16[32,16,1024]{2,1,0:T(8,128)(2,1)} custom-call(bf16[32,1,16,2048]{3,2,1,0:T(8,128)(2,1)} %imaginary.3, bf16[32,1,16,2048]{3,2,1,0:T(8,128)(2,1)} %imaginary.3), custom_call_target="tpu_custom_call" | custom-call | tf_op jit(solution)/shard_map/pallas_call | solution.py:45
  2.7 11.9 %all-to-all-start = ((bf16[32,16,1024]{2,1,0:T(8,128)(2,1)}), bf16[32,16,1024]{2,1,0:T(8,128)(2,1)S(1)}, u32[]{:S(2)}, u32[]{:S(2)}) async-start(bf16[32,16,1024]{2,1,0:T(8,128)(2,1)} %shard_map.30), calls=%async_computation | async-start | bytes 2097152 | tf_op jit(solution)/shard_map/all_to_all | solution.py:32
  14.6 2.1 %shard_map.31 = bf16[32,16,1024]{2,1,0:T(8,128)(2,1)} custom-call(bf16[32,1,16,2048]{3,2,1,0:T(8,128)(2,1)} %imaginary.3, bf16[32,1,16,2048]{3,2,1,0:T(8,128)(2,1)} %imaginary.3), custom_call_target="tpu_custom_call" | custom-call | tf_op jit(solution)/shard_map/pallas_call | solution.py:45
  16.6 2.7 %collective-permute-start = (bf16[32,16,1024]{2,1,0:T(8,128)(2,1)}, bf16[32,16,1024]{2,1,0:T(8,128)(2,1)}, u32[]{:S(2)}, u32[]{:S(2)}) collective-permute-start(bf16[32,16,1024]{2,1,0:T(8,128)(2,1)} %shard_map.31), channel_id=1, source_target_pairs={{2,0},{4,2},{6,4},{0,6},{3,1},{5,3},{7,5},{1,7},{10,8},{12,10},{14... | collective-permute-start | bytes 3145736 | tf_op jit(solution)/shard_map/ppermute | solution.py:14
  19.3 21.8 %collective-permute-done = bf16[32,16,1024]{2,1,0:T(8,128)(2,1)} collective-permute-done((bf16[32,16,1024]{2,1,0:T(8,128)(2,1)}, bf16[32,16,1024]{2,1,0:T(8,128)(2,1)}, u32[]{:S(2)}, u32[]{:S(2)}) %collective-permute-start) | collective-permute-done | bytes 1048608 | tf_op jit(solution)/shard_map/ppermute | solution.py:14
  41.2 0.0 all-to-all-done
  41.2 8.9 %all-to-all-start.1 = ((bf16[32,16,1024]{2,1,0:T(8,128)(2,1)}), bf16[32,16,1024]{2,1,0:T(8,128)(2,1)S(1)}, u32[]{:S(2)}, u32[]{:S(2)}) async-start(bf16[32,16,1024]{2,1,0:T(8,128)(2,1)} %collective-permute-done), calls=%async_computation.1 | async-start | bytes 2097152 | tf_op jit(solution)/shard_map/all_to_all | solution.py:32
  50.1 0.1 slice.16
  50.2 3.5 %collective-permute-start.1 = (bf16[320,1024]{1,0:T(8,128)(2,1)S(1)}, bf16[320,1024]{1,0:T(8,128)(2,1)}, u32[]{:S(2)}, u32[]{:S(2)}) collective-permute-start(bf16[320,1024]{1,0:T(8,128)(2,1)S(1)} %bitcast.12), channel_id=1, source_target_pairs={{2,0},{4,2},{6,4},{0,6},{3,1},{5,3},{7,5},{1,7},{10,8},{12,10},{14... | collective-permute-start | bytes 1966088 | tf_op jit(solution)/shard_map/ppermute | solution.py:14
  53.7 0.1 collective-permute-start.2
  53.8 9.1 %collective-permute-done.2 = bf16[192,1024]{1,0:T(8,128)(2,1)S(1)} collective-permute-done((bf16[192,1024]{1,0:T(8,128)(2,1)S(1)}, bf16[192,1024]{1,0:T(8,128)(2,1)S(1)}, u32[]{:S(2)}, u32[]{:S(2)}) %collective-permute-start.2) | collective-permute-done | bytes 393248 | tf_op jit(solution)/shard_map/ppermute | solution.py:14
  62.9 2.4 %collective-permute-done.1.down_1 = bf16[320,1024]{1,0:T(8,128)(2,1)} collective-permute-done((bf16[320,1024]{1,0:T(8,128)(2,1)S(1)}, bf16[320,1024]{1,0:T(8,128)(2,1)}, u32[]{:S(2)}, u32[]{:S(2)}) %collective-permute-start.1) | collective-permute-done | bytes 655392 | tf_op jit(solution)/shard_map/ppermute | solution.py:14
  65.2 3.5 %collective-permute-start.6 = (bf16[320,1024]{1,0:T(8,128)(2,1)}, bf16[320,1024]{1,0:T(8,128)(2,1)}, u32[]{:S(2)}, u32[]{:S(2)}) collective-permute-start(bf16[320,1024]{1,0:T(8,128)(2,1)} %collective-permute-done.1.down_1), channel_id=1, source_target_pairs={{2,0},{4,2},{6,4},{0,6},{3,1},{5,3},{7,5},{1,7},{10,8},{12,10},{14... | collective-permute-start | bytes 1966088 | tf_op jit(solution)/shard_map/ppermute | solution.py:14
  68.7 2.3 %collective-permute-done.3.up_2 = bf16[192,1024]{1,0:T(8,128)(2,1)S(1)} collective-permute-done((bf16[192,1024]{1,0:T(8,128)(2,1)S(1)}, bf16[192,1024]{1,0:T(8,128)(2,1)S(1)}, u32[]{:S(2)}, u32[]{:S(2)}) %collective-permute-start.3) | collective-permute-done | bytes 393248 | tf_op jit(solution)/shard_map/ppermute | solution.py:14
  71.0 0.1 pad_add_fusion.place
  71.1 6.7 %collective-permute-start.7 = (bf16[512,1024]{1,0:T(8,128)(2,1)S(1)}, bf16[512,1024]{1,0:T(8,128)(2,1)S(1)}, u32[]{:S(2)}, u32[]{:S(2)}) collective-permute-start(bf16[512,1024]{1,0:T(8,128)(2,1)S(1)} %bitcast.6), channel_id=1, source_target_pairs={{1,0},{3,2},{5,4},{7,6},{9,8},{11,10},{13,12},{15,14},{17,16},{19,... | collective-permute-start | bytes 3145736 | tf_op jit(solution)/shard_map/ppermute | solution.py:28
  77.8 0.0 all-to-all-done.1
  77.8 0.1 collective-permute-start.4
  77.9 1.3 %collective-permute-done.5.up_3 = bf16[192,1024]{1,0:T(8,128)(2,1)} collective-permute-done((bf16[192,1024]{1,0:T(8,128)(2,1)S(1)}, bf16[192,1024]{1,0:T(8,128)(2,1)}, u32[]{:S(2)}, u32[]{:S(2)}) %collective-permute-start.5) | collective-permute-done | bytes 393248 | tf_op jit(solution)/shard_map/ppermute | solution.py:14
  79.2 0.5 collective-permute-done.6.down_2
  79.7 2.0 %shard_map.32 = (bf16[512,1024]{1,0:T(8,128)(2,1)S(1)}, bf16[512,1024]{1,0:T(8,128)(2,1)S(1)}) custom-call(s32[2]{0:T(128)S(1)} %pad_add_fusion.place, bf16[320,1024]{1,0:T(8,128)(2,1)} %collective-permute-done.1.down_1, bf16[192,1024]{1,0:T(8,128)(2,1)} %collective-permute-done.5.up_3, bf16[320,1024]{1,0:T(8,128)(2,1)} %collective-permute-done.6.down_2, ...), custom_call_target="tpu_custom_call" | custom-call | flops 17179869184 | bytes 33554432 | tf_op jit(solution)/shard_map/pallas_call | solution.py:216
  81.7 7.4 %collective-permute-start.8 = (bf16[512,1024]{1,0:T(8,128)(2,1)S(1)}, bf16[512,1024]{1,0:T(8,128)(2,1)S(1)}, u32[]{:S(2)}, u32[]{:S(2)}) collective-permute-start(bf16[512,1024]{1,0:T(8,128)(2,1)S(1)} %get-tuple-element.19.ahead_at), channel_id=1, source_target_pairs={{1,0},{0,1},{3,2},{2,3},{5,4},{4,5},{7,6},{6,7},{9,8},{8,9},{11,10... | collective-permute-start | bytes 3145736 | tf_op jit(solution)/shard_map/ppermute | solution.py:28
  89.1 1.3 %collective-permute-start.9 = (bf16[512,1024]{1,0:T(8,128)(2,1)S(1)}, bf16[512,1024]{1,0:T(8,128)(2,1)S(1)}, u32[]{:S(2)}, u32[]{:S(2)}) collective-permute-start(bf16[512,1024]{1,0:T(8,128)(2,1)S(1)} %get-tuple-element.20.beyond_at), channel_id=1, source_target_pairs={{0,1},{2,3},{4,5},{6,7},{8,9},{10,11},{12,13},{14,15},{16,17},{18,... | collective-permute-start | bytes 3145736 | tf_op jit(solution)/shard_map/ppermute | solution.py:28
  90.4 1.3 %collective-permute-start.11 = (bf16[512,1024]{1,0:T(8,128)(2,1)S(1)}, bf16[512,1024]{1,0:T(8,128)(2,1)S(1)}, u32[]{:S(2)}, u32[]{:S(2)}) collective-permute-start(bf16[512,1024]{1,0:T(8,128)(2,1)S(1)} %bitcast.9), channel_id=1, source_target_pairs={{1,0},{0,1},{3,2},{2,3},{5,4},{4,5},{7,6},{6,7},{9,8},{8,9},{11,10... | collective-permute-start | bytes 3145736 | tf_op jit(solution)/shard_map/ppermute | solution.py:28
  91.7 3.6 %collective-permute-done.4.first = bf16[512,1024]{1,0:T(8,128)(2,1)S(1)} collective-permute-done((bf16[512,1024]{1,0:T(8,128)(2,1)S(1)}, bf16[512,1024]{1,0:T(8,128)(2,1)S(1)}, u32[]{:S(2)}, u32[]{:S(2)}) %collective-permute-start.4) | collective-permute-done | bytes 1048608 | tf_op jit(solution)/shard_map/ppermute | solution.py:24
  95.3 0.0 collective-permute-start.12
  95.3 3.2 %collective-permute-start.10 = (bf16[512,1024]{1,0:T(8,128)(2,1)S(1)}, bf16[512,1024]{1,0:T(8,128)(2,1)S(1)}, u32[]{:S(2)}, u32[]{:S(2)}) collective-permute-start(bf16[512,1024]{1,0:T(8,128)(2,1)S(1)} %bitcast.10), channel_id=1, source_target_pairs={{6,0},{3,1},{0,2},{5,3},{2,4},{7,5},{4,6},{1,7},{14,8},{11,9},{8,1... | collective-permute-start | bytes 3145736 | tf_op jit(solution)/shard_map/ppermute | solution.py:24
  98.6 7.0 %shard_map.33 = (f32[1,2,1,4,512,512]{5,4,3,2,1,0:T(8,128)S(1)}, f32[1,2,1,256,512]{4,3,2,1,0:T(8,128)S(1)}) custom-call(s32[2]{0:T(128)S(1)} %pad_add_fusion.place, bf16[512,1024]{1,0:T(8,128)(2,1)S(1)} %bitcast.7, bf16[512,1024]{1,0:T(8,128)(2,1)S(1)} %get-tuple-element.19.ahead_at, bf16[512,1024]{1,0:T(8,128)(2,1)S(1)} %get-tuple-element.20.beyond_at, ...), custom_call_target="tpu_custom_call" | custom-call | flops 2147483648 | bytes 4194304 | tf_op jit(solution)/shard_map/pallas_call | solution.py:216
  105.6 0.0 collective-permute-done.11.sib_ahead_at
  105.6 0.0 collective-permute-done.12.sib_first
  105.6 4.7 %collective-permute-done.10.second = bf16[512,1024]{1,0:T(8,128)(2,1)S(1)} collective-permute-done((bf16[512,1024]{1,0:T(8,128)(2,1)S(1)}, bf16[512,1024]{1,0:T(8,128)(2,1)S(1)}, u32[]{:S(2)}, u32[]{:S(2)}) %collective-permute-start.10) | collective-permute-done | bytes 1048608 | tf_op jit(solution)/shard_map/ppermute | solution.py:24
  110.3 8.3 %shard_map.34 = (f32[1,2,1,4,512,512]{5,4,3,2,1,0:T(8,128)}, f32[1,2,1,256,512]{4,3,2,1,0:T(8,128)}) custom-call(s32[2]{0:T(128)S(1)} %pad_add_fusion.place, f32[1,2,1,4,512,512]{5,4,3,2,1,0:T(8,128)S(1)} %get-tuple-element.22.band_in, f32[1,2,1,256,512]{4,3,2,1,0:T(8,128)S(1)} %get-tuple-element.23.far_in, ...), custom_call_target="tpu_custom_call" | custom-call | flops 5368709120 | bytes 10485760 | tf_op jit(solution)/shard_map/pallas_call | solution.py:216
  (6 shorter events, 0.0 us)
Async XLA Ops:
  2.7 38.5 %all-to-all-start = ((bf16[32,16,1024]{2,1,0:T(8,128)(2,1)}), bf16[32,16,1024]{2,1,0:T(8,128)(2,1)S(1)}, u32[]{:S(2)}, u32[]{:S(2)}) async-start(bf16[32,16,1024]{2,1,0:T(8,128)(2,1)} %shard_map.30), calls=%async_computation | async-start | bytes 2097152 | tf_op jit(solution)/shard_map/all_to_all | solution.py:32
  16.6 24.6 %collective-permute-start = (bf16[32,16,1024]{2,1,0:T(8,128)(2,1)}, bf16[32,16,1024]{2,1,0:T(8,128)(2,1)}, u32[]{:S(2)}, u32[]{:S(2)}) collective-permute-start(bf16[32,16,1024]{2,1,0:T(8,128)(2,1)} %shard_map.31), channel_id=1, source_target_pairs={{2,0},{4,2},{6,4},{0,6},{3,1},{5,3},{7,5},{1,7},{10,8},{12,10},{14... | collective-permute-start | bytes 3145736 | tf_op jit(solution)/shard_map/ppermute | solution.py:14
  41.2 36.7 %all-to-all-start.1 = ((bf16[32,16,1024]{2,1,0:T(8,128)(2,1)}), bf16[32,16,1024]{2,1,0:T(8,128)(2,1)S(1)}, u32[]{:S(2)}, u32[]{:S(2)}) async-start(bf16[32,16,1024]{2,1,0:T(8,128)(2,1)} %collective-permute-done), calls=%async_computation.1 | async-start | bytes 2097152 | tf_op jit(solution)/shard_map/all_to_all | solution.py:32
  50.2 15.1 %collective-permute-start.1 = (bf16[320,1024]{1,0:T(8,128)(2,1)S(1)}, bf16[320,1024]{1,0:T(8,128)(2,1)}, u32[]{:S(2)}, u32[]{:S(2)}) collective-permute-start(bf16[320,1024]{1,0:T(8,128)(2,1)S(1)} %bitcast.12), channel_id=1, source_target_pairs={{2,0},{4,2},{6,4},{0,6},{3,1},{5,3},{7,5},{1,7},{10,8},{12,10},{14... | collective-permute-start | bytes 1966088 | tf_op jit(solution)/shard_map/ppermute | solution.py:14
  53.7 9.2 %collective-permute-start.2 = (bf16[192,1024]{1,0:T(8,128)(2,1)S(1)}, bf16[192,1024]{1,0:T(8,128)(2,1)S(1)}, u32[]{:S(2)}, u32[]{:S(2)}) collective-permute-start(bf16[192,1024]{1,0:T(8,128)(2,1)S(1)} %bitcast.13), channel_id=1, source_target_pairs={{6,0},{0,2},{2,4},{4,6},{7,1},{1,3},{3,5},{5,7},{14,8},{8,10},{10,... | collective-permute-start | bytes 1179656 | tf_op jit(solution)/shard_map/ppermute | solution.py:14
  62.9 8.2 %collective-permute-start.3 = (bf16[192,1024]{1,0:T(8,128)(2,1)S(1)}, bf16[192,1024]{1,0:T(8,128)(2,1)S(1)}, u32[]{:S(2)}, u32[]{:S(2)}) collective-permute-start(bf16[192,1024]{1,0:T(8,128)(2,1)S(1)} %collective-permute-done.2), channel_id=1, source_target_pairs={{6,0},{0,2},{2,4},{4,6},{7,1},{1,3},{3,5},{5,7},{14,8},{8,10},{10,... | collective-permute-start | bytes 1179656 | tf_op jit(solution)/shard_map/ppermute | solution.py:14
  65.2 14.5 %collective-permute-start.6 = (bf16[320,1024]{1,0:T(8,128)(2,1)}, bf16[320,1024]{1,0:T(8,128)(2,1)}, u32[]{:S(2)}, u32[]{:S(2)}) collective-permute-start(bf16[320,1024]{1,0:T(8,128)(2,1)} %collective-permute-done.1.down_1), channel_id=1, source_target_pairs={{2,0},{4,2},{6,4},{0,6},{3,1},{5,3},{7,5},{1,7},{10,8},{12,10},{14... | collective-permute-start | bytes 1966088 | tf_op jit(solution)/shard_map/ppermute | solution.py:14
  71.0 8.2 %collective-permute-start.5 = (bf16[192,1024]{1,0:T(8,128)(2,1)S(1)}, bf16[192,1024]{1,0:T(8,128)(2,1)}, u32[]{:S(2)}, u32[]{:S(2)}) collective-permute-start(bf16[192,1024]{1,0:T(8,128)(2,1)S(1)} %collective-permute-done.3.up_2), channel_id=1, source_target_pairs={{6,0},{0,2},{2,4},{4,6},{7,1},{1,3},{3,5},{5,7},{14,8},{8,10},{10,... | collective-permute-start | bytes 1179656 | tf_op jit(solution)/shard_map/ppermute | solution.py:14
  71.1 20.6 %collective-permute-start.7 = (bf16[512,1024]{1,0:T(8,128)(2,1)S(1)}, bf16[512,1024]{1,0:T(8,128)(2,1)S(1)}, u32[]{:S(2)}, u32[]{:S(2)}) collective-permute-start(bf16[512,1024]{1,0:T(8,128)(2,1)S(1)} %bitcast.6), channel_id=1, source_target_pairs={{1,0},{3,2},{5,4},{7,6},{9,8},{11,10},{13,12},{15,14},{17,16},{19,... | collective-permute-start | bytes 3145736 | tf_op jit(solution)/shard_map/ppermute | solution.py:28
  77.8 17.5 %collective-permute-start.4 = (bf16[512,1024]{1,0:T(8,128)(2,1)S(1)}, bf16[512,1024]{1,0:T(8,128)(2,1)S(1)}, u32[]{:S(2)}, u32[]{:S(2)}) collective-permute-start(bf16[512,1024]{1,0:T(8,128)(2,1)S(1)} %bitcast.8), channel_id=1, source_target_pairs={{2,0},{7,1},{4,2},{1,3},{6,4},{3,5},{0,6},{5,7},{10,8},{15,9},{12,... | collective-permute-start | bytes 3145736 | tf_op jit(solution)/shard_map/ppermute | solution.py:24
  81.7 16.8 %collective-permute-start.8 = (bf16[512,1024]{1,0:T(8,128)(2,1)S(1)}, bf16[512,1024]{1,0:T(8,128)(2,1)S(1)}, u32[]{:S(2)}, u32[]{:S(2)}) collective-permute-start(bf16[512,1024]{1,0:T(8,128)(2,1)S(1)} %get-tuple-element.19.ahead_at), channel_id=1, source_target_pairs={{1,0},{0,1},{3,2},{2,3},{5,4},{4,5},{7,6},{6,7},{9,8},{8,9},{11,10... | collective-permute-start | bytes 3145736 | tf_op jit(solution)/shard_map/ppermute | solution.py:28
  89.1 9.4 %collective-permute-start.9 = (bf16[512,1024]{1,0:T(8,128)(2,1)S(1)}, bf16[512,1024]{1,0:T(8,128)(2,1)S(1)}, u32[]{:S(2)}, u32[]{:S(2)}) collective-permute-start(bf16[512,1024]{1,0:T(8,128)(2,1)S(1)} %get-tuple-element.20.beyond_at), channel_id=1, source_target_pairs={{0,1},{2,3},{4,5},{6,7},{8,9},{10,11},{12,13},{14,15},{16,17},{18,... | collective-permute-start | bytes 3145736 | tf_op jit(solution)/shard_map/ppermute | solution.py:28
  90.4 15.2 %collective-permute-start.11 = (bf16[512,1024]{1,0:T(8,128)(2,1)S(1)}, bf16[512,1024]{1,0:T(8,128)(2,1)S(1)}, u32[]{:S(2)}, u32[]{:S(2)}) collective-permute-start(bf16[512,1024]{1,0:T(8,128)(2,1)S(1)} %bitcast.9), channel_id=1, source_target_pairs={{1,0},{0,1},{3,2},{2,3},{5,4},{4,5},{7,6},{6,7},{9,8},{8,9},{11,10... | collective-permute-start | bytes 3145736 | tf_op jit(solution)/shard_map/ppermute | solution.py:28
  95.3 10.3 %collective-permute-start.12 = (bf16[512,1024]{1,0:T(8,128)(2,1)S(1)}, bf16[512,1024]{1,0:T(8,128)(2,1)S(1)}, u32[]{:S(2)}, u32[]{:S(2)}) collective-permute-start(bf16[512,1024]{1,0:T(8,128)(2,1)S(1)} %collective-permute-done.4.first), channel_id=1, source_target_pairs={{1,0},{0,1},{3,2},{2,3},{5,4},{4,5},{7,6},{6,7},{9,8},{8,9},{11,10... | collective-permute-start | bytes 3145736 | tf_op jit(solution)/shard_map/ppermute | solution.py:28
  95.3 15.0 %collective-permute-start.10 = (bf16[512,1024]{1,0:T(8,128)(2,1)S(1)}, bf16[512,1024]{1,0:T(8,128)(2,1)S(1)}, u32[]{:S(2)}, u32[]{:S(2)}) collective-permute-start(bf16[512,1024]{1,0:T(8,128)(2,1)S(1)} %bitcast.10), channel_id=1, source_target_pairs={{6,0},{3,1},{0,2},{5,3},{2,4},{7,5},{4,6},{1,7},{14,8},{11,9},{8,1... | collective-permute-start | bytes 3145736 | tf_op jit(solution)/shard_map/ppermute | solution.py:24

commit v9 on v8

--- a/solution.py
+++ b/solution.py
@@ -139,8 +139,8 @@
 
 
 def late_kernel(
-    place, band_in, far_in, first, second, ahead_at, sib_ahead_at, sib_first, band, far_at, left,
-    ahead, beyond, sib_ahead, other, far, sems,
+    place, band_in, far_in, first, second, ahead_at, sib_ahead_at, sib_upper, sib_lower, band, far_at,
+    left, ahead, beyond, sib_ahead, other, far, sems,
 ):
     core, upper = place[0], place[1]
     step = pl.program_id(0)
@@ -151,7 +151,9 @@
         return pltpu.make_async_copy(source, target, sems.at[number])
 
     loads = [
-        load(2, ahead_at, ahead), load(3, sib_ahead_at, sib_ahead), load(4, sib_first, other)
+        load(2, ahead_at, ahead), load(3, sib_ahead_at, sib_ahead),
+        load(4, sib_upper, other.at[pl.ds(0, rows // 2)]),
+        load(6, sib_lower, other.at[pl.ds(rows // 2, rows // 2)]),
     ]
     store = pltpu.make_async_copy(far, far_at.at[0, :, 0], sems.at[5])
 
@@ -199,6 +201,7 @@
     @pl.when(step == 3)
     def _():
         loads[2].wait()
+        loads[3].wait()
         tile(1 + 2 * core, other)
         store.wait()
 
@@ -263,11 +266,12 @@
     sib_ahead = from_sibling(ahead)
     sib_beyond = from_sibling(beyond, (1,))
     late_sib_ahead = from_sibling(late_ahead)
-    late_ahead, late_first, ahead, beyond, sib_own = lax.optimization_barrier(
-        (late_ahead, late_first, ahead, beyond, sib_own)
+    late_ahead, ahead, beyond, sib_own = lax.optimization_barrier(
+        (late_ahead, ahead, beyond, sib_own)
     )
     late_second = from_both_sides(late_ahead, 1)
-    late_sib_first = from_sibling(late_first)
+    half = rows // 2
+    late_sib_first = [from_sibling(late_first[:half]), from_sibling(late_first[half:])]
     band_sum, far_sum = call(
         early_kernel, (1,), place, (own, ahead, beyond, sib_own, sib_ahead, sib_beyond), (),
         [pltpu.VMEM(band_shape, jnp.float32), pltpu.VMEM(far_shape, jnp.float32)],
@@ -277,7 +281,7 @@
     far_out = jax.ShapeDtypeStruct(far_shape, jnp.float32)
     band, far = call(
         late_kernel, (4,), place,
-        (late_first, late_second, late_ahead, late_sib_ahead, late_sib_first),
+        (late_first, late_second, late_ahead, late_sib_ahead, *late_sib_first),
         (band_sum, far_sum), [band_out, far_out],
         [
             pl.BlockSpec(
@@ -294,7 +298,7 @@
         ],
         {}, 5,
         [pltpu.VMEM((2 * rows, late_ahead.shape[1]), late_ahead.dtype)] + [block] * 4
-        + [pltpu.VMEM((2, rows // 2, rows), jnp.float32), pltpu.SemaphoreType.DMA((6,))],
+        + [pltpu.VMEM((2, rows // 2, rows), jnp.float32), pltpu.SemaphoreType.DMA((7,))],
     )
     return band, far
 

time: 119 us -> 115 us (0.966)
  waiting for transfers between devices: 45.7 us -> 42.1 us
    ppermute x2, waiting for transfers between devices: 8.3 us -> 4.67 us  [from_both_sides(): return lax.ppermute(block, ('arow', 'acol'), route)]
    ppermute x2, starting transfers between devices: 3.32 us -> 0.44 us  [from_both_sides(): return lax.ppermute(block, ('arow', 'acol'), route)]
    ppermute x5 -> x6, starting transfers between devices: 16.7 us -> 18.8 us  [from_sibling(): return lax.ppermute(block, 'acol', [(1 - core, core) for core in cores])]
  transfers between devices with their start and end apart: 15 -> 16, of which waited for: 8 -> 8; matrix products, arithmetic and copies ran while one was open for 0% -> 0% of each run, Pallas kernels for 9% -> 10%
where the time goes in v9:
time: 115 us; the launch traced here: 114 us
  starting transfers between devices  49.9 us (43%)
  waiting for transfers between devices  42.1 us (37%)
  Pallas kernels  21.4 us (19%)
    ppermute x6, waiting for transfers between devices, from_ahead(): lax.ppermute(block, 'arow', [((i + distance) % size, i) for i in range(si...  37.4 us
    all_to_all x2, starting transfers between devices, turn(): lax.all_to_all(block, 'chan', split_axis=0, concat_axis=0, tiled=True)  20.8 us
    ppermute x6, starting transfers between devices, from_sibling(): return lax.ppermute(block, 'acol', [(1 - core, core) for core in cores])  18.8 us
    pallas_call x3, Pallas kernels, call(): pl.pallas_call(kernel, out_shape=outs, grid_spec=pltpu.PrefetchScalarGrid...  17.3 us
    ppermute x6, starting transfers between devices, from_ahead(): lax.ppermute(block, 'arow', [((i + distance) % size, i) for i in range(si...  9.83 us
    ppermute x2, waiting for transfers between devices, from_both_sides(): return lax.ppermute(block, ('arow', 'acol'), route)  4.67 us
    pallas_call x2, Pallas kernels, half_of(): pl.pallas_call(cut_kernel, out_shape=jax.ShapeDtypeStruct((channels, rows...  4.1 us
  transfers between devices with their start and end apart: 16, of which 8 were waited for; matrix products, arithmetic and copies ran while one was open for 0% of the time, Pallas kernels for 10%

profile of v9, /device:TPU:1, one launch (start us, length us, event | category | flops | bytes accessed | tf_op | source)
XLA Modules:
  0.0 114.5 jit_solution(3265180580006949151)
XLA Ops:
  0.6 2.1 %shard_map.30 = bf16[32,16,1024]{2,1,0:T(8,128)(2,1)} custom-call(bf16[32,1,16,2048]{3,2,1,0:T(8,128)(2,1)} %imaginary.3, bf16[32,1,16,2048]{3,2,1,0:T(8,128)(2,1)} %imaginary.3), custom_call_target="tpu_custom_call" | custom-call | tf_op jit(solution)/shard_map/pallas_call | solution.py:45
  2.7 11.9 %all-to-all-start = ((bf16[32,16,1024]{2,1,0:T(8,128)(2,1)}), bf16[32,16,1024]{2,1,0:T(8,128)(2,1)S(1)}, u32[]{:S(2)}, u32[]{:S(2)}) async-start(bf16[32,16,1024]{2,1,0:T(8,128)(2,1)} %shard_map.30), calls=%async_computation | async-start | bytes 2097152 | tf_op jit(solution)/shard_map/all_to_all | solution.py:32
  14.6 2.1 %shard_map.31 = bf16[32,16,1024]{2,1,0:T(8,128)(2,1)} custom-call(bf16[32,1,16,2048]{3,2,1,0:T(8,128)(2,1)} %imaginary.3, bf16[32,1,16,2048]{3,2,1,0:T(8,128)(2,1)} %imaginary.3), custom_call_target="tpu_custom_call" | custom-call | tf_op jit(solution)/shard_map/pallas_call | solution.py:45
  16.6 2.7 %collective-permute-start = (bf16[32,16,1024]{2,1,0:T(8,128)(2,1)}, bf16[32,16,1024]{2,1,0:T(8,128)(2,1)}, u32[]{:S(2)}, u32[]{:S(2)}) collective-permute-start(bf16[32,16,1024]{2,1,0:T(8,128)(2,1)} %shard_map.31), channel_id=1, source_target_pairs={{2,0},{4,2},{6,4},{0,6},{3,1},{5,3},{7,5},{1,7},{10,8},{12,10},{14... | collective-permute-start | bytes 3145736 | tf_op jit(solution)/shard_map/ppermute | solution.py:14
  19.3 21.8 %collective-permute-done = bf16[32,16,1024]{2,1,0:T(8,128)(2,1)} collective-permute-done((bf16[32,16,1024]{2,1,0:T(8,128)(2,1)}, bf16[32,16,1024]{2,1,0:T(8,128)(2,1)}, u32[]{:S(2)}, u32[]{:S(2)}) %collective-permute-start) | collective-permute-done | bytes 1048608 | tf_op jit(solution)/shard_map/ppermute | solution.py:14
  41.2 8.9 %all-to-all-start.1 = ((bf16[32,16,1024]{2,1,0:T(8,128)(2,1)}), bf16[32,16,1024]{2,1,0:T(8,128)(2,1)S(1)}, u32[]{:S(2)}, u32[]{:S(2)}) async-start(bf16[32,16,1024]{2,1,0:T(8,128)(2,1)} %collective-permute-done), calls=%async_computation.1 | async-start | bytes 2097152 | tf_op jit(solution)/shard_map/all_to_all | solution.py:32
  50.1 0.1 slice.24
  50.2 3.5 %collective-permute-start.1 = (bf16[320,1024]{1,0:T(8,128)(2,1)S(1)}, bf16[320,1024]{1,0:T(8,128)(2,1)}, u32[]{:S(2)}, u32[]{:S(2)}) collective-permute-start(bf16[320,1024]{1,0:T(8,128)(2,1)S(1)} %bitcast.12), channel_id=1, source_target_pairs={{2,0},{4,2},{6,4},{0,6},{3,1},{5,3},{7,5},{1,7},{10,8},{12,10},{14... | collective-permute-start | bytes 1966088 | tf_op jit(solution)/shard_map/ppermute | solution.py:14
  53.7 0.1 collective-permute-start.2
  53.8 9.1 %collective-permute-done.2 = bf16[192,1024]{1,0:T(8,128)(2,1)S(1)} collective-permute-done((bf16[192,1024]{1,0:T(8,128)(2,1)S(1)}, bf16[192,1024]{1,0:T(8,128)(2,1)S(1)}, u32[]{:S(2)}, u32[]{:S(2)}) %collective-permute-start.2) | collective-permute-done | bytes 393248 | tf_op jit(solution)/shard_map/ppermute | solution.py:14
  62.9 2.4 %collective-permute-done.1.down_1 = bf16[320,1024]{1,0:T(8,128)(2,1)} collective-permute-done((bf16[320,1024]{1,0:T(8,128)(2,1)S(1)}, bf16[320,1024]{1,0:T(8,128)(2,1)}, u32[]{:S(2)}, u32[]{:S(2)}) %collective-permute-start.1) | collective-permute-done | bytes 655392 | tf_op jit(solution)/shard_map/ppermute | solution.py:14
  65.2 3.5 %collective-permute-start.5 = (bf16[320,1024]{1,0:T(8,128)(2,1)}, bf16[320,1024]{1,0:T(8,128)(2,1)}, u32[]{:S(2)}, u32[]{:S(2)}) collective-permute-start(bf16[320,1024]{1,0:T(8,128)(2,1)} %collective-permute-done.1.down_1), channel_id=1, source_target_pairs={{2,0},{4,2},{6,4},{0,6},{3,1},{5,3},{7,5},{1,7},{10,8},{12,10},{14... | collective-permute-start | bytes 1966088 | tf_op jit(solution)/shard_map/ppermute | solution.py:14
  68.7 2.3 %collective-permute-done.3.up_2 = bf16[192,1024]{1,0:T(8,128)(2,1)S(1)} collective-permute-done((bf16[192,1024]{1,0:T(8,128)(2,1)S(1)}, bf16[192,1024]{1,0:T(8,128)(2,1)S(1)}, u32[]{:S(2)}, u32[]{:S(2)}) %collective-permute-start.3) | collective-permute-done | bytes 393248 | tf_op jit(solution)/shard_map/ppermute | solution.py:14
  71.0 0.0 collective-permute-start.4
  71.0 0.1 pad_add_fusion.place
  71.1 6.7 %collective-permute-start.6 = (bf16[512,1024]{1,0:T(8,128)(2,1)S(1)}, bf16[512,1024]{1,0:T(8,128)(2,1)S(1)}, u32[]{:S(2)}, u32[]{:S(2)}) collective-permute-start(bf16[512,1024]{1,0:T(8,128)(2,1)S(1)} %bitcast.6), channel_id=1, source_target_pairs={{1,0},{3,2},{5,4},{7,6},{9,8},{11,10},{13,12},{15,14},{17,16},{19,... | collective-permute-start | bytes 3145736 | tf_op jit(solution)/shard_map/ppermute | solution.py:28
  77.8 0.1 collective-permute-start.9
  77.9 1.3 %collective-permute-done.4.up_3 = bf16[192,1024]{1,0:T(8,128)(2,1)} collective-permute-done((bf16[192,1024]{1,0:T(8,128)(2,1)S(1)}, bf16[192,1024]{1,0:T(8,128)(2,1)}, u32[]{:S(2)}, u32[]{:S(2)}) %collective-permute-start.4) | collective-permute-done | bytes 393248 | tf_op jit(solution)/shard_map/ppermute | solution.py:14
  79.2 0.5 collective-permute-done.5.down_2
  79.7 2.0 %shard_map.32 = (bf16[512,1024]{1,0:T(8,128)(2,1)S(1)}, bf16[512,1024]{1,0:T(8,128)(2,1)S(1)}) custom-call(s32[2]{0:T(128)S(1)} %pad_add_fusion.place, bf16[320,1024]{1,0:T(8,128)(2,1)} %collective-permute-done.1.down_1, bf16[192,1024]{1,0:T(8,128)(2,1)} %collective-permute-done.4.up_3, bf16[320,1024]{1,0:T(8,128)(2,1)} %collective-permute-done.5.down_2, ...), custom_call_target="tpu_custom_call" | custom-call | flops 17179869184 | bytes 33554432 | tf_op jit(solution)/shard_map/pallas_call | solution.py:219
  81.7 7.4 %collective-permute-start.7 = (bf16[512,1024]{1,0:T(8,128)(2,1)S(1)}, bf16[512,1024]{1,0:T(8,128)(2,1)S(1)}, u32[]{:S(2)}, u32[]{:S(2)}) collective-permute-start(bf16[512,1024]{1,0:T(8,128)(2,1)S(1)} %get-tuple-element.18.ahead_at), channel_id=1, source_target_pairs={{1,0},{0,1},{3,2},{2,3},{5,4},{4,5},{7,6},{6,7},{9,8},{8,9},{11,10... | collective-permute-start | bytes 3145736 | tf_op jit(solution)/shard_map/ppermute | solution.py:28
  89.1 1.3 %collective-permute-start.8 = (bf16[512,1024]{1,0:T(8,128)(2,1)S(1)}, bf16[512,1024]{1,0:T(8,128)(2,1)S(1)}, u32[]{:S(2)}, u32[]{:S(2)}) collective-permute-start(bf16[512,1024]{1,0:T(8,128)(2,1)S(1)} %get-tuple-element.19.beyond_at), channel_id=1, source_target_pairs={{0,1},{2,3},{4,5},{6,7},{8,9},{10,11},{12,13},{14,15},{16,17},{18,... | collective-permute-start | bytes 3145736 | tf_op jit(solution)/shard_map/ppermute | solution.py:28
  90.4 1.3 %collective-permute-start.11 = (bf16[512,1024]{1,0:T(8,128)(2,1)S(1)}, bf16[512,1024]{1,0:T(8,128)(2,1)S(1)}, u32[]{:S(2)}, u32[]{:S(2)}) collective-permute-start(bf16[512,1024]{1,0:T(8,128)(2,1)S(1)} %bitcast.9), channel_id=1, source_target_pairs={{1,0},{0,1},{3,2},{2,3},{5,4},{4,5},{7,6},{6,7},{9,8},{8,9},{11,10... | collective-permute-start | bytes 3145736 | tf_op jit(solution)/shard_map/ppermute | solution.py:28
  91.7 0.0 collective-permute-done.6.sib_own
  91.7 0.4 collective-permute-start.10
  92.1 3.2 %collective-permute-done.9.first = bf16[512,1024]{1,0:T(8,128)(2,1)S(1)} collective-permute-done((bf16[512,1024]{1,0:T(8,128)(2,1)S(1)}, bf16[512,1024]{1,0:T(8,128)(2,1)S(1)}, u32[]{:S(2)}, u32[]{:S(2)}) %collective-permute-start.9) | collective-permute-done | bytes 1048608 | tf_op jit(solution)/shard_map/ppermute | solution.py:24
  95.3 0.1 fusion
  95.4 2.0 %collective-permute-start.13 = (bf16[256,1024]{1,0:T(8,128)(2,1)S(1)}, bf16[256,1024]{1,0:T(8,128)(2,1)S(1)}, u32[]{:S(2)}, u32[]{:S(2)}) collective-permute-start(bf16[256,1024]{1,0:T(8,128)(2,1)S(1)} %get-tuple-element.24), channel_id=1, source_target_pairs={{1,0},{0,1},{3,2},{2,3},{5,4},{4,5},{7,6},{6,7},{9,8},{8,9},{11,10... | collective-permute-start | bytes 1572872 | tf_op jit(solution)/shard_map/ppermute | solution.py:28
  97.4 0.1 collective-permute-start.12
  97.5 7.0 %shard_map.33 = (f32[1,2,1,4,512,512]{5,4,3,2,1,0:T(8,128)S(1)}, f32[1,2,1,256,512]{4,3,2,1,0:T(8,128)S(1)}) custom-call(s32[2]{0:T(128)S(1)} %pad_add_fusion.place, bf16[512,1024]{1,0:T(8,128)(2,1)S(1)} %bitcast.7, bf16[512,1024]{1,0:T(8,128)(2,1)S(1)} %get-tuple-element.18.ahead_at, bf16[512,1024]{1,0:T(8,128)(2,1)S(1)} %get-tuple-element.19.beyond_at, ...), custom_call_target="tpu_custom_call" | custom-call | flops 2147483648 | bytes 4194304 | tf_op jit(solution)/shard_map/pallas_call | solution.py:219
  104.6 1.4 %collective-permute-done.10.second = bf16[512,1024]{1,0:T(8,128)(2,1)S(1)} collective-permute-done((bf16[512,1024]{1,0:T(8,128)(2,1)S(1)}, bf16[512,1024]{1,0:T(8,128)(2,1)S(1)}, u32[]{:S(2)}, u32[]{:S(2)}) %collective-permute-start.10) | collective-permute-done | bytes 1048608 | tf_op jit(solution)/shard_map/ppermute | solution.py:24
  106.0 8.3 %shard_map.34 = (f32[1,2,1,4,512,512]{5,4,3,2,1,0:T(8,128)}, f32[1,2,1,256,512]{4,3,2,1,0:T(8,128)}) custom-call(s32[2]{0:T(128)S(1)} %pad_add_fusion.place, f32[1,2,1,4,512,512]{5,4,3,2,1,0:T(8,128)S(1)} %get-tuple-element.21.band_in, f32[1,2,1,256,512]{4,3,2,1,0:T(8,128)S(1)} %get-tuple-element.22.far_in, ...), custom_call_target="tpu_custom_call" | custom-call | flops 5368709120 | bytes 10485760 | tf_op jit(solution)/shard_map/pallas_call | solution.py:219
  (9 shorter events, 0.0 us)
Async XLA Ops:
  2.7 38.5 %all-to-all-start = ((bf16[32,16,1024]{2,1,0:T(8,128)(2,1)}), bf16[32,16,1024]{2,1,0:T(8,128)(2,1)S(1)}, u32[]{:S(2)}, u32[]{:S(2)}) async-start(bf16[32,16,1024]{2,1,0:T(8,128)(2,1)} %shard_map.30), calls=%async_computation | async-start | bytes 2097152 | tf_op jit(solution)/shard_map/all_to_all | solution.py:32
  16.6 24.6 %collective-permute-start = (bf16[32,16,1024]{2,1,0:T(8,128)(2,1)}, bf16[32,16,1024]{2,1,0:T(8,128)(2,1)}, u32[]{:S(2)}, u32[]{:S(2)}) collective-permute-start(bf16[32,16,1024]{2,1,0:T(8,128)(2,1)} %shard_map.31), channel_id=1, source_target_pairs={{2,0},{4,2},{6,4},{0,6},{3,1},{5,3},{7,5},{1,7},{10,8},{12,10},{14... | collective-permute-start | bytes 3145736 | tf_op jit(solution)/shard_map/ppermute | solution.py:14
  41.2 36.7 %all-to-all-start.1 = ((bf16[32,16,1024]{2,1,0:T(8,128)(2,1)}), bf16[32,16,1024]{2,1,0:T(8,128)(2,1)S(1)}, u32[]{:S(2)}, u32[]{:S(2)}) async-start(bf16[32,16,1024]{2,1,0:T(8,128)(2,1)} %collective-permute-done), calls=%async_computation.1 | async-start | bytes 2097152 | tf_op jit(solution)/shard_map/all_to_all | solution.py:32
  50.2 15.1 %collective-permute-start.1 = (bf16[320,1024]{1,0:T(8,128)(2,1)S(1)}, bf16[320,1024]{1,0:T(8,128)(2,1)}, u32[]{:S(2)}, u32[]{:S(2)}) collective-permute-start(bf16[320,1024]{1,0:T(8,128)(2,1)S(1)} %bitcast.12), channel_id=1, source_target_pairs={{2,0},{4,2},{6,4},{0,6},{3,1},{5,3},{7,5},{1,7},{10,8},{12,10},{14... | collective-permute-start | bytes 1966088 | tf_op jit(solution)/shard_map/ppermute | solution.py:14
  53.7 9.2 %collective-permute-start.2 = (bf16[192,1024]{1,0:T(8,128)(2,1)S(1)}, bf16[192,1024]{1,0:T(8,128)(2,1)S(1)}, u32[]{:S(2)}, u32[]{:S(2)}) collective-permute-start(bf16[192,1024]{1,0:T(8,128)(2,1)S(1)} %bitcast.13), channel_id=1, source_target_pairs={{6,0},{0,2},{2,4},{4,6},{7,1},{1,3},{3,5},{5,7},{14,8},{8,10},{10,... | collective-permute-start | bytes 1179656 | tf_op jit(solution)/shard_map/ppermute | solution.py:14
  62.9 8.2 %collective-permute-start.3 = (bf16[192,1024]{1,0:T(8,128)(2,1)S(1)}, bf16[192,1024]{1,0:T(8,128)(2,1)S(1)}, u32[]{:S(2)}, u32[]{:S(2)}) collective-permute-start(bf16[192,1024]{1,0:T(8,128)(2,1)S(1)} %collective-permute-done.2), channel_id=1, source_target_pairs={{6,0},{0,2},{2,4},{4,6},{7,1},{1,3},{3,5},{5,7},{14,8},{8,10},{10,... | collective-permute-start | bytes 1179656 | tf_op jit(solution)/shard_map/ppermute | solution.py:14
  65.2 14.5 %collective-permute-start.5 = (bf16[320,1024]{1,0:T(8,128)(2,1)}, bf16[320,1024]{1,0:T(8,128)(2,1)}, u32[]{:S(2)}, u32[]{:S(2)}) collective-permute-start(bf16[320,1024]{1,0:T(8,128)(2,1)} %collective-permute-done.1.down_1), channel_id=1, source_target_pairs={{2,0},{4,2},{6,4},{0,6},{3,1},{5,3},{7,5},{1,7},{10,8},{12,10},{14... | collective-permute-start | bytes 1966088 | tf_op jit(solution)/shard_map/ppermute | solution.py:14
  71.0 8.2 %collective-permute-start.4 = (bf16[192,1024]{1,0:T(8,128)(2,1)S(1)}, bf16[192,1024]{1,0:T(8,128)(2,1)}, u32[]{:S(2)}, u32[]{:S(2)}) collective-permute-start(bf16[192,1024]{1,0:T(8,128)(2,1)S(1)} %collective-permute-done.3.up_2), channel_id=1, source_target_pairs={{6,0},{0,2},{2,4},{4,6},{7,1},{1,3},{3,5},{5,7},{14,8},{8,10},{10,... | collective-permute-start | bytes 1179656 | tf_op jit(solution)/shard_map/ppermute | solution.py:14
  71.1 20.6 %collective-permute-start.6 = (bf16[512,1024]{1,0:T(8,128)(2,1)S(1)}, bf16[512,1024]{1,0:T(8,128)(2,1)S(1)}, u32[]{:S(2)}, u32[]{:S(2)}) collective-permute-start(bf16[512,1024]{1,0:T(8,128)(2,1)S(1)} %bitcast.6), channel_id=1, source_target_pairs={{1,0},{3,2},{5,4},{7,6},{9,8},{11,10},{13,12},{15,14},{17,16},{19,... | collective-permute-start | bytes 3145736 | tf_op jit(solution)/shard_map/ppermute | solution.py:28
  77.8 17.5 %collective-permute-start.9 = (bf16[512,1024]{1,0:T(8,128)(2,1)S(1)}, bf16[512,1024]{1,0:T(8,128)(2,1)S(1)}, u32[]{:S(2)}, u32[]{:S(2)}) collective-permute-start(bf16[512,1024]{1,0:T(8,128)(2,1)S(1)} %bitcast.8), channel_id=1, source_target_pairs={{2,0},{7,1},{4,2},{1,3},{6,4},{3,5},{0,6},{5,7},{10,8},{15,9},{12,... | collective-permute-start | bytes 3145736 | tf_op jit(solution)/shard_map/ppermute | solution.py:24
  81.7 15.7 %collective-permute-start.7 = (bf16[512,1024]{1,0:T(8,128)(2,1)S(1)}, bf16[512,1024]{1,0:T(8,128)(2,1)S(1)}, u32[]{:S(2)}, u32[]{:S(2)}) collective-permute-start(bf16[512,1024]{1,0:T(8,128)(2,1)S(1)} %get-tuple-element.18.ahead_at), channel_id=1, source_target_pairs={{1,0},{0,1},{3,2},{2,3},{5,4},{4,5},{7,6},{6,7},{9,8},{8,9},{11,10... | collective-permute-start | bytes 3145736 | tf_op jit(solution)/shard_map/ppermute | solution.py:28
  89.1 8.4 %collective-permute-start.8 = (bf16[512,1024]{1,0:T(8,128)(2,1)S(1)}, bf16[512,1024]{1,0:T(8,128)(2,1)S(1)}, u32[]{:S(2)}, u32[]{:S(2)}) collective-permute-start(bf16[512,1024]{1,0:T(8,128)(2,1)S(1)} %get-tuple-element.19.beyond_at), channel_id=1, source_target_pairs={{0,1},{2,3},{4,5},{6,7},{8,9},{10,11},{12,13},{14,15},{16,17},{18,... | collective-permute-start | bytes 3145736 | tf_op jit(solution)/shard_map/ppermute | solution.py:28
  90.4 14.1 %collective-permute-start.11 = (bf16[512,1024]{1,0:T(8,128)(2,1)S(1)}, bf16[512,1024]{1,0:T(8,128)(2,1)S(1)}, u32[]{:S(2)}, u32[]{:S(2)}) collective-permute-start(bf16[512,1024]{1,0:T(8,128)(2,1)S(1)} %bitcast.9), channel_id=1, source_target_pairs={{1,0},{0,1},{3,2},{2,3},{5,4},{4,5},{7,6},{6,7},{9,8},{8,9},{11,10... | collective-permute-start | bytes 3145736 | tf_op jit(solution)/shard_map/ppermute | solution.py:28
  91.7 14.3 %collective-permute-start.10 = (bf16[512,1024]{1,0:T(8,128)(2,1)S(1)}, bf16[512,1024]{1,0:T(8,128)(2,1)S(1)}, u32[]{:S(2)}, u32[]{:S(2)}) collective-permute-start(bf16[512,1024]{1,0:T(8,128)(2,1)S(1)} %bitcast.10), channel_id=1, source_target_pairs={{6,0},{3,1},{0,2},{5,3},{2,4},{7,5},{4,6},{1,7},{14,8},{11,9},{8,1... | collective-permute-start | bytes 3145736 | tf_op jit(solution)/shard_map/ppermute | solution.py:24
  95.4 10.6 %collective-permute-start.13 = (bf16[256,1024]{1,0:T(8,128)(2,1)S(1)}, bf16[256,1024]{1,0:T(8,128)(2,1)S(1)}, u32[]{:S(2)}, u32[]{:S(2)}) collective-permute-start(bf16[256,1024]{1,0:T(8,128)(2,1)S(1)} %get-tuple-element.24), channel_id=1, source_target_pairs={{1,0},{0,1},{3,2},{2,3},{5,4},{4,5},{7,6},{6,7},{9,8},{8,9},{11,10... | collective-permute-start | bytes 1572872 | tf_op jit(solution)/shard_map/ppermute | solution.py:28
  97.4 8.6 %collective-permute-start.12 = (bf16[256,1024]{1,0:T(8,128)(2,1)S(1)}, bf16[256,1024]{1,0:T(8,128)(2,1)S(1)}, u32[]{:S(2)}, u32[]{:S(2)}) collective-permute-start(bf16[256,1024]{1,0:T(8,128)(2,1)S(1)} %get-tuple-element.25), channel_id=1, source_target_pairs={{1,0},{0,1},{3,2},{2,3},{5,4},{4,5},{7,6},{6,7},{9,8},{8,9},{11,10... | collective-permute-start | bytes 1572872 | tf_op jit(solution)/shard_map/ppermute | solution.py:28

commit v10 on v9

--- a/solution.py
+++ b/solution.py
@@ -163,22 +163,23 @@
             here = product[part * rows : (part + 1) * rows]
             band[0, part, 0, 0] = here + band_in[0, part, 0, slot]
 
-    @pl.when(step == 0)
-    def _():
-        @pl.when(core == 0)
-        def _():
-            load(0, second, own).start()
-            load(1, first, beyond).start()
-
-        @pl.when(core != 0)
-        def _():
-            load(0, first, own).start()
-            load(1, second, beyond).start()
-
+    def begin(mine, theirs):
+        load(1, theirs, beyond).start()
         for copy in loads:
             copy.start()
-        load(0, first, own).wait()
-        swapped[...] = quadrature(own[...])
+        own[...] = mine[...]
+        swapped[...] = quadrature(mine[...])
+
+    @pl.when((step == 0) & (core == 0))
+    def _():
+        begin(second, first)
+
+    @pl.when((step == 0) & (core != 0))
+    def _():
+        begin(first, second)
+
+    @pl.when(step == 0)
+    def _():
         tile(0, own)
 
     @pl.when(step == 1)
@@ -281,8 +282,8 @@
     far_out = jax.ShapeDtypeStruct(far_shape, jnp.float32)
     band, far = call(
         late_kernel, (4,), place,
-        (late_first, late_second, late_ahead, late_sib_ahead, *late_sib_first),
-        (band_sum, far_sum), [band_out, far_out],
+        (late_ahead, late_sib_ahead, *late_sib_first),
+        (band_sum, far_sum, late_first, late_second), [band_out, far_out],
         [
             pl.BlockSpec(
                 (1, 2, 1, 1, rows, rows),

time: 115 us -> 115 us (level)
  no operation moved by 1% of the time
where the time goes in v10:
time: 115 us
  starting transfers between devices  49.9 us (43%)
  waiting for transfers between devices  42.1 us (37%)
  Pallas kernels  21.5 us (19%)
    ppermute x6, waiting for transfers between devices, from_ahead(): lax.ppermute(block, 'arow', [((i + distance) % size, i) for i in range(si...  37.4 us
    all_to_all x2, starting transfers between devices, turn(): lax.all_to_all(block, 'chan', split_axis=0, concat_axis=0, tiled=True)  20.8 us
    ppermute x6, starting transfers between devices, from_sibling(): return lax.ppermute(block, 'acol', [(1 - core, core) for core in cores])  18.8 us
    pallas_call x3, Pallas kernels, call(): pl.pallas_call(kernel, out_shape=outs, grid_spec=pltpu.PrefetchScalarGrid...  17.4 us
    ppermute x6, starting transfers between devices, from_ahead(): lax.ppermute(block, 'arow', [((i + distance) % size, i) for i in range(si...  9.83 us
    ppermute x2, waiting for transfers between devices, from_both_sides(): return lax.ppermute(block, ('arow', 'acol'), route)  4.67 us
    pallas_call x2, Pallas kernels, half_of(): pl.pallas_call(cut_kernel, out_shape=jax.ShapeDtypeStruct((channels, rows...  4.1 us
  transfers between devices with their start and end apart: 16, of which 8 were waited for; matrix products, arithmetic and copies ran while one was open for 0% of the time, Pallas kernels for 10%

profile of v10, /device:TPU:1, one launch (start us, length us, event | category | flops | bytes accessed | tf_op | source)
XLA Modules:
  0.0 114.6 jit_solution(143537642255698476)
XLA Ops:
  0.6 2.1 %shard_map.30 = bf16[32,16,1024]{2,1,0:T(8,128)(2,1)} custom-call(bf16[32,1,16,2048]{3,2,1,0:T(8,128)(2,1)} %imaginary.3, bf16[32,1,16,2048]{3,2,1,0:T(8,128)(2,1)} %imaginary.3), custom_call_target="tpu_custom_call" | custom-call | tf_op jit(solution)/shard_map/pallas_call | solution.py:45
  2.7 11.9 %all-to-all-start = ((bf16[32,16,1024]{2,1,0:T(8,128)(2,1)}), bf16[32,16,1024]{2,1,0:T(8,128)(2,1)S(1)}, u32[]{:S(2)}, u32[]{:S(2)}) async-start(bf16[32,16,1024]{2,1,0:T(8,128)(2,1)} %shard_map.30), calls=%async_computation | async-start | bytes 2097152 | tf_op jit(solution)/shard_map/all_to_all | solution.py:32
  14.6 2.1 %shard_map.31 = bf16[32,16,1024]{2,1,0:T(8,128)(2,1)} custom-call(bf16[32,1,16,2048]{3,2,1,0:T(8,128)(2,1)} %imaginary.3, bf16[32,1,16,2048]{3,2,1,0:T(8,128)(2,1)} %imaginary.3), custom_call_target="tpu_custom_call" | custom-call | tf_op jit(solution)/shard_map/pallas_call | solution.py:45
  16.6 2.7 %collective-permute-start = (bf16[32,16,1024]{2,1,0:T(8,128)(2,1)}, bf16[32,16,1024]{2,1,0:T(8,128)(2,1)}, u32[]{:S(2)}, u32[]{:S(2)}) collective-permute-start(bf16[32,16,1024]{2,1,0:T(8,128)(2,1)} %shard_map.31), channel_id=1, source_target_pairs={{2,0},{4,2},{6,4},{0,6},{3,1},{5,3},{7,5},{1,7},{10,8},{12,10},{14... | collective-permute-start | bytes 3145736 | tf_op jit(solution)/shard_map/ppermute | solution.py:14
  19.3 21.8 %collective-permute-done = bf16[32,16,1024]{2,1,0:T(8,128)(2,1)} collective-permute-done((bf16[32,16,1024]{2,1,0:T(8,128)(2,1)}, bf16[32,16,1024]{2,1,0:T(8,128)(2,1)}, u32[]{:S(2)}, u32[]{:S(2)}) %collective-permute-start) | collective-permute-done | bytes 1048608 | tf_op jit(solution)/shard_map/ppermute | solution.py:14
  41.2 8.9 %all-to-all-start.1 = ((bf16[32,16,1024]{2,1,0:T(8,128)(2,1)}), bf16[32,16,1024]{2,1,0:T(8,128)(2,1)S(1)}, u32[]{:S(2)}, u32[]{:S(2)}) async-start(bf16[32,16,1024]{2,1,0:T(8,128)(2,1)} %collective-permute-done), calls=%async_computation.1 | async-start | bytes 2097152 | tf_op jit(solution)/shard_map/all_to_all | solution.py:32
  50.1 0.1 slice.24
  50.2 3.5 %collective-permute-start.1 = (bf16[320,1024]{1,0:T(8,128)(2,1)S(1)}, bf16[320,1024]{1,0:T(8,128)(2,1)}, u32[]{:S(2)}, u32[]{:S(2)}) collective-permute-start(bf16[320,1024]{1,0:T(8,128)(2,1)S(1)} %bitcast.12), channel_id=1, source_target_pairs={{2,0},{4,2},{6,4},{0,6},{3,1},{5,3},{7,5},{1,7},{10,8},{12,10},{14... | collective-permute-start | bytes 1966088 | tf_op jit(solution)/shard_map/ppermute | solution.py:14
  53.7 0.1 collective-permute-start.2
  53.8 9.1 %collective-permute-done.2 = bf16[192,1024]{1,0:T(8,128)(2,1)S(1)} collective-permute-done((bf16[192,1024]{1,0:T(8,128)(2,1)S(1)}, bf16[192,1024]{1,0:T(8,128)(2,1)S(1)}, u32[]{:S(2)}, u32[]{:S(2)}) %collective-permute-start.2) | collective-permute-done | bytes 393248 | tf_op jit(solution)/shard_map/ppermute | solution.py:14
  62.9 2.4 %collective-permute-done.1.down_1 = bf16[320,1024]{1,0:T(8,128)(2,1)} collective-permute-done((bf16[320,1024]{1,0:T(8,128)(2,1)S(1)}, bf16[320,1024]{1,0:T(8,128)(2,1)}, u32[]{:S(2)}, u32[]{:S(2)}) %collective-permute-start.1) | collective-permute-done | bytes 655392 | tf_op jit(solution)/shard_map/ppermute | solution.py:14
  65.2 3.5 %collective-permute-start.5 = (bf16[320,1024]{1,0:T(8,128)(2,1)}, bf16[320,1024]{1,0:T(8,128)(2,1)}, u32[]{:S(2)}, u32[]{:S(2)}) collective-permute-start(bf16[320,1024]{1,0:T(8,128)(2,1)} %collective-permute-done.1.down_1), channel_id=1, source_target_pairs={{2,0},{4,2},{6,4},{0,6},{3,1},{5,3},{7,5},{1,7},{10,8},{12,10},{14... | collective-permute-start | bytes 1966088 | tf_op jit(solution)/shard_map/ppermute | solution.py:14
  68.7 2.3 %collective-permute-done.3.up_2 = bf16[192,1024]{1,0:T(8,128)(2,1)S(1)} collective-permute-done((bf16[192,1024]{1,0:T(8,128)(2,1)S(1)}, bf16[192,1024]{1,0:T(8,128)(2,1)S(1)}, u32[]{:S(2)}, u32[]{:S(2)}) %collective-permute-start.3) | collective-permute-done | bytes 393248 | tf_op jit(solution)/shard_map/ppermute | solution.py:14
  71.0 0.0 collective-permute-start.4
  71.0 0.1 pad_add_fusion.place
  71.1 6.7 %collective-permute-start.6 = (bf16[512,1024]{1,0:T(8,128)(2,1)S(1)}, bf16[512,1024]{1,0:T(8,128)(2,1)S(1)}, u32[]{:S(2)}, u32[]{:S(2)}) collective-permute-start(bf16[512,1024]{1,0:T(8,128)(2,1)S(1)} %bitcast.6), channel_id=1, source_target_pairs={{1,0},{3,2},{5,4},{7,6},{9,8},{11,10},{13,12},{15,14},{17,16},{19,... | collective-permute-start | bytes 3145736 | tf_op jit(solution)/shard_map/ppermute | solution.py:28
  77.8 0.1 collective-permute-start.9
  77.9 1.3 %collective-permute-done.4.up_3 = bf16[192,1024]{1,0:T(8,128)(2,1)} collective-permute-done((bf16[192,1024]{1,0:T(8,128)(2,1)S(1)}, bf16[192,1024]{1,0:T(8,128)(2,1)}, u32[]{:S(2)}, u32[]{:S(2)}) %collective-permute-start.4) | collective-permute-done | bytes 393248 | tf_op jit(solution)/shard_map/ppermute | solution.py:14
  79.2 0.5 collective-permute-done.5.down_2
  79.7 2.0 %shard_map.32 = (bf16[512,1024]{1,0:T(8,128)(2,1)S(1)}, bf16[512,1024]{1,0:T(8,128)(2,1)S(1)}) custom-call(s32[2]{0:T(128)S(1)} %pad_add_fusion.place, bf16[320,1024]{1,0:T(8,128)(2,1)} %collective-permute-done.1.down_1, bf16[192,1024]{1,0:T(8,128)(2,1)} %collective-permute-done.4.up_3, bf16[320,1024]{1,0:T(8,128)(2,1)} %collective-permute-done.5.down_2, ...), custom_call_target="tpu_custom_call" | custom-call | flops 17179869184 | bytes 33554432 | tf_op jit(solution)/shard_map/pallas_call | solution.py:220
  81.7 7.4 %collective-permute-start.7 = (bf16[512,1024]{1,0:T(8,128)(2,1)S(1)}, bf16[512,1024]{1,0:T(8,128)(2,1)S(1)}, u32[]{:S(2)}, u32[]{:S(2)}) collective-permute-start(bf16[512,1024]{1,0:T(8,128)(2,1)S(1)} %get-tuple-element.18.ahead_at), channel_id=1, source_target_pairs={{1,0},{0,1},{3,2},{2,3},{5,4},{4,5},{7,6},{6,7},{9,8},{8,9},{11,10... | collective-permute-start | bytes 3145736 | tf_op jit(solution)/shard_map/ppermute | solution.py:28
  89.1 1.3 %collective-permute-start.8 = (bf16[512,1024]{1,0:T(8,128)(2,1)S(1)}, bf16[512,1024]{1,0:T(8,128)(2,1)S(1)}, u32[]{:S(2)}, u32[]{:S(2)}) collective-permute-start(bf16[512,1024]{1,0:T(8,128)(2,1)S(1)} %get-tuple-element.19.beyond_at), channel_id=1, source_target_pairs={{0,1},{2,3},{4,5},{6,7},{8,9},{10,11},{12,13},{14,15},{16,17},{18,... | collective-permute-start | bytes 3145736 | tf_op jit(solution)/shard_map/ppermute | solution.py:28
  90.4 1.3 %collective-permute-start.11 = (bf16[512,1024]{1,0:T(8,128)(2,1)S(1)}, bf16[512,1024]{1,0:T(8,128)(2,1)S(1)}, u32[]{:S(2)}, u32[]{:S(2)}) collective-permute-start(bf16[512,1024]{1,0:T(8,128)(2,1)S(1)} %bitcast.9), channel_id=1, source_target_pairs={{1,0},{0,1},{3,2},{2,3},{5,4},{4,5},{7,6},{6,7},{9,8},{8,9},{11,10... | collective-permute-start | bytes 3145736 | tf_op jit(solution)/shard_map/ppermute | solution.py:28
  91.7 0.0 collective-permute-done.6.sib_own
  91.7 0.4 collective-permute-start.10
  92.1 3.2 %collective-permute-done.9.first = bf16[512,1024]{1,0:T(8,128)(2,1)S(1)} collective-permute-done((bf16[512,1024]{1,0:T(8,128)(2,1)S(1)}, bf16[512,1024]{1,0:T(8,128)(2,1)S(1)}, u32[]{:S(2)}, u32[]{:S(2)}) %collective-permute-start.9) | collective-permute-done | bytes 1048608 | tf_op jit(solution)/shard_map/ppermute | solution.py:24
  95.3 0.1 fusion
  95.4 2.0 %collective-permute-start.13 = (bf16[256,1024]{1,0:T(8,128)(2,1)S(1)}, bf16[256,1024]{1,0:T(8,128)(2,1)S(1)}, u32[]{:S(2)}, u32[]{:S(2)}) collective-permute-start(bf16[256,1024]{1,0:T(8,128)(2,1)S(1)} %get-tuple-element.24), channel_id=1, source_target_pairs={{1,0},{0,1},{3,2},{2,3},{5,4},{4,5},{7,6},{6,7},{9,8},{8,9},{11,10... | collective-permute-start | bytes 1572872 | tf_op jit(solution)/shard_map/ppermute | solution.py:28
  97.4 0.1 collective-permute-start.12
  97.5 7.0 %shard_map.33 = (f32[1,2,1,4,512,512]{5,4,3,2,1,0:T(8,128)S(1)}, f32[1,2,1,256,512]{4,3,2,1,0:T(8,128)S(1)}) custom-call(s32[2]{0:T(128)S(1)} %pad_add_fusion.place, bf16[512,1024]{1,0:T(8,128)(2,1)S(1)} %bitcast.7, bf16[512,1024]{1,0:T(8,128)(2,1)S(1)} %get-tuple-element.18.ahead_at, bf16[512,1024]{1,0:T(8,128)(2,1)S(1)} %get-tuple-element.19.beyond_at, ...), custom_call_target="tpu_custom_call" | custom-call | flops 2147483648 | bytes 4194304 | tf_op jit(solution)/shard_map/pallas_call | solution.py:220
  104.6 1.4 %collective-permute-done.10.second = bf16[512,1024]{1,0:T(8,128)(2,1)S(1)} collective-permute-done((bf16[512,1024]{1,0:T(8,128)(2,1)S(1)}, bf16[512,1024]{1,0:T(8,128)(2,1)S(1)}, u32[]{:S(2)}, u32[]{:S(2)}) %collective-permute-start.10) | collective-permute-done | bytes 1048608 | tf_op jit(solution)/shard_map/ppermute | solution.py:24
  106.0 8.4 %shard_map.34 = (f32[1,2,1,4,512,512]{5,4,3,2,1,0:T(8,128)}, f32[1,2,1,256,512]{4,3,2,1,0:T(8,128)}) custom-call(s32[2]{0:T(128)S(1)} %pad_add_fusion.place, f32[1,2,1,4,512,512]{5,4,3,2,1,0:T(8,128)S(1)} %get-tuple-element.21.band_in, f32[1,2,1,256,512]{4,3,2,1,0:T(8,128)S(1)} %get-tuple-element.22.far_in, ...), custom_call_target="tpu_custom_call" | custom-call | flops 5368709120 | bytes 10485760 | tf_op jit(solution)/shard_map/pallas_call | solution.py:220
  (9 shorter events, 0.0 us)
Async XLA Ops:
  2.7 38.5 %all-to-all-start = ((bf16[32,16,1024]{2,1,0:T(8,128)(2,1)}), bf16[32,16,1024]{2,1,0:T(8,128)(2,1)S(1)}, u32[]{:S(2)}, u32[]{:S(2)}) async-start(bf16[32,16,1024]{2,1,0:T(8,128)(2,1)} %shard_map.30), calls=%async_computation | async-start | bytes 2097152 | tf_op jit(solution)/shard_map/all_to_all | solution.py:32
  16.6 24.6 %collective-permute-start = (bf16[32,16,1024]{2,1,0:T(8,128)(2,1)}, bf16[32,16,1024]{2,1,0:T(8,128)(2,1)}, u32[]{:S(2)}, u32[]{:S(2)}) collective-permute-start(bf16[32,16,1024]{2,1,0:T(8,128)(2,1)} %shard_map.31), channel_id=1, source_target_pairs={{2,0},{4,2},{6,4},{0,6},{3,1},{5,3},{7,5},{1,7},{10,8},{12,10},{14... | collective-permute-start | bytes 3145736 | tf_op jit(solution)/shard_map/ppermute | solution.py:14
  41.2 36.7 %all-to-all-start.1 = ((bf16[32,16,1024]{2,1,0:T(8,128)(2,1)}), bf16[32,16,1024]{2,1,0:T(8,128)(2,1)S(1)}, u32[]{:S(2)}, u32[]{:S(2)}) async-start(bf16[32,16,1024]{2,1,0:T(8,128)(2,1)} %collective-permute-done), calls=%async_computation.1 | async-start | bytes 2097152 | tf_op jit(solution)/shard_map/all_to_all | solution.py:32
  50.2 15.1 %collective-permute-start.1 = (bf16[320,1024]{1,0:T(8,128)(2,1)S(1)}, bf16[320,1024]{1,0:T(8,128)(2,1)}, u32[]{:S(2)}, u32[]{:S(2)}) collective-permute-start(bf16[320,1024]{1,0:T(8,128)(2,1)S(1)} %bitcast.12), channel_id=1, source_target_pairs={{2,0},{4,2},{6,4},{0,6},{3,1},{5,3},{7,5},{1,7},{10,8},{12,10},{14... | collective-permute-start | bytes 1966088 | tf_op jit(solution)/shard_map/ppermute | solution.py:14
  53.7 9.2 %collective-permute-start.2 = (bf16[192,1024]{1,0:T(8,128)(2,1)S(1)}, bf16[192,1024]{1,0:T(8,128)(2,1)S(1)}, u32[]{:S(2)}, u32[]{:S(2)}) collective-permute-start(bf16[192,1024]{1,0:T(8,128)(2,1)S(1)} %bitcast.13), channel_id=1, source_target_pairs={{6,0},{0,2},{2,4},{4,6},{7,1},{1,3},{3,5},{5,7},{14,8},{8,10},{10,... | collective-permute-start | bytes 1179656 | tf_op jit(solution)/shard_map/ppermute | solution.py:14
  62.9 8.2 %collective-permute-start.3 = (bf16[192,1024]{1,0:T(8,128)(2,1)S(1)}, bf16[192,1024]{1,0:T(8,128)(2,1)S(1)}, u32[]{:S(2)}, u32[]{:S(2)}) collective-permute-start(bf16[192,1024]{1,0:T(8,128)(2,1)S(1)} %collective-permute-done.2), channel_id=1, source_target_pairs={{6,0},{0,2},{2,4},{4,6},{7,1},{1,3},{3,5},{5,7},{14,8},{8,10},{10,... | collective-permute-start | bytes 1179656 | tf_op jit(solution)/shard_map/ppermute | solution.py:14
  65.2 14.5 %collective-permute-start.5 = (bf16[320,1024]{1,0:T(8,128)(2,1)}, bf16[320,1024]{1,0:T(8,128)(2,1)}, u32[]{:S(2)}, u32[]{:S(2)}) collective-permute-start(bf16[320,1024]{1,0:T(8,128)(2,1)} %collective-permute-done.1.down_1), channel_id=1, source_target_pairs={{2,0},{4,2},{6,4},{0,6},{3,1},{5,3},{7,5},{1,7},{10,8},{12,10},{14... | collective-permute-start | bytes 1966088 | tf_op jit(solution)/shard_map/ppermute | solution.py:14
  71.0 8.2 %collective-permute-start.4 = (bf16[192,1024]{1,0:T(8,128)(2,1)S(1)}, bf16[192,1024]{1,0:T(8,128)(2,1)}, u32[]{:S(2)}, u32[]{:S(2)}) collective-permute-start(bf16[192,1024]{1,0:T(8,128)(2,1)S(1)} %collective-permute-done.3.up_2), channel_id=1, source_target_pairs={{6,0},{0,2},{2,4},{4,6},{7,1},{1,3},{3,5},{5,7},{14,8},{8,10},{10,... | collective-permute-start | bytes 1179656 | tf_op jit(solution)/shard_map/ppermute | solution.py:14
  71.1 20.6 %collective-permute-start.6 = (bf16[512,1024]{1,0:T(8,128)(2,1)S(1)}, bf16[512,1024]{1,0:T(8,128)(2,1)S(1)}, u32[]{:S(2)}, u32[]{:S(2)}) collective-permute-start(bf16[512,1024]{1,0:T(8,128)(2,1)S(1)} %bitcast.6), channel_id=1, source_target_pairs={{1,0},{3,2},{5,4},{7,6},{9,8},{11,10},{13,12},{15,14},{17,16},{19,... | collective-permute-start | bytes 3145736 | tf_op jit(solution)/shard_map/ppermute | solution.py:28
  77.8 17.5 %collective-permute-start.9 = (bf16[512,1024]{1,0:T(8,128)(2,1)S(1)}, bf16[512,1024]{1,0:T(8,128)(2,1)S(1)}, u32[]{:S(2)}, u32[]{:S(2)}) collective-permute-start(bf16[512,1024]{1,0:T(8,128)(2,1)S(1)} %bitcast.8), channel_id=1, source_target_pairs={{2,0},{7,1},{4,2},{1,3},{6,4},{3,5},{0,6},{5,7},{10,8},{15,9},{12,... | collective-permute-start | bytes 3145736 | tf_op jit(solution)/shard_map/ppermute | solution.py:24
  81.7 15.7 %collective-permute-start.7 = (bf16[512,1024]{1,0:T(8,128)(2,1)S(1)}, bf16[512,1024]{1,0:T(8,128)(2,1)S(1)}, u32[]{:S(2)}, u32[]{:S(2)}) collective-permute-start(bf16[512,1024]{1,0:T(8,128)(2,1)S(1)} %get-tuple-element.18.ahead_at), channel_id=1, source_target_pairs={{1,0},{0,1},{3,2},{2,3},{5,4},{4,5},{7,6},{6,7},{9,8},{8,9},{11,10... | collective-permute-start | bytes 3145736 | tf_op jit(solution)/shard_map/ppermute | solution.py:28
  89.1 8.4 %collective-permute-start.8 = (bf16[512,1024]{1,0:T(8,128)(2,1)S(1)}, bf16[512,1024]{1,0:T(8,128)(2,1)S(1)}, u32[]{:S(2)}, u32[]{:S(2)}) collective-permute-start(bf16[512,1024]{1,0:T(8,128)(2,1)S(1)} %get-tuple-element.19.beyond_at), channel_id=1, source_target_pairs={{0,1},{2,3},{4,5},{6,7},{8,9},{10,11},{12,13},{14,15},{16,17},{18,... | collective-permute-start | bytes 3145736 | tf_op jit(solution)/shard_map/ppermute | solution.py:28
  90.4 14.1 %collective-permute-start.11 = (bf16[512,1024]{1,0:T(8,128)(2,1)S(1)}, bf16[512,1024]{1,0:T(8,128)(2,1)S(1)}, u32[]{:S(2)}, u32[]{:S(2)}) collective-permute-start(bf16[512,1024]{1,0:T(8,128)(2,1)S(1)} %bitcast.9), channel_id=1, source_target_pairs={{1,0},{0,1},{3,2},{2,3},{5,4},{4,5},{7,6},{6,7},{9,8},{8,9},{11,10... | collective-permute-start | bytes 3145736 | tf_op jit(solution)/shard_map/ppermute | solution.py:28
  91.7 14.3 %collective-permute-start.10 = (bf16[512,1024]{1,0:T(8,128)(2,1)S(1)}, bf16[512,1024]{1,0:T(8,128)(2,1)S(1)}, u32[]{:S(2)}, u32[]{:S(2)}) collective-permute-start(bf16[512,1024]{1,0:T(8,128)(2,1)S(1)} %bitcast.10), channel_id=1, source_target_pairs={{6,0},{3,1},{0,2},{5,3},{2,4},{7,5},{4,6},{1,7},{14,8},{11,9},{8,1... | collective-permute-start | bytes 3145736 | tf_op jit(solution)/shard_map/ppermute | solution.py:24
  95.4 10.6 %collective-permute-start.13 = (bf16[256,1024]{1,0:T(8,128)(2,1)S(1)}, bf16[256,1024]{1,0:T(8,128)(2,1)S(1)}, u32[]{:S(2)}, u32[]{:S(2)}) collective-permute-start(bf16[256,1024]{1,0:T(8,128)(2,1)S(1)} %get-tuple-element.24), channel_id=1, source_target_pairs={{1,0},{0,1},{3,2},{2,3},{5,4},{4,5},{7,6},{6,7},{9,8},{8,9},{11,10... | collective-permute-start | bytes 1572872 | tf_op jit(solution)/shard_map/ppermute | solution.py:28
  97.4 8.6 %collective-permute-start.12 = (bf16[256,1024]{1,0:T(8,128)(2,1)S(1)}, bf16[256,1024]{1,0:T(8,128)(2,1)S(1)}, u32[]{:S(2)}, u32[]{:S(2)}) collective-permute-start(bf16[256,1024]{1,0:T(8,128)(2,1)S(1)} %get-tuple-element.25), channel_id=1, source_target_pairs={{1,0},{0,1},{3,2},{2,3},{5,4},{4,5},{7,6},{6,7},{9,8},{8,9},{11,10... | collective-permute-start | bytes 1572872 | tf_op jit(solution)/shard_map/ppermute | solution.py:28

commit v11 on v9

--- a/solution.py
+++ b/solution.py
@@ -5,7 +5,7 @@
 from jax.experimental.pallas import tpu as pltpu
 from jax.sharding import PartitionSpec as P
 
-DOWN_ROWS = 320
+DOWN_ROWS = 304
 VMEM_BYTES = 28 * 1024 * 1024
 
 

time: 115 us -> 115 us (level)
  no operation moved by 1% of the time
where the time goes in v11:
time: 115 us
  starting transfers between devices  49.2 us (43%)
  waiting for transfers between devices  42.8 us (37%)
  Pallas kernels  21.5 us (19%)
    ppermute x6, waiting for transfers between devices, from_ahead(): lax.ppermute(block, 'arow', [((i + distance) % size, i) for i in range(si...  38.1 us
    all_to_all x2, starting transfers between devices, turn(): lax.all_to_all(block, 'chan', split_axis=0, concat_axis=0, tiled=True)  20.8 us
    ppermute x6, starting transfers between devices, from_sibling(): return lax.ppermute(block, 'acol', [(1 - core, core) for core in cores])  18.5 us
    pallas_call x3, Pallas kernels, call(): pl.pallas_call(kernel, out_shape=outs, grid_spec=pltpu.PrefetchScalarGrid...  17.4 us
    ppermute x6, starting transfers between devices, from_ahead(): lax.ppermute(block, 'arow', [((i + distance) % size, i) for i in range(si...  9.84 us
    ppermute x2, waiting for transfers between devices, from_both_sides(): return lax.ppermute(block, ('arow', 'acol'), route)  4.67 us
    pallas_call x2, Pallas kernels, half_of(): pl.pallas_call(cut_kernel, out_shape=jax.ShapeDtypeStruct((channels, rows...  4.1 us
  transfers between devices with their start and end apart: 16, of which 8 were waited for; matrix products, arithmetic and copies ran while one was open for 0% of the time, Pallas kernels for 10%

profile of v11, /device:TPU:1, one launch (start us, length us, event | category | flops | bytes accessed | tf_op | source)
XLA Modules:
  0.0 114.7 jit_solution(2971736174377826224)
XLA Ops:
  0.6 2.1 %shard_map.30 = bf16[32,16,1024]{2,1,0:T(8,128)(2,1)} custom-call(bf16[32,1,16,2048]{3,2,1,0:T(8,128)(2,1)} %imaginary.3, bf16[32,1,16,2048]{3,2,1,0:T(8,128)(2,1)} %imaginary.3), custom_call_target="tpu_custom_call" | custom-call | tf_op jit(solution)/shard_map/pallas_call | solution.py:45
  2.7 11.9 %all-to-all-start = ((bf16[32,16,1024]{2,1,0:T(8,128)(2,1)}), bf16[32,16,1024]{2,1,0:T(8,128)(2,1)S(1)}, u32[]{:S(2)}, u32[]{:S(2)}) async-start(bf16[32,16,1024]{2,1,0:T(8,128)(2,1)} %shard_map.30), calls=%async_computation | async-start | bytes 2097152 | tf_op jit(solution)/shard_map/all_to_all | solution.py:32
  14.6 2.1 %shard_map.31 = bf16[32,16,1024]{2,1,0:T(8,128)(2,1)} custom-call(bf16[32,1,16,2048]{3,2,1,0:T(8,128)(2,1)} %imaginary.3, bf16[32,1,16,2048]{3,2,1,0:T(8,128)(2,1)} %imaginary.3), custom_call_target="tpu_custom_call" | custom-call | tf_op jit(solution)/shard_map/pallas_call | solution.py:45
  16.6 2.7 %collective-permute-start = (bf16[32,16,1024]{2,1,0:T(8,128)(2,1)}, bf16[32,16,1024]{2,1,0:T(8,128)(2,1)}, u32[]{:S(2)}, u32[]{:S(2)}) collective-permute-start(bf16[32,16,1024]{2,1,0:T(8,128)(2,1)} %shard_map.31), channel_id=1, source_target_pairs={{2,0},{4,2},{6,4},{0,6},{3,1},{5,3},{7,5},{1,7},{10,8},{12,10},{14... | collective-permute-start | bytes 3145736 | tf_op jit(solution)/shard_map/ppermute | solution.py:14
  19.3 21.8 %collective-permute-done = bf16[32,16,1024]{2,1,0:T(8,128)(2,1)} collective-permute-done((bf16[32,16,1024]{2,1,0:T(8,128)(2,1)}, bf16[32,16,1024]{2,1,0:T(8,128)(2,1)}, u32[]{:S(2)}, u32[]{:S(2)}) %collective-permute-start) | collective-permute-done | bytes 1048608 | tf_op jit(solution)/shard_map/ppermute | solution.py:14
  41.2 0.0 all-to-all-done
  41.2 8.9 %all-to-all-start.1 = ((bf16[32,16,1024]{2,1,0:T(8,128)(2,1)}), bf16[32,16,1024]{2,1,0:T(8,128)(2,1)S(1)}, u32[]{:S(2)}, u32[]{:S(2)}) async-start(bf16[32,16,1024]{2,1,0:T(8,128)(2,1)} %collective-permute-done), calls=%async_computation.1 | async-start | bytes 2097152 | tf_op jit(solution)/shard_map/all_to_all | solution.py:32
  50.1 0.8 collective-permute-start.2
  51.0 2.7 %collective-permute-start.1 = (bf16[304,1024]{1,0:T(8,128)(2,1)S(1)}, bf16[304,1024]{1,0:T(8,128)(2,1)}, u32[]{:S(2)}, u32[]{:S(2)}) collective-permute-start(bf16[304,1024]{1,0:T(8,128)(2,1)S(1)} %bitcast.12), channel_id=1, source_target_pairs={{2,0},{4,2},{6,4},{0,6},{3,1},{5,3},{7,5},{1,7},{10,8},{12,10},{14... | collective-permute-start | bytes 1867784 | tf_op jit(solution)/shard_map/ppermute | solution.py:14
  53.8 7.5 %collective-permute-done.2 = bf16[208,1024]{1,0:T(8,128)(2,1)S(1)} collective-permute-done((bf16[208,1024]{1,0:T(8,128)(2,1)S(1)}, bf16[208,1024]{1,0:T(8,128)(2,1)S(1)}, u32[]{:S(2)}, u32[]{:S(2)}) %collective-permute-start.2) | collective-permute-done | bytes 426016 | tf_op jit(solution)/shard_map/ppermute | solution.py:14
  61.3 3.3 %collective-permute-done.1.down_1 = bf16[304,1024]{1,0:T(8,128)(2,1)} collective-permute-done((bf16[304,1024]{1,0:T(8,128)(2,1)S(1)}, bf16[304,1024]{1,0:T(8,128)(2,1)}, u32[]{:S(2)}, u32[]{:S(2)}) %collective-permute-start.1) | collective-permute-done | bytes 622624 | tf_op jit(solution)/shard_map/ppermute | solution.py:14
  64.7 3.5 %collective-permute-start.5 = (bf16[304,1024]{1,0:T(8,128)(2,1)}, bf16[304,1024]{1,0:T(8,128)(2,1)}, u32[]{:S(2)}, u32[]{:S(2)}) collective-permute-start(bf16[304,1024]{1,0:T(8,128)(2,1)} %collective-permute-done.1.down_1), channel_id=1, source_target_pairs={{2,0},{4,2},{6,4},{0,6},{3,1},{5,3},{7,5},{1,7},{10,8},{12,10},{14... | collective-permute-start | bytes 1867784 | tf_op jit(solution)/shard_map/ppermute | solution.py:14
  68.2 2.7 %collective-permute-done.3.up_2 = bf16[208,1024]{1,0:T(8,128)(2,1)} collective-permute-done((bf16[208,1024]{1,0:T(8,128)(2,1)S(1)}, bf16[208,1024]{1,0:T(8,128)(2,1)}, u32[]{:S(2)}, u32[]{:S(2)}) %collective-permute-start.3) | collective-permute-done | bytes 426016 | tf_op jit(solution)/shard_map/ppermute | solution.py:14
  70.9 0.1 pad_add_fusion.place
  70.9 6.0 %collective-permute-start.6 = (bf16[512,1024]{1,0:T(8,128)(2,1)S(1)}, bf16[512,1024]{1,0:T(8,128)(2,1)S(1)}, u32[]{:S(2)}, u32[]{:S(2)}) collective-permute-start(bf16[512,1024]{1,0:T(8,128)(2,1)S(1)} %bitcast.6), channel_id=1, source_target_pairs={{1,0},{3,2},{5,4},{7,6},{9,8},{11,10},{13,12},{15,14},{17,16},{19,... | collective-permute-start | bytes 3145736 | tf_op jit(solution)/shard_map/ppermute | solution.py:28
  76.9 0.0 all-to-all-done.1
  76.9 0.1 collective-permute-start.9
  77.0 1.4 %collective-permute-done.5.down_2 = bf16[304,1024]{1,0:T(8,128)(2,1)} collective-permute-done((bf16[304,1024]{1,0:T(8,128)(2,1)}, bf16[304,1024]{1,0:T(8,128)(2,1)}, u32[]{:S(2)}, u32[]{:S(2)}) %collective-permute-start.5) | collective-permute-done | bytes 622624 | tf_op jit(solution)/shard_map/ppermute | solution.py:14
  78.4 1.2 %collective-permute-done.4.up_3 = bf16[208,1024]{1,0:T(8,128)(2,1)} collective-permute-done((bf16[208,1024]{1,0:T(8,128)(2,1)}, bf16[208,1024]{1,0:T(8,128)(2,1)}, u32[]{:S(2)}, u32[]{:S(2)}) %collective-permute-start.4) | collective-permute-done | bytes 426016 | tf_op jit(solution)/shard_map/ppermute | solution.py:14
  79.7 2.1 %shard_map.32 = (bf16[512,1024]{1,0:T(8,128)(2,1)S(1)}, bf16[512,1024]{1,0:T(8,128)(2,1)S(1)}) custom-call(s32[2]{0:T(128)S(1)} %pad_add_fusion.place, bf16[304,1024]{1,0:T(8,128)(2,1)} %collective-permute-done.1.down_1, bf16[208,1024]{1,0:T(8,128)(2,1)} %collective-permute-done.4.up_3, bf16[304,1024]{1,0:T(8,128)(2,1)} %collective-permute-done.5.down_2, ...), custom_call_target="tpu_custom_call" | custom-call | flops 17179869184 | bytes 33554432 | tf_op jit(solution)/shard_map/pallas_call | solution.py:219
  81.8 7.9 %collective-permute-start.7 = (bf16[512,1024]{1,0:T(8,128)(2,1)S(1)}, bf16[512,1024]{1,0:T(8,128)(2,1)S(1)}, u32[]{:S(2)}, u32[]{:S(2)}) collective-permute-start(bf16[512,1024]{1,0:T(8,128)(2,1)S(1)} %get-tuple-element.18.ahead_at), channel_id=1, source_target_pairs={{1,0},{0,1},{3,2},{2,3},{5,4},{4,5},{7,6},{6,7},{9,8},{8,9},{11,10... | collective-permute-start | bytes 3145736 | tf_op jit(solution)/shard_map/ppermute | solution.py:28
  89.6 1.3 %collective-permute-start.8 = (bf16[512,1024]{1,0:T(8,128)(2,1)S(1)}, bf16[512,1024]{1,0:T(8,128)(2,1)S(1)}, u32[]{:S(2)}, u32[]{:S(2)}) collective-permute-start(bf16[512,1024]{1,0:T(8,128)(2,1)S(1)} %get-tuple-element.19.beyond_at), channel_id=1, source_target_pairs={{0,1},{2,3},{4,5},{6,7},{8,9},{10,11},{12,13},{14,15},{16,17},{18,... | collective-permute-start | bytes 3145736 | tf_op jit(solution)/shard_map/ppermute | solution.py:28
  90.9 1.3 %collective-permute-start.11 = (bf16[512,1024]{1,0:T(8,128)(2,1)S(1)}, bf16[512,1024]{1,0:T(8,128)(2,1)S(1)}, u32[]{:S(2)}, u32[]{:S(2)}) collective-permute-start(bf16[512,1024]{1,0:T(8,128)(2,1)S(1)} %bitcast.9), channel_id=1, source_target_pairs={{1,0},{0,1},{3,2},{2,3},{5,4},{4,5},{7,6},{6,7},{9,8},{8,9},{11,10... | collective-permute-start | bytes 3145736 | tf_op jit(solution)/shard_map/ppermute | solution.py:28
  92.2 0.0 collective-permute-done.6.sib_own
  92.2 0.0 collective-permute-start.10
  92.2 2.8 %collective-permute-done.9.first = bf16[512,1024]{1,0:T(8,128)(2,1)S(1)} collective-permute-done((bf16[512,1024]{1,0:T(8,128)(2,1)S(1)}, bf16[512,1024]{1,0:T(8,128)(2,1)S(1)}, u32[]{:S(2)}, u32[]{:S(2)}) %collective-permute-start.9) | collective-permute-done | bytes 1048608 | tf_op jit(solution)/shard_map/ppermute | solution.py:24
  95.1 0.1 fusion
  95.1 2.1 %collective-permute-start.13 = (bf16[256,1024]{1,0:T(8,128)(2,1)S(1)}, bf16[256,1024]{1,0:T(8,128)(2,1)S(1)}, u32[]{:S(2)}, u32[]{:S(2)}) collective-permute-start(bf16[256,1024]{1,0:T(8,128)(2,1)S(1)} %get-tuple-element.24), channel_id=1, source_target_pairs={{1,0},{0,1},{3,2},{2,3},{5,4},{4,5},{7,6},{6,7},{9,8},{8,9},{11,10... | collective-permute-start | bytes 1572872 | tf_op jit(solution)/shard_map/ppermute | solution.py:28
  97.2 0.1 collective-permute-start.12
  97.3 7.0 %shard_map.33 = (f32[1,2,1,4,512,512]{5,4,3,2,1,0:T(8,128)S(1)}, f32[1,2,1,256,512]{4,3,2,1,0:T(8,128)S(1)}) custom-call(s32[2]{0:T(128)S(1)} %pad_add_fusion.place, bf16[512,1024]{1,0:T(8,128)(2,1)S(1)} %bitcast.7, bf16[512,1024]{1,0:T(8,128)(2,1)S(1)} %get-tuple-element.18.ahead_at, bf16[512,1024]{1,0:T(8,128)(2,1)S(1)} %get-tuple-element.19.beyond_at, ...), custom_call_target="tpu_custom_call" | custom-call | flops 2147483648 | bytes 4194304 | tf_op jit(solution)/shard_map/pallas_call | solution.py:219
  104.3 1.8 %collective-permute-done.10.second = bf16[512,1024]{1,0:T(8,128)(2,1)S(1)} collective-permute-done((bf16[512,1024]{1,0:T(8,128)(2,1)S(1)}, bf16[512,1024]{1,0:T(8,128)(2,1)S(1)}, u32[]{:S(2)}, u32[]{:S(2)}) %collective-permute-start.10) | collective-permute-done | bytes 1048608 | tf_op jit(solution)/shard_map/ppermute | solution.py:24
  106.2 8.3 %shard_map.34 = (f32[1,2,1,4,512,512]{5,4,3,2,1,0:T(8,128)}, f32[1,2,1,256,512]{4,3,2,1,0:T(8,128)}) custom-call(s32[2]{0:T(128)S(1)} %pad_add_fusion.place, f32[1,2,1,4,512,512]{5,4,3,2,1,0:T(8,128)S(1)} %get-tuple-element.21.band_in, f32[1,2,1,256,512]{4,3,2,1,0:T(8,128)S(1)} %get-tuple-element.22.far_in, ...), custom_call_target="tpu_custom_call" | custom-call | flops 5368709120 | bytes 10485760 | tf_op jit(solution)/shard_map/pallas_call | solution.py:219
  (9 shorter events, 0.1 us)
Async XLA Ops:
  2.7 38.5 %all-to-all-start = ((bf16[32,16,1024]{2,1,0:T(8,128)(2,1)}), bf16[32,16,1024]{2,1,0:T(8,128)(2,1)S(1)}, u32[]{:S(2)}, u32[]{:S(2)}) async-start(bf16[32,16,1024]{2,1,0:T(8,128)(2,1)} %shard_map.30), calls=%async_computation | async-start | bytes 2097152 | tf_op jit(solution)/shard_map/all_to_all | solution.py:32
  16.6 24.6 %collective-permute-start = (bf16[32,16,1024]{2,1,0:T(8,128)(2,1)}, bf16[32,16,1024]{2,1,0:T(8,128)(2,1)}, u32[]{:S(2)}, u32[]{:S(2)}) collective-permute-start(bf16[32,16,1024]{2,1,0:T(8,128)(2,1)} %shard_map.31), channel_id=1, source_target_pairs={{2,0},{4,2},{6,4},{0,6},{3,1},{5,3},{7,5},{1,7},{10,8},{12,10},{14... | collective-permute-start | bytes 3145736 | tf_op jit(solution)/shard_map/ppermute | solution.py:14
  41.2 35.7 %all-to-all-start.1 = ((bf16[32,16,1024]{2,1,0:T(8,128)(2,1)}), bf16[32,16,1024]{2,1,0:T(8,128)(2,1)S(1)}, u32[]{:S(2)}, u32[]{:S(2)}) async-start(bf16[32,16,1024]{2,1,0:T(8,128)(2,1)} %collective-permute-done), calls=%async_computation.1 | async-start | bytes 2097152 | tf_op jit(solution)/shard_map/all_to_all | solution.py:32
  50.1 11.2 %collective-permute-start.2 = (bf16[208,1024]{1,0:T(8,128)(2,1)S(1)}, bf16[208,1024]{1,0:T(8,128)(2,1)S(1)}, u32[]{:S(2)}, u32[]{:S(2)}) collective-permute-start(bf16[208,1024]{1,0:T(8,128)(2,1)S(1)} %bitcast.13), channel_id=1, source_target_pairs={{6,0},{0,2},{2,4},{4,6},{7,1},{1,3},{3,5},{5,7},{14,8},{8,10},{10,... | collective-permute-start | bytes 1277960 | tf_op jit(solution)/shard_map/ppermute | solution.py:14
  51.0 13.6 %collective-permute-start.1 = (bf16[304,1024]{1,0:T(8,128)(2,1)S(1)}, bf16[304,1024]{1,0:T(8,128)(2,1)}, u32[]{:S(2)}, u32[]{:S(2)}) collective-permute-start(bf16[304,1024]{1,0:T(8,128)(2,1)S(1)} %bitcast.12), channel_id=1, source_target_pairs={{2,0},{4,2},{6,4},{0,6},{3,1},{5,3},{7,5},{1,7},{10,8},{12,10},{14... | collective-permute-start | bytes 1867784 | tf_op jit(solution)/shard_map/ppermute | solution.py:14
  61.3 9.5 %collective-permute-start.3 = (bf16[208,1024]{1,0:T(8,128)(2,1)S(1)}, bf16[208,1024]{1,0:T(8,128)(2,1)}, u32[]{:S(2)}, u32[]{:S(2)}) collective-permute-start(bf16[208,1024]{1,0:T(8,128)(2,1)S(1)} %collective-permute-done.2), channel_id=1, source_target_pairs={{6,0},{0,2},{2,4},{4,6},{7,1},{1,3},{3,5},{5,7},{14,8},{8,10},{10,... | collective-permute-start | bytes 1277960 | tf_op jit(solution)/shard_map/ppermute | solution.py:14
  64.7 13.8 %collective-permute-start.5 = (bf16[304,1024]{1,0:T(8,128)(2,1)}, bf16[304,1024]{1,0:T(8,128)(2,1)}, u32[]{:S(2)}, u32[]{:S(2)}) collective-permute-start(bf16[304,1024]{1,0:T(8,128)(2,1)} %collective-permute-done.1.down_1), channel_id=1, source_target_pairs={{2,0},{4,2},{6,4},{0,6},{3,1},{5,3},{7,5},{1,7},{10,8},{12,10},{14... | collective-permute-start | bytes 1867784 | tf_op jit(solution)/shard_map/ppermute | solution.py:14
  70.9 8.8 %collective-permute-start.4 = (bf16[208,1024]{1,0:T(8,128)(2,1)}, bf16[208,1024]{1,0:T(8,128)(2,1)}, u32[]{:S(2)}, u32[]{:S(2)}) collective-permute-start(bf16[208,1024]{1,0:T(8,128)(2,1)} %collective-permute-done.3.up_2), channel_id=1, source_target_pairs={{6,0},{0,2},{2,4},{4,6},{7,1},{1,3},{3,5},{5,7},{14,8},{8,10},{10,... | collective-permute-start | bytes 1277960 | tf_op jit(solution)/shard_map/ppermute | solution.py:14
  70.9 21.3 %collective-permute-start.6 = (bf16[512,1024]{1,0:T(8,128)(2,1)S(1)}, bf16[512,1024]{1,0:T(8,128)(2,1)S(1)}, u32[]{:S(2)}, u32[]{:S(2)}) collective-permute-start(bf16[512,1024]{1,0:T(8,128)(2,1)S(1)} %bitcast.6), channel_id=1, source_target_pairs={{1,0},{3,2},{5,4},{7,6},{9,8},{11,10},{13,12},{15,14},{17,16},{19,... | collective-permute-start | bytes 3145736 | tf_op jit(solution)/shard_map/ppermute | solution.py:28
  76.9 18.1 %collective-permute-start.9 = (bf16[512,1024]{1,0:T(8,128)(2,1)S(1)}, bf16[512,1024]{1,0:T(8,128)(2,1)S(1)}, u32[]{:S(2)}, u32[]{:S(2)}) collective-permute-start(bf16[512,1024]{1,0:T(8,128)(2,1)S(1)} %bitcast.8), channel_id=1, source_target_pairs={{2,0},{7,1},{4,2},{1,3},{6,4},{3,5},{0,6},{5,7},{10,8},{15,9},{12,... | collective-permute-start | bytes 3145736 | tf_op jit(solution)/shard_map/ppermute | solution.py:24
  81.8 15.4 %collective-permute-start.7 = (bf16[512,1024]{1,0:T(8,128)(2,1)S(1)}, bf16[512,1024]{1,0:T(8,128)(2,1)S(1)}, u32[]{:S(2)}, u32[]{:S(2)}) collective-permute-start(bf16[512,1024]{1,0:T(8,128)(2,1)S(1)} %get-tuple-element.18.ahead_at), channel_id=1, source_target_pairs={{1,0},{0,1},{3,2},{2,3},{5,4},{4,5},{7,6},{6,7},{9,8},{8,9},{11,10... | collective-permute-start | bytes 3145736 | tf_op jit(solution)/shard_map/ppermute | solution.py:28
  89.6 7.6 %collective-permute-start.8 = (bf16[512,1024]{1,0:T(8,128)(2,1)S(1)}, bf16[512,1024]{1,0:T(8,128)(2,1)S(1)}, u32[]{:S(2)}, u32[]{:S(2)}) collective-permute-start(bf16[512,1024]{1,0:T(8,128)(2,1)S(1)} %get-tuple-element.19.beyond_at), channel_id=1, source_target_pairs={{0,1},{2,3},{4,5},{6,7},{8,9},{10,11},{12,13},{14,15},{16,17},{18,... | collective-permute-start | bytes 3145736 | tf_op jit(solution)/shard_map/ppermute | solution.py:28
  90.9 13.4 %collective-permute-start.11 = (bf16[512,1024]{1,0:T(8,128)(2,1)S(1)}, bf16[512,1024]{1,0:T(8,128)(2,1)S(1)}, u32[]{:S(2)}, u32[]{:S(2)}) collective-permute-start(bf16[512,1024]{1,0:T(8,128)(2,1)S(1)} %bitcast.9), channel_id=1, source_target_pairs={{1,0},{0,1},{3,2},{2,3},{5,4},{4,5},{7,6},{6,7},{9,8},{8,9},{11,10... | collective-permute-start | bytes 3145736 | tf_op jit(solution)/shard_map/ppermute | solution.py:28
  92.2 13.9 %collective-permute-start.10 = (bf16[512,1024]{1,0:T(8,128)(2,1)S(1)}, bf16[512,1024]{1,0:T(8,128)(2,1)S(1)}, u32[]{:S(2)}, u32[]{:S(2)}) collective-permute-start(bf16[512,1024]{1,0:T(8,128)(2,1)S(1)} %bitcast.10), channel_id=1, source_target_pairs={{6,0},{3,1},{0,2},{5,3},{2,4},{7,5},{4,6},{1,7},{14,8},{11,9},{8,1... | collective-permute-start | bytes 3145736 | tf_op jit(solution)/shard_map/ppermute | solution.py:24
  95.1 11.0 %collective-permute-start.13 = (bf16[256,1024]{1,0:T(8,128)(2,1)S(1)}, bf16[256,1024]{1,0:T(8,128)(2,1)S(1)}, u32[]{:S(2)}, u32[]{:S(2)}) collective-permute-start(bf16[256,1024]{1,0:T(8,128)(2,1)S(1)} %get-tuple-element.24), channel_id=1, source_target_pairs={{1,0},{0,1},{3,2},{2,3},{5,4},{4,5},{7,6},{6,7},{9,8},{8,9},{11,10... | collective-permute-start | bytes 1572872 | tf_op jit(solution)/shard_map/ppermute | solution.py:28
  97.2 9.0 %collective-permute-start.12 = (bf16[256,1024]{1,0:T(8,128)(2,1)S(1)}, bf16[256,1024]{1,0:T(8,128)(2,1)S(1)}, u32[]{:S(2)}, u32[]{:S(2)}) collective-permute-start(bf16[256,1024]{1,0:T(8,128)(2,1)S(1)} %get-tuple-element.25), channel_id=1, source_target_pairs={{1,0},{0,1},{3,2},{2,3},{5,4},{4,5},{7,6},{6,7},{9,8},{8,9},{11,10... | collective-permute-start | bytes 1572872 | tf_op jit(solution)/shard_map/ppermute | solution.py:28
